TPU v7x, 512 devices: a whole 4x8x8 slice. The times are simulated.
512 devices in a mesh: grp: 32 (over x, z), vocab: 16 (over y, core).
Axes of the slice: x: 4, y: 8, z: 8, core: 2. Of those that a mesh axis runs over, the one named last changes fastest.
Arguments:
- teacher_rows: bfloat16 [64, 8, 4096], P('grp', None, 'vocab'), may hold values from -160 to 160
- student_rows: bfloat16 [32, 8, 5120], P('grp', None, 'vocab'), may hold values from -160 to 160
- teacher_head: bfloat16 [4096, 131072], P(None, ('grp', 'vocab')), may hold values from -0.25 to 0.25
- student_head: bfloat16 [5120, 131072], P(None, ('grp', 'vocab')), may hold values from -0.25 to 0.25
- lengths: int32 [64], replicated, may hold values from 1 to 7, as said below
- owner: int32 [64], replicated, may hold values from 0 to 31, as said below
Outputs:
- divergence: float32 [32, 8], P('grp')
- grad_student: bfloat16 [32, 8, 5120], P('grp', None, 'vocab')
Inputs may be any that keep to these rules, and one draw needn't show every extreme that they name: All 2 sequences of one teacher group share one owner, and each student group owns the sequences of exactly one teacher group. The lengths of the 2 sequences of one teacher group sum to at most 8, and to exactly 8 for some group.
All inputs are finite; a program needn't handle non-finite values.
Results may differ from a plain program's by a relative error of at most 0.018.
Values may be sent and summed in bfloat16 or wider, within the bound.
No kernel may reach another device: no remote copies, remote signals or barrier semaphores. Data moves between devices by JAX's collectives and lax.ppermute only.
A program may use at most 64 MiB of HBM per device.

v0:
```python
import jax
import jax.numpy as jnp
from jax import lax
from jax.sharding import Mesh
from jax.sharding import PartitionSpec as P

GRP = ("grp_0", "grp_1")
VOCAB = ("vocab_0", "vocab_1")
GRP_VOCAB = ("grp_0", "grp_1", "vocab_0", "vocab_1")


def in_order(pieces, dim):
    pieces = jnp.moveaxis(pieces, 0, dim)
    shape = pieces.shape
    return pieces.reshape(*shape[:dim], shape[dim] * shape[dim + 1], *shape[dim + 2 :])


def one_gather(arrays, axis, dims):
    flat = jnp.concatenate([a.reshape(-1) for a in arrays])
    lines, at, outs = (lax.all_gather(flat, axis), 0, [])
    for a, dim in zip(arrays, dims):
        pieces = lines[:, at : at + a.size].reshape(-1, *a.shape)
        outs.append(in_order(pieces, dim))
        at += a.size
    return tuple(outs)


def stacked_from(shard, axes, sequence):
    pieces = shard
    for k in sequence:
        pieces = lax.all_gather(pieces, axes[k])
    done = sequence[::-1]
    back = [done.index(k) for k in range(len(axes))]
    pieces = pieces.transpose(*back, *range(len(axes), pieces.ndim))
    return pieces.reshape(-1, *shard.shape)


def gathered_by_axis(shard, axes, sequence, dim):
    return in_order(stacked_from(shard, axes, sequence), dim)


def collected_together(shard, axis):
    leaves = jax.tree.leaves(shard)
    sequence = sorted(range(len(leaves)), key=lambda k: -leaves[k].size)
    width = (1, *leaves[sequence[0]].shape)[-1]
    lines = [
        jnp.pad(leaves[k].reshape(-1), (0, -leaves[k].size % width)).reshape(-1, width)
        for k in sequence
    ]
    both, at, found = (lax.all_gather(jnp.concatenate(lines), axis), 0, {})
    for k, line in zip(sequence, lines):
        section = both[:, at : at + len(line)].reshape(len(both), -1)
        found[k] = section[:, : leaves[k].size].reshape(-1, *leaves[k].shape)
        at += len(line)
    numbers = iter(range(len(leaves)))
    return jax.tree.map(lambda _: found[next(numbers)], shard)


def combined_by_axis(shard, axes, combine):
    for axis in axes:
        pieces = collected_together(shard, axis)
        shard = jax.tree.map(lambda part: part[0], pieces)
        for k in range(1, lax.axis_size(axis)):
            shard = combine(shard, jax.tree.map(lambda part: part[k], pieces))
    return shard


def in_blocks(shard, dim, count):
    shape = shard.shape
    pieces = shard.reshape(*shape[:dim], count, shape[dim] // count, *shape[dim + 1 :])
    return jnp.moveaxis(pieces, dim, 0)


def sum_at_owner(shard, axis, dim):
    count = lax.axis_size(axis)
    pieces = lax.all_to_all(in_blocks(shard, dim, count), axis, 0, 0, tiled=True)
    return jnp.sum(pieces.astype(jnp.float32), axis=0)


def routing_tables(lengths, owner, groups, seq_count, positions, pad_rows):
    slot_count = seq_count * positions
    group_ids = jnp.arange(groups, dtype=jnp.int32)
    length_table = lengths.reshape(groups, seq_count)
    owner_table = owner.reshape(groups, seq_count)[:, 0]
    teacher_of = jnp.sum(
        (owner_table[None, :] == group_ids[:, None]).astype(jnp.int32) * group_ids[None, :], axis=1
    )
    position_ids = jnp.arange(positions, dtype=jnp.int32)
    live_slots = (position_ids[None, None, :] < length_table[:, :, None]).reshape(
        groups, slot_count
    )
    ranked = jnp.cumsum(live_slots.astype(jnp.int32), axis=1) - 1
    target = jnp.where(live_slots, ranked, pad_rows)
    matches = target[:, None, :] == jnp.arange(pad_rows, dtype=jnp.int32)[None, :, None]
    source = jnp.sum(
        matches.astype(jnp.int32) * jnp.arange(slot_count, dtype=jnp.int32)[None, None, :], axis=2
    )
    totals = jnp.sum(length_table, axis=1)
    owned_total = jnp.take(totals, teacher_of, axis=0)
    student_live = jnp.arange(pad_rows, dtype=jnp.int32)[None, :] < owned_total[:, None]
    return (teacher_of, source, student_live)


def combine(left_part, right_part):
    teacher_top = jnp.maximum(left_part[0], right_part[0])
    teacher_total = left_part[1] * jnp.exp(left_part[0] - teacher_top) + right_part[1] * jnp.exp(
        right_part[0] - teacher_top
    )
    student_top = jnp.maximum(left_part[2], right_part[2])
    left_scale = jnp.exp(left_part[2] - student_top)
    right_factor = jnp.exp(right_part[2] - student_top)
    student_total = left_part[3] * left_scale + right_part[3] * right_factor
    weighted = left_part[4] * left_scale + right_part[4] * right_factor
    return (teacher_top, teacher_total, student_top, student_total, weighted)


def per_device(teacher_rows, student_rows, teacher_head, student_head, lengths, owner):
    groups = lax.axis_size(GRP)
    seq_count = teacher_rows.shape[0]
    positions = teacher_rows.shape[1]
    slot_count = seq_count * positions
    pad_rows = student_rows.shape[1]
    own_group = lax.axis_index(GRP)
    teacher_of, source, student_live = routing_tables(
        lengths, owner, groups, seq_count, positions, pad_rows
    )
    local_teacher = teacher_rows.reshape(slot_count, teacher_rows.shape[2])
    local_student = student_rows.reshape(pad_rows, student_rows.shape[2])
    own_source = lax.dynamic_index_in_dim(source, own_group, 0, keepdims=False)
    sent_teacher = jnp.take(local_teacher, own_source, axis=0)
    row_position = teacher_of[:, None] * pad_rows + jnp.arange(pad_rows, dtype=jnp.int32)[None, :]
    teacher_full, student_full = one_gather((sent_teacher, local_student), VOCAB, (1, 1))
    raw_teacher = jnp.dot(
        lax.all_gather(teacher_full, GRP, axis=0, tiled=True),
        teacher_head,
        preferred_element_type=jnp.float32,
    )
    student_logits = jnp.dot(
        gathered_by_axis(student_full, GRP, (0, 1), 0),
        student_head,
        preferred_element_type=jnp.float32,
    )
    teacher_logits = jnp.take(raw_teacher, row_position.reshape(-1), axis=0)
    weight = student_live.reshape(-1).astype(jnp.float32)
    local_teacher_top = jnp.max(teacher_logits, axis=1)
    local_student_top = jnp.max(student_logits, axis=1)
    student_exp = jnp.exp(student_logits - local_student_top[:, None])
    merged = combined_by_axis(
        (
            local_teacher_top,
            jnp.sum(jnp.exp(teacher_logits - local_teacher_top[:, None]), axis=1),
            local_student_top,
            jnp.sum(student_exp, axis=1),
            jnp.sum(student_exp * (student_logits - teacher_logits), axis=1),
        ),
        GRP_VOCAB,
        combine,
    )
    teacher_lse = merged[0] + jnp.log(merged[1])
    student_lse = merged[2] + jnp.log(merged[3])
    log_q = student_logits - student_lse[:, None]
    log_p = teacher_logits - teacher_lse[:, None]
    student_prob = jnp.exp(log_q)
    log_ratio = log_q - log_p
    kl_rows = merged[4] / merged[3] - student_lse + teacher_lse
    kl_rows = kl_rows * weight
    grad_logits = (weight[:, None] * student_prob * (log_ratio - kl_rows[:, None])).astype(
        jnp.bfloat16
    )
    partial_value = jnp.einsum(
        "rv,dv->rd", grad_logits, student_head, preferred_element_type=jnp.float32
    )
    feature_totals_acc = sum_at_owner(partial_value.astype(jnp.bfloat16), VOCAB, 1)
    grad_rows = sum_at_owner(feature_totals_acc.astype(jnp.bfloat16), GRP, 0).astype(jnp.bfloat16)
    divergence = lax.dynamic_slice_in_dim(kl_rows, own_group * pad_rows, pad_rows, 0)
    return (divergence.reshape(1, pad_rows), grad_rows.reshape(1, pad_rows, grad_rows.shape[1]))


def solution(mesh):
    torus = Mesh(mesh.devices.reshape(4, 8, 8, 2), ("grp_0", "grp_1", "vocab_0", "vocab_1"))
    return jax.shard_map(
        per_device,
        mesh=torus,
        in_specs=(
            P(GRP, None, VOCAB),
            P(GRP, None, VOCAB),
            P(None, GRP_VOCAB),
            P(None, GRP_VOCAB),
            P(),
            P(),
        ),
        out_specs=(P(GRP, None), P(GRP, None, VOCAB)),
        check_vma=False,
    )
```

profile of v0, /device:TPU:1, one launch (start us, length us, event | category | flops | bytes accessed | tf_op | source)
XLA Modules:
  0.0 332.1 jit_solution(13637512223904512838)
XLA Ops:
  7.2 0.9 reshape.2804
  8.9 0.8 reshape_reshape.6
  9.7 1.3 gather_fusion.1
  11.1 21.7 %all-gather.6 = bf16[16,1,4608]{2,1,0:T(2,128)(2,1)S(1)} all-gather(bf16[1,1,4608]{2,1,0:T(2,128)(2,1)S(1)} %reshape.2848), channel_id=2, replica_groups=mesh['grp_0'=4,'grp_1'=8,'vocab_0'=8,'vocab_1'=2] {'vocab_0','vocab_1'}, dimensions={0}, use_global_device_ids=true | all-gather | bytes 156672 | tf_op jit(solution)/shard_map/all_gather | solution.py:20
  33.8 10.2 %all_gather.45 = bf16[4,8,5120]{2,1,0:T(8,128)(2,1)} all-gather(bf16[1,8,5120]{2,1,0:T(8,128)(2,1)S(1)} %all_gather_reshape.3), channel_id=1, replica_groups=mesh['grp_0'=4,'grp_1'=8,'vocab_0'=8,'vocab_1'=2] {'grp_0'}, dimensions={0}, use_global_device_ids=true | all-gather | bytes 409600 | tf_op jit(solution)/shard_map/all_gather | solution.py:31
  44.5 0.7 gather_fusion
  45.7 67.2 %all-gather.14.cloned.1.call-done = bf16[256,4096]{1,0:T(8,128)(2,1)} async-done(((bf16[8,4096]{1,0:T(8,128)(2,1)}), bf16[256,4096]{1,0:T(8,128)(2,1)}) %all-gather.14.cloned.1.call-update) | async-done | bytes 2097168 | tf_op jit(solution)/shard_map/all_gather | solution.py:134
  113.0 2.9 fusion.212
  115.9 1.0 gather_fusion.2
  117.1 41.4 %all-gather.16.cloned.1.call-done = bf16[32,8,5120]{2,1,0:T(8,128)(2,1)} async-done(((bf16[4,8,5120]{2,1,0:T(8,128)(2,1)}), bf16[32,8,5120]{2,1,0:T(8,128)(2,1)}) %all-gather.16.cloned.1.call-update) | async-done | bytes 2621456 | tf_op jit(solution)/shard_map/all_gather | solution.py:31
  158.4 1.9 copy.40
  160.4 1.1 fusion.211
  161.7 9.3 %all-gather.7 = f32[4,5,256]{2,1,0:T(8,128)S(1)} all-gather(f32[1,5,256]{2,1,0:T(8,128)S(1)} %bitcast.1105), channel_id=4, replica_groups=mesh['grp_0'=4,'grp_1'=8,'vocab_0'=8,'vocab_1'=2] {'grp_0'}, dimensions={0}, use_global_device_ids=true | all-gather | bytes 25600 | tf_op jit(solution)/shard_map/all_gather | solution.py:50
  171.1 18.3 %all-gather.8 = f32[8,5,256]{2,1,0:T(8,128)S(1)} all-gather(f32[1,5,256]{2,1,0:T(8,128)S(1)} %bitcast.1106), channel_id=5, replica_groups=mesh['grp_0'=4,'grp_1'=8,'vocab_0'=8,'vocab_1'=2] {'grp_1'}, dimensions={0}, use_global_device_ids=true | all-gather | bytes 46080 | tf_op jit(solution)/shard_map/all_gather | solution.py:50
  189.6 19.3 %all-gather.9 = f32[8,5,256]{2,1,0:T(8,128)S(1)} all-gather(f32[1,5,256]{2,1,0:T(8,128)S(1)} %bitcast.1107), channel_id=6, replica_groups=mesh['grp_0'=4,'grp_1'=8,'vocab_0'=8,'vocab_1'=2] {'vocab_0'}, dimensions={0}, use_global_device_ids=true | all-gather | bytes 46080 | tf_op jit(solution)/shard_map/all_gather | solution.py:50
  209.0 20.9 %all-gather.10 = f32[2,5,256]{2,1,0:T(8,128)S(1)} all-gather(f32[1,5,256]{2,1,0:T(8,128)S(1)} %bitcast.1108), channel_id=7, replica_groups=mesh['grp_0'=4,'grp_1'=8,'vocab_0'=8,'vocab_1'=2] {'vocab_1'}, dimensions={0}, use_global_device_ids=true | all-gather | bytes 15360 | tf_op jit(solution)/shard_map/all_gather | solution.py:50
  229.9 2.5 convolution_convert_fusion
  232.4 4.4 %copy.41 = bf16[256,5120]{0,1:T(8,128)(2,1)} copy(bf16[256,5120]{1,0:T(8,128)(2,1)} %convolution_convert_fusion) | data formatting | bytes 5242880 | tf_op jit(solution)/shard_map/convert_element_type | solution.py:173
  236.8 68.4 %all_to_all.10 = bf16[16,256,320]{1,2,0:T(8,128)(2,1)} all-to-all(bf16[16,256,320]{1,2,0:T(8,128)(2,1)} %bitcast.1097), channel_id=1, replica_groups=mesh['grp_0'=4,'grp_1'=8,'vocab_0'=8,'vocab_1'=2] {'vocab_0','vocab_1'}, dimensions={0} | all-to-all | bytes 5242880 | tf_op jit(solution)/shard_map/all_to_all | solution.py:76
  305.1 2.1 reduce_sum.87
  307.3 0.8 copy.42
  308.1 6.0 %all-to-all-start.1 = ((bf16[32,8,320]{2,1,0:T(8,128)(2,1)}), bf16[32,8,320]{2,1,0:T(8,128)(2,1)S(1)}, u32[]{:S(2)}, u32[]{:S(2)}) async-start(bf16[32,8,320]{2,1,0:T(8,128)(2,1)} %bitcast.134), calls=%async_computation.1 | async-start | bytes 393216 | tf_op jit(solution)/shard_map/all_to_all | solution.py:76
  314.7 10.0 %all-to-all-done.1 = bf16[32,8,320]{2,1,0:T(8,128)(2,1)S(1)} async-done(((bf16[32,8,320]{2,1,0:T(8,128)(2,1)}), bf16[32,8,320]{2,1,0:T(8,128)(2,1)S(1)}, u32[]{:S(2)}, u32[]{:S(2)}) %all-to-all-start.1) | async-done | bytes 163872 | tf_op jit(solution)/shard_map/all_to_all | solution.py:76
  324.6 0.6 reduce_sum.88
  (67 shorter events, 4.1 us)
Async XLA Ops:
  7.2 153.2 %copy-start = (bf16[5120,256]{1,0:T(8,128)(2,1)S(1)}, bf16[5120,256]{1,0:T(8,128)(2,1)}, u32[]{:S(2)}) copy-start(bf16[5120,256]{1,0:T(8,128)(2,1)} %param.9) | copy-start | bytes 7864324
  7.2 37.0 %copy-start.1 = (s32[64]{0:T(128)S(1)}, s32[64]{0:T(128)}, u32[]{:S(2)}) copy-start(s32[64]{0:T(128)} %param.11) | copy-start | bytes 772
  7.2 105.8 %all-gather.14.cloned.1.call-start = ((), (), s32[]{:S(2)}) async-start(), calls=%async_computation.2 | async-start | bytes 2162688 | tf_op jit(solution)/shard_map/all_gather | solution.py:134
  33.4 125.0 %all-gather.16.cloned.1.call-start = ((), (), s32[]{:S(2)}) async-start(), calls=%async_computation.3 | async-start | bytes 2949120 | tf_op jit(solution)/shard_map/all_gather | solution.py:31
  308.1 16.6 %all-to-all-start.1 = ((bf16[32,8,320]{2,1,0:T(8,128)(2,1)}), bf16[32,8,320]{2,1,0:T(8,128)(2,1)S(1)}, u32[]{:S(2)}, u32[]{:S(2)}) async-start(bf16[32,8,320]{2,1,0:T(8,128)(2,1)} %bitcast.134), calls=%async_computation.1 | async-start | bytes 393216 | tf_op jit(solution)/shard_map/all_to_all | solution.py:76
Sparse Core Ops, SparseCore 0:
  33.6 79.3 all-gather.13
  115.1 43.3 all-gather.15
where the time goes:
time: 333 us; the launch traced here: 332 us
  blocking collectives  168 us (50%)
  waiting for transfers between devices  119 us (36%)
  local copies, waits for them, and re-layouts  14.5 us (4%)
  between operations  14.3 us (4%)
  matrix products  6.54 us (2%)
  starting transfers between devices  6.08 us (2%)
  other arithmetic  3.99 us (1%)
    all_to_all x1, blocking collectives, sum_at_owner(): lax.all_to_all(in_blocks(shard, dim, count), axis, 0, 0, tiled=True)  68.4 us
    all_gather x4, blocking collectives, collected_together(): both, at, found = (lax.all_gather(jnp.concatenate(lines), axis), 0, {})  67.8 us
    all_gather x1, waiting for transfers between devices, per_device(): lax.all_gather(teacher_full, GRP, axis=0, tiled=True)  67.2 us
    all_gather x1, waiting for transfers between devices, stacked_from(): pieces = lax.all_gather(pieces, axes[k])  41.4 us
    all_gather x1, blocking collectives, one_gather(): lines, at, outs = (lax.all_gather(flat, axis), 0, [])  21.7 us
    all_gather x1, blocking collectives, stacked_from(): pieces = lax.all_gather(pieces, axes[k])  10.2 us
    all_to_all x1, waiting for transfers between devices, sum_at_owner(): lax.all_to_all(in_blocks(shard, dim, count), axis, 0, 0, tiled=True)  9.96 us
  transfers between devices with their start and end apart: 3, of which 3 were waited for; matrix products, arithmetic and copies ran while one was open for 2% of the time, Pallas kernels for 0%

commit v1 on v0

v1 whole, which is shorter than its diff:
```python
import functools

import jax
import jax.numpy as jnp
from jax import lax
from jax.experimental import pallas as pl
from jax.experimental.pallas import tpu as pltpu
from jax.sharding import Mesh
from jax.sharding import PartitionSpec as P

GRP = ("x", "z")
VOCAB = ("y", "c")
OWNER = ("x", "z", "c")
CAPACITIES = (256,)
F32 = jnp.float32
BF16 = jnp.bfloat16
VMEM = pl.BlockSpec(memory_space=pltpu.VMEM)
SMEM = pl.BlockSpec(memory_space=pltpu.SMEM)
PARAMS = pltpu.CompilerParams(vmem_limit_bytes=48 * 1024 * 1024)


def iota(shape, dim):
    return lax.broadcasted_iota(jnp.int32, shape, dim)


def exchange(pieces, axes):
    return lax.all_to_all(pieces, axes, 0, 0, tiled=True)


def arrange_kernel(group_ref, lengths_ref, teacher_ref, student_ref, out_ref):
    count, pad, _ = out_ref.shape
    width = teacher_ref.shape[2]
    first = lengths_ref[2 * group_ref[0]]
    upper = teacher_ref[0].astype(F32)
    lower = pltpu.roll(teacher_ref[1].astype(F32), first, 0)
    chosen = jnp.where(iota(upper.shape, 0) < first, upper, lower).astype(BF16)
    for k in range(count):
        out_ref[k, :, :width] = chosen
        out_ref[k, :, width:] = student_ref[0]


def arrange(group, lengths, teacher_rows, student_rows, count):
    pad = student_rows.shape[1]
    width = teacher_rows.shape[2] + student_rows.shape[2]
    return pl.pallas_call(
        arrange_kernel,
        out_shape=jax.ShapeDtypeStruct((count, pad, width), BF16),
        in_specs=[SMEM, SMEM, VMEM, VMEM],
        out_specs=VMEM,
    )(group, lengths, teacher_rows, student_rows)


def logits_kernel(teacher_width, rows_ref, teacher_ref, student_ref, t_ref, s_ref):
    @pl.when(pl.program_id(0) == 0)
    def _():
        t_ref[...] = jnp.zeros_like(t_ref)
        s_ref[...] = jnp.zeros_like(s_ref)

    student_width = rows_ref.shape[2] - teacher_width
    t, s = t_ref[...], s_ref[...]
    for k in range(rows_ref.shape[0]):
        t += jnp.dot(
            rows_ref[k, :, :teacher_width],
            teacher_ref[k * teacher_width : (k + 1) * teacher_width, :],
            preferred_element_type=F32,
        )
        s += jnp.dot(
            rows_ref[k, :, teacher_width:],
            student_ref[k * student_width : (k + 1) * student_width, :],
            preferred_element_type=F32,
        )
    t_ref[...] = t
    s_ref[...] = s


def logits(rows, teacher_head, student_head, teacher_width):
    count, slots, width = rows.shape
    steps = 4
    vocab = teacher_head.shape[1]
    return pl.pallas_call(
        functools.partial(logits_kernel, teacher_width),
        grid=(steps,),
        out_shape=[jax.ShapeDtypeStruct((slots, vocab), F32)] * 2,
        in_specs=[
            pl.BlockSpec((count // steps, slots, width), lambda i: (i, 0, 0)),
            pl.BlockSpec((teacher_head.shape[0] // steps, vocab), lambda i: (i, 0)),
            pl.BlockSpec((student_head.shape[0] // steps, vocab), lambda i: (i, 0)),
        ],
        out_specs=[pl.BlockSpec((slots, vocab), lambda i: (0, 0))] * 2,
        compiler_params=PARAMS,
    )(rows, teacher_head, student_head)


def local_kernel(t_ref, s_ref, t_place_ref, s_place_ref, logit_ref, gap_ref, stat_ref):
    lanes = logit_ref.shape[0]
    place = iota((lanes, t_ref.shape[0]), 0)

    def packed(place_ref, ref):
        pick = (place == place_ref[...]).astype(F32)
        return jnp.dot(
            pick, ref[...], preferred_element_type=F32, precision=lax.Precision.HIGHEST
        )

    t = packed(t_place_ref, t_ref)
    s = packed(s_place_ref, s_ref)
    gap = s - t
    t_top = jnp.max(t, axis=1, keepdims=True)
    t_lse = t_top + jnp.log(jnp.sum(jnp.exp(t - t_top), axis=1, keepdims=True))
    s_top = jnp.max(s, axis=1, keepdims=True)
    e = jnp.exp(s - s_top)
    total = jnp.sum(e, axis=1, keepdims=True)
    weighted = jnp.sum(e * gap, axis=1, keepdims=True)
    logit_ref[...] = s
    gap_ref[...] = gap
    lane = iota((lanes, 128), 1)
    table = jnp.where(
        lane == 0,
        s_top,
        jnp.where(lane == 1, total, jnp.where(lane == 2, weighted, t_lse)),
    )
    table = table.T[:4]
    for k in range(stat_ref.shape[0]):
        stat_ref[k] = table


def local(t, s, t_place, s_place, lanes, count):
    return pl.pallas_call(
        local_kernel,
        out_shape=[
            jax.ShapeDtypeStruct((lanes, t.shape[1]), F32),
            jax.ShapeDtypeStruct((lanes, t.shape[1]), F32),
            jax.ShapeDtypeStruct((count, 4, lanes), F32),
        ],
        in_specs=[VMEM] * 4,
        out_specs=[VMEM] * 3,
        compiler_params=PARAMS,
    )(t, s, t_place, s_place)


def merged(stat_ref):
    top = stat_ref[:, 0, :]
    high = jnp.max(top, axis=0, keepdims=True)
    scale = jnp.exp(top - high)
    total = jnp.sum(scale * stat_ref[:, 1, :], axis=0, keepdims=True)
    weighted = jnp.sum(scale * stat_ref[:, 2, :], axis=0, keepdims=True)
    t_lse = stat_ref[:, 3, :]
    t_high = jnp.max(t_lse, axis=0, keepdims=True)
    t_lse = t_high + jnp.log(jnp.sum(jnp.exp(t_lse - t_high), axis=0, keepdims=True))
    return high, total, weighted, t_lse


def merge_kernel(stat_ref, out_ref):
    high, total, weighted, t_lse = merged(stat_ref)
    table = jnp.concatenate([high, total, weighted, t_lse], axis=0)
    for k in range(out_ref.shape[0]):
        out_ref[k] = table


def merge(stat, count):
    return pl.pallas_call(
        merge_kernel,
        out_shape=jax.ShapeDtypeStruct((count, *stat.shape[1:]), F32),
        in_specs=[VMEM],
        out_specs=VMEM,
    )(stat)


def gradient_kernel(
    core_ref, stat_ref, logit_ref, gap_ref, head_ref, keep_ref, send_ref, kl_ref, g_ref
):
    @pl.when(pl.program_id(0) == 0)
    def _():
        high, total, weighted, t_lse = merged(stat_ref)
        lanes = high.shape[1]
        mean = weighted / total
        kl_ref[...] = mean - (high + jnp.log(total)) + t_lse
        row = iota((128, lanes), 0)
        table = jnp.where(row == 0, high, jnp.where(row == 1, 1.0 / total, mean)).T
        q = jnp.exp(logit_ref[...] - table[:, 0:1]) * table[:, 1:2]
        g = q * (gap_ref[...] - table[:, 2:3])
        g_ref[...] = g[: g_ref.shape[0]].astype(BF16)

    width = keep_ref.shape[2]
    half = keep_ref.shape[1]
    low = core_ref[0] == 0
    for k in range(keep_ref.shape[0]):
        part = lax.dot_general(
            g_ref[...],
            head_ref[k * width : (k + 1) * width, :],
            (((1,), (1,)), ((), ())),
            preferred_element_type=F32,
        ).astype(BF16)
        keep_ref[k] = jnp.where(low, part[:half], part[half:])
        send_ref[k] = jnp.where(low, part[half:], part[:half])


def gradient(core, stat, logit, gap, head, rows, count):
    steps = 4
    width = head.shape[0] // count
    part = jax.ShapeDtypeStruct((count, rows // 2, width), BF16)
    block = pl.BlockSpec((count // steps, rows // 2, width), lambda i: (i, 0, 0))
    whole = lambda a: pl.BlockSpec(a.shape, lambda i: (0,) * a.ndim)
    return pl.pallas_call(
        gradient_kernel,
        grid=(steps,),
        out_shape=[part, part, jax.ShapeDtypeStruct((1, logit.shape[0]), F32)],
        in_specs=[
            SMEM,
            whole(stat),
            whole(logit),
            whole(gap),
            pl.BlockSpec((head.shape[0] // steps, head.shape[1]), lambda i: (i, 0)),
        ],
        out_specs=[block, block, pl.BlockSpec((1, logit.shape[0]), lambda i: (0, 0))],
        scratch_shapes=[pltpu.VMEM((rows, head.shape[1]), BF16)],
        compiler_params=PARAMS,
    )(core, stat, logit, gap, head)


def spread_kernel(core_ref, part_ref, place_ref, out_ref):
    count, pad, width = out_ref.shape
    rows = part_ref.shape[1]
    total = part_ref[0].astype(F32)
    for k in range(1, part_ref.shape[0]):
        total += part_ref[k].astype(F32)
    total = total.astype(BF16)
    slots = place_ref.shape[0]
    target = iota((slots, rows), 1) + core_ref[0] * rows
    pick = (place_ref[...] == target).astype(F32).astype(BF16)
    for c in range(2):
        found = jnp.dot(
            pick, total[:, c * width : (c + 1) * width], preferred_element_type=F32
        )
        found = found.astype(BF16).reshape(count // 2, pad, width)
        for k in range(count // 2):
            out_ref[2 * k + c] = found[k]


def spread(core, parts, place, pad):
    slots = place.shape[0]
    return pl.pallas_call(
        spread_kernel,
        out_shape=jax.ShapeDtypeStruct(
            (2 * slots // pad, pad, parts.shape[2] // 2), BF16
        ),
        in_specs=[SMEM, VMEM, VMEM],
        out_specs=VMEM,
        compiler_params=PARAMS,
    )(core, parts, place)


def tail(rows, pad, operands):
    core, t, s, t_place, s_place, s_column, student_head = operands
    lanes = -(-rows // 128) * 128
    ring = lax.axis_size("y")
    logit, gap, stat = local(t, s, t_place, s_place, lanes, lax.axis_size(VOCAB))
    stat = merge(exchange(stat, VOCAB), lax.axis_size(GRP))
    stat = exchange(stat, GRP)
    keep, send, kl = gradient(core, stat, logit, gap, student_head, rows, ring)
    came = lax.ppermute(send, "c", ((0, 1), (1, 0)))
    both = (keep.astype(F32) + came.astype(F32)).astype(BF16)
    pieces = spread(core, exchange(both, "y"), s_column, pad)
    pieces = exchange(pieces, OWNER)
    grad = jnp.sum(pieces.astype(F32), axis=0).astype(BF16)
    kl = jnp.pad(kl[0], (0, t.shape[0] + pad - lanes))
    return kl, grad


def routing(lengths, owner, groups, pad):
    totals = jnp.sum(lengths.reshape(groups, -1), axis=1)
    owners = owner.reshape(groups, -1)[:, 0]
    ids = jnp.arange(groups, dtype=jnp.int32)
    step = jnp.arange(pad, dtype=jnp.int32)
    t_start = jnp.sum(jnp.where(owners[None, :] < owners[:, None], totals[None, :], 0), axis=1)
    s_start = jnp.sum(jnp.where(owners[None, :] < ids[:, None], totals[None, :], 0), axis=1)
    s_total = jnp.sum(jnp.where(owners[None, :] == ids[:, None], totals[None, :], 0), axis=1)

    def places(start, total):
        return jnp.where(step[None, :] < total[:, None], start[:, None] + step[None, :], -1)

    return places(t_start, totals), places(s_start, s_total), jnp.sum(totals)


def per_device(teacher_rows, student_rows, teacher_head, student_head, lengths, owner):
    groups = lax.axis_size(GRP)
    pad = student_rows.shape[1]
    group = lax.axis_index(GRP).astype(jnp.int32)
    core = lax.axis_index("c").astype(jnp.int32).reshape(1)
    teacher_width = teacher_rows.shape[2]
    mine = arrange(group.reshape(1), lengths, teacher_rows, student_rows, groups)
    rows = exchange(mine, GRP).reshape(groups * pad, mine.shape[2])
    rows = lax.all_gather(rows, VOCAB)
    t_place, s_place, live = routing(lengths, owner, groups, pad)
    t, s = logits(rows, teacher_head, student_head, teacher_width)
    operands = (
        core,
        t,
        s,
        t_place.reshape(1, -1),
        s_place.reshape(1, -1),
        s_place.reshape(-1, 1),
        student_head,
    )
    branches = [functools.partial(tail, c, pad) for c in CAPACITIES]
    which = sum((live > c).astype(jnp.int32) for c in CAPACITIES[:-1])
    kl, grad = lax.switch(which, branches, operands) if len(branches) > 1 else branches[0](operands)
    own = lax.dynamic_index_in_dim(s_place, group, 0, keepdims=False)
    found = lax.dynamic_slice_in_dim(kl, jnp.maximum(own[0], 0), pad, 0)
    divergence = jnp.where(own >= 0, found, 0.0)
    return divergence.reshape(1, pad), grad.reshape(1, pad, grad.shape[1])


def solution(mesh):
    torus = Mesh(mesh.devices.reshape(4, 8, 8, 2), ("x", "z", "y", "c"))
    return jax.shard_map(
        per_device,
        mesh=torus,
        in_specs=(
            P(GRP, None, VOCAB),
            P(GRP, None, VOCAB),
            P(None, (*GRP, *VOCAB)),
            P(None, (*GRP, *VOCAB)),
            P(),
            P(),
        ),
        out_specs=(P(GRP, None), P(GRP, None, VOCAB)),
        check_vma=False,
    )
```

time: 333 us -> 204 us (0.61)
  blocking collectives: 168 us -> 36.1 us
  starting transfers between devices: 6.08 us -> 22.1 us
  waiting for transfers between devices: 119 us -> 105 us
  Pallas kernels: 0 us -> 11.6 us
  matrix products: 6.54 us -> 0 us
  local copies, waits for them, and re-layouts: 14.5 us -> 10.9 us
    all_gather x6 -> x0, blocking collectives: 99.7 us -> none  [the longest x4 67.8 us: collected_together(): both, at, found = (lax.all_gather(jnp.concatenate(lines), axis), 0, {})]
    all_gather x2 -> x1, waiting for transfers between devices: 109 us -> 44.8 us  [per_device(): rows = lax.all_gather(rows, VOCAB)]
    all_to_all x1 -> x3, waiting for transfers between devices: 9.96 us -> 57.9 us  [exchange(): return lax.all_to_all(pieces, axes, 0, 0, tiled=True)]
    all_to_all x1 -> x2, blocking collectives: 68.4 us -> 36.1 us  [exchange(): return lax.all_to_all(pieces, axes, 0, 0, tiled=True)]
    all_to_all x1 -> x3, starting transfers between devices: 6 us -> 18 us  [exchange(): return lax.all_to_all(pieces, axes, 0, 0, tiled=True)]
    pallas_call x0 -> x6, Pallas kernels: none -> 11.6 us  [the longest x1 4.51 us: logits(): pl.pallas_call(functools.partial(logits_kernel, teacher_width), grid=(ste...]
    all_gather x0 -> x1, local copies, waits for them, and re-layouts: none -> 7.85 us  [per_device(): rows = lax.all_gather(rows, VOCAB)]
    dot_general x3 -> x0, matrix products: 6.54 us -> none  [the longest x1 2.92 us: per_device(): jnp.dot(lax.all_gather(teacher_full, GRP, axis=0, tiled=True), teacher_he...]
  transfers between devices with their start and end apart: 3 -> 5, of which waited for: 3 -> 5; matrix products, arithmetic and copies ran while one was open for 2% -> 1% of each run, Pallas kernels for 0% -> 0%
where the time goes in v1:
time: 204 us; the launch traced here: 203 us
  waiting for transfers between devices  105 us (51%)
  blocking collectives  36.1 us (18%)
  starting transfers between devices  22.1 us (11%)
  between operations  14.2 us (7%)
  Pallas kernels  11.6 us (6%)
  local copies, waits for them, and re-layouts  10.9 us (5%)
  other arithmetic  3.1 us (2%)
    all_to_all x3, waiting for transfers between devices, exchange(): return lax.all_to_all(pieces, axes, 0, 0, tiled=True)  57.9 us
    all_gather x1, waiting for transfers between devices, per_device(): rows = lax.all_gather(rows, VOCAB)  44.8 us
    all_to_all x2, blocking collectives, exchange(): return lax.all_to_all(pieces, axes, 0, 0, tiled=True)  36.1 us
    all_to_all x3, starting transfers between devices, exchange(): return lax.all_to_all(pieces, axes, 0, 0, tiled=True)  18 us
    all_gather x1, local copies, waits for them, and re-layouts, per_device(): rows = lax.all_gather(rows, VOCAB)  7.85 us
    pallas_call x1, Pallas kernels, logits(): pl.pallas_call(functools.partial(logits_kernel, teacher_width), grid=(ste...  4.51 us
  transfers between devices with their start and end apart: 5, of which 5 were waited for; matrix products, arithmetic and copies ran while one was open for 1% of the time, Pallas kernels for 0%

profile of v1, /device:TPU:1, one launch (start us, length us, event | category | flops | bytes accessed | tf_op | source)
XLA Modules:
  0.0 203.3 jit_solution(5468570115046112007)
XLA Ops:
  7.2 1.5 shard_map.77
  8.7 23.9 %all_to_all.25 = bf16[32,8,576]{2,1,0:T(8,128)(2,1)S(1)} all-to-all(bf16[32,8,576]{2,1,0:T(8,128)(2,1)} %shard_map.77), channel_id=1, replica_groups=mesh['x'=4,'z'=8,'y'=8,'c'=2] {'x','z'}, dimensions={0} | all-to-all | bytes 589824 | tf_op jit(solution)/shard_map/all_to_all | solution.py:27
  32.6 0.9 copy.12
  33.9 0.2 select_reduce_fusion
  34.4 44.8 %all-gather.2.cloned.1.call-done = bf16[16,256,576]{1,2,0:T(8,128)(2,1)} async-done(((bf16[1,256,576]{1,2,0:T(8,128)(2,1)}), bf16[16,256,576]{1,2,0:T(8,128)(2,1)}) %all-gather.2.cloned.1.call-update) | async-done | bytes 4718608 | tf_op jit(solution)/shard_map/all_gather | solution.py:292
  79.3 7.8 %copy.13.rows_ref = bf16[16,256,576]{2,1,0:T(8,128)(2,1)} copy(bf16[16,256,576]{1,2,0:T(8,128)(2,1)} %all-gather.2.cloned.1.call-done) | data formatting | bytes 9437184 | tf_op jit(solution)/shard_map/all_gather | solution.py:292
  87.1 1.6 copy-done.1
  88.7 4.5 %shard_map.78 = (f32[256,256]{1,0:T(8,128)S(1)}, f32[256,256]{1,0:T(8,128)S(1)}) custom-call(bf16[16,256,576]{2,1,0:T(8,128)(2,1)} %copy.13.rows_ref, bf16[4096,256]{1,0:T(8,128)(2,1)S(1)} %copy-done.1, bf16[5120,256]{1,0:T(8,128)(2,1)S(1)} %copy-done), custom_call_target="tpu_custom_call" | custom-call | tf_op jit(solution)/shard_map/pallas_call | solution.py:80
  93.2 0.9 shard_map.79
  94.2 12.2 %all_to_all.26.stat_ref = f32[16,4,256]{2,1,0:T(4,128)} all-to-all(f32[16,4,256]{2,1,0:T(4,128)S(1)} %get-tuple-element.12), channel_id=1, replica_groups=mesh['x'=4,'z'=8,'y'=8,'c'=2] {'y','c'}, dimensions={0} | all-to-all | bytes 131072 | tf_op jit(solution)/shard_map/all_to_all | solution.py:27
  106.4 1.5 shard_map.80
  107.9 9.9 %all-to-all-start.2 = ((f32[32,4,256]{2,1,0:T(4,128)}), f32[32,4,256]{2,1,0:T(4,128)S(1)}, u32[]{:S(2)}, u32[]{:S(2)}) async-start(f32[32,4,256]{2,1,0:T(4,128)} %shard_map.80), calls=%async_computation.2 | async-start | bytes 262144 | tf_op jit(solution)/shard_map/all_to_all | solution.py:27
  117.8 9.1 %all-to-all-done.2.stat_ref = f32[32,4,256]{2,1,0:T(4,128)S(1)} async-done(((f32[32,4,256]{2,1,0:T(4,128)}), f32[32,4,256]{2,1,0:T(4,128)S(1)}, u32[]{:S(2)}, u32[]{:S(2)}) %all-to-all-start.2) | async-done | bytes 131104 | tf_op jit(solution)/shard_map/all_to_all | solution.py:27
  127.0 2.0 shard_map.81
  129.0 4.0 %collective-permute-start = (bf16[8,128,640]{2,1,0:T(8,128)(2,1)S(1)}, bf16[8,128,640]{2,1,0:T(8,128)(2,1)S(1)}, u32[]{:S(2)}, u32[]{:S(2)}) collective-permute-start(bf16[8,128,640]{2,1,0:T(8,128)(2,1)S(1)} %get-tuple-element.17), channel_id=1, source_target_pairs={{0,1},{1,0},{2,3},{3,2},{4,5},{5,4},{6,7},{7,6},{8,9},{9,8},{10,11... | collective-permute-start | bytes 3932168 | tf_op jit(solution)/shard_map/ppermute | solution.py:260
  133.0 2.6 %collective-permute-done = bf16[8,128,640]{2,1,0:T(8,128)(2,1)S(1)} collective-permute-done((bf16[8,128,640]{2,1,0:T(8,128)(2,1)S(1)}, bf16[8,128,640]{2,1,0:T(8,128)(2,1)S(1)}, u32[]{:S(2)}, u32[]{:S(2)}) %collective-permute-start) | collective-permute-done | bytes 1310752 | tf_op jit(solution)/shard_map/ppermute | solution.py:260
  135.7 1.4 add_convert_fusion
  137.1 3.6 %all-to-all-start.3 = ((bf16[8,128,640]{2,1,0:T(8,128)(2,1)}), bf16[8,128,640]{2,1,0:T(8,128)(2,1)S(1)}, u32[]{:S(2)}, u32[]{:S(2)}) async-start(bf16[8,128,640]{2,1,0:T(8,128)(2,1)} %add_convert_fusion), calls=%async_computation.3 | async-start | bytes 2621440 | tf_op jit(solution)/shard_map/all_to_all | solution.py:27
  140.7 34.6 %all-to-all-done.3.part_ref = bf16[8,128,640]{2,1,0:T(8,128)(2,1)S(1)} async-done(((bf16[8,128,640]{2,1,0:T(8,128)(2,1)}), bf16[8,128,640]{2,1,0:T(8,128)(2,1)S(1)}, u32[]{:S(2)}, u32[]{:S(2)}) %all-to-all-start.3) | async-done | bytes 1310752 | tf_op jit(solution)/shard_map/all_to_all | solution.py:27
  175.4 1.1 shard_map.82
  176.5 4.5 %all-to-all-start.4 = ((bf16[64,8,320]{2,1,0:T(8,128)(2,1)}), bf16[64,8,320]{2,1,0:T(8,128)(2,1)S(1)}, u32[]{:S(2)}, u32[]{:S(2)}) async-start(bf16[64,8,320]{2,1,0:T(8,128)(2,1)} %shard_map.82), calls=%async_computation.4 | async-start | bytes 786432 | tf_op jit(solution)/shard_map/all_to_all | solution.py:27
  181.1 0.6 fusion
  181.7 14.1 %all-to-all-done.4 = bf16[64,8,320]{2,1,0:T(8,128)(2,1)S(1)} async-done(((bf16[64,8,320]{2,1,0:T(8,128)(2,1)}), bf16[64,8,320]{2,1,0:T(8,128)(2,1)S(1)}, u32[]{:S(2)}, u32[]{:S(2)}) %all-to-all-start.4) | async-done | bytes 327712 | tf_op jit(solution)/shard_map/all_to_all | solution.py:27
  195.8 0.7 reduce_sum.52
  (18 shorter events, 0.8 us)
Async XLA Ops:
  7.2 26.3 %copy-start.2 = (s32[64]{0:T(128)S(1)}, s32[64]{0:T(128)}, u32[]{:S(2)}) copy-start(s32[64]{0:T(128)} %lengths_ref.1) | copy-start | bytes 772
  7.2 26.4 %copy-start.3 = (s32[64]{0:T(128)S(1)}, s32[64]{0:T(128)}, u32[]{:S(2)}) copy-start(s32[64]{0:T(128)} %param.11) | copy-start | bytes 772
  7.2 72.1 %all-gather.2.cloned.1.call-start = ((), (), s32[]{:S(2)}) async-start(), calls=%async_computation.5 | async-start | bytes 5013504 | tf_op jit(solution)/shard_map/all_gather | solution.py:292
  79.3 7.9 %copy-start = (bf16[5120,256]{1,0:T(8,128)(2,1)S(1)}, bf16[5120,256]{1,0:T(8,128)(2,1)}, u32[]{:S(2)}) copy-start(bf16[5120,256]{1,0:T(8,128)(2,1)} %head_ref.1) | copy-start | bytes 7864324
  87.1 1.6 copy-start.1
  107.9 19.1 %all-to-all-start.2 = ((f32[32,4,256]{2,1,0:T(4,128)}), f32[32,4,256]{2,1,0:T(4,128)S(1)}, u32[]{:S(2)}, u32[]{:S(2)}) async-start(f32[32,4,256]{2,1,0:T(4,128)} %shard_map.80), calls=%async_computation.2 | async-start | bytes 262144 | tf_op jit(solution)/shard_map/all_to_all | solution.py:27
  129.0 6.7 %collective-permute-start = (bf16[8,128,640]{2,1,0:T(8,128)(2,1)S(1)}, bf16[8,128,640]{2,1,0:T(8,128)(2,1)S(1)}, u32[]{:S(2)}, u32[]{:S(2)}) collective-permute-start(bf16[8,128,640]{2,1,0:T(8,128)(2,1)S(1)} %get-tuple-element.17), channel_id=1, source_target_pairs={{0,1},{1,0},{2,3},{3,2},{4,5},{5,4},{6,7},{7,6},{8,9},{9,8},{10,11... | collective-permute-start | bytes 3932168 | tf_op jit(solution)/shard_map/ppermute | solution.py:260
  137.1 38.3 %all-to-all-start.3 = ((bf16[8,128,640]{2,1,0:T(8,128)(2,1)}), bf16[8,128,640]{2,1,0:T(8,128)(2,1)S(1)}, u32[]{:S(2)}, u32[]{:S(2)}) async-start(bf16[8,128,640]{2,1,0:T(8,128)(2,1)} %add_convert_fusion), calls=%async_computation.3 | async-start | bytes 2621440 | tf_op jit(solution)/shard_map/all_to_all | solution.py:27
  176.5 19.3 %all-to-all-start.4 = ((bf16[64,8,320]{2,1,0:T(8,128)(2,1)}), bf16[64,8,320]{2,1,0:T(8,128)(2,1)S(1)}, u32[]{:S(2)}, u32[]{:S(2)}) async-start(bf16[64,8,320]{2,1,0:T(8,128)(2,1)} %shard_map.82), calls=%async_computation.4 | async-start | bytes 786432 | tf_op jit(solution)/shard_map/all_to_all | solution.py:27
Sparse Core Ops, SparseCore 0:
  33.6 45.6 all-gather.1

commit v2 on v1

v2 whole, which is shorter than its diff:
```python
import functools

import jax
import jax.numpy as jnp
from jax import lax
from jax.experimental import pallas as pl
from jax.experimental.pallas import tpu as pltpu
from jax.sharding import Mesh
from jax.sharding import PartitionSpec as P

GRP = ("x", "z")
VOCAB = ("y", "c")
OWNER = ("x", "z", "c")
CAPACITIES = (128, 160, 256)
F32 = jnp.float32
BF16 = jnp.bfloat16
VMEM = pl.BlockSpec(memory_space=pltpu.VMEM)
SMEM = pl.BlockSpec(memory_space=pltpu.SMEM)
PARAMS = pltpu.CompilerParams(vmem_limit_bytes=20 * 1024 * 1024)


def iota(shape, dim):
    return lax.broadcasted_iota(jnp.int32, shape, dim)


def exchange(pieces, axes):
    return lax.all_to_all(pieces, axes, 0, 0, tiled=True)


def arrange_kernel(group_ref, lengths_ref, teacher_ref, student_ref, out_ref):
    count, pad, _ = out_ref.shape
    width = teacher_ref.shape[2]
    rest = out_ref.shape[2] - width - student_ref.shape[2]
    first = lengths_ref[2 * group_ref[0]]
    upper = teacher_ref[0].astype(F32)
    lower = pltpu.roll(teacher_ref[1].astype(F32), first, 0)
    chosen = jnp.where(iota(upper.shape, 0) < first, upper, lower).astype(BF16)
    for k in range(count):
        out_ref[k, :, :width] = chosen
        out_ref[k, :, width : width + student_ref.shape[2]] = student_ref[0]
        if rest:
            out_ref[k, :, -rest:] = jnp.zeros((pad, rest), BF16)


def arrange(group, lengths, teacher_rows, student_rows, count):
    pad = student_rows.shape[1]
    width = -(-(teacher_rows.shape[2] + student_rows.shape[2]) // 128) * 128
    return pl.pallas_call(
        arrange_kernel,
        out_shape=jax.ShapeDtypeStruct((count, pad, width), BF16),
        in_specs=[SMEM, SMEM, VMEM, VMEM],
        out_specs=VMEM,
    )(group, lengths, teacher_rows, student_rows)


def stage_kernel(teacher_ref, student_ref, t_out_ref, s_out_ref, sems):
    copies = [
        pltpu.make_async_copy(teacher_ref, t_out_ref, sems.at[0]),
        pltpu.make_async_copy(student_ref, s_out_ref, sems.at[1]),
    ]
    for copy in copies:
        copy.start()
    for copy in copies:
        copy.wait()


def stage(teacher_head, student_head):
    size = 2 * (teacher_head.size + student_head.size)
    return pl.pallas_call(
        stage_kernel,
        out_shape=[
            jax.ShapeDtypeStruct(teacher_head.shape, BF16),
            jax.ShapeDtypeStruct(student_head.shape, BF16),
        ],
        in_specs=[pl.BlockSpec(memory_space=pl.ANY)] * 2,
        out_specs=[VMEM] * 2,
        scratch_shapes=[pltpu.SemaphoreType.DMA((2,))],
        compiler_params=PARAMS,
        cost_estimate=pl.CostEstimate(flops=0, bytes_accessed=2 * size, transcendentals=0),
    )(teacher_head, student_head)


def logits_step(teacher_width, steps, rows_ref, teacher_ref, student_ref, t_ref, s_ref):
    @pl.when(pl.program_id(0) == 0)
    def _():
        t_ref[...] = jnp.zeros_like(t_ref)
        s_ref[...] = jnp.zeros_like(s_ref)

    pieces = range(rows_ref.shape[0])
    student_width = student_ref.shape[0] // (steps * len(pieces))
    whole = student_width // 128 * 128
    end = teacher_width + whole
    stop = teacher_width + student_width
    step = pl.program_id(0)
    deep = len(pieces) * teacher_width
    first = pl.multiple_of(step * deep, deep)
    t_ref[...] += jnp.dot(
        jnp.concatenate([rows_ref[k, :, :teacher_width] for k in pieces], axis=1),
        teacher_ref[pl.ds(first, deep), :],
        preferred_element_type=F32,
    )
    base = step * len(pieces) * student_width

    def heads(k, start, count):
        return student_ref[pl.ds(pl.multiple_of(base + k * student_width + start, 64), count), :]

    s_ref[...] += jnp.dot(
        jnp.concatenate(
            [rows_ref[k, :, teacher_width:end] for k in pieces]
            + [rows_ref[k, :, end:stop] for k in pieces],
            axis=1,
        ),
        jnp.concatenate(
            [heads(k, 0, whole) for k in pieces]
            + [heads(k, whole, student_width - whole) for k in pieces],
            axis=0,
        ),
        preferred_element_type=F32,
    )


def logits(rows, teacher_head, student_head, teacher_width):
    count, slots, width = rows.shape
    steps = 4
    vocab = teacher_head.shape[1]
    return pl.pallas_call(
        functools.partial(logits_step, teacher_width, steps),
        grid=(steps,),
        out_shape=[jax.ShapeDtypeStruct((slots, vocab), F32)] * 2,
        in_specs=[
            pl.BlockSpec((count // steps, slots, width), lambda i: (i, 0, 0)),
            VMEM,
            VMEM,
        ],
        out_specs=[pl.BlockSpec((slots, vocab), lambda i: (0, 0))] * 2,
        compiler_params=pltpu.CompilerParams(vmem_limit_bytes=50 * 1024 * 1024),
    )(rows, teacher_head, student_head)


def local_kernel(t_ref, s_ref, t_place_ref, s_place_ref, logit_ref, gap_ref, stat_ref):
    lanes = logit_ref.shape[0]
    place = iota((lanes, t_ref.shape[0]), 0)

    def packed(place_ref, ref):
        pick = (place == place_ref[...]).astype(F32)
        return jnp.dot(
            pick, ref[...], preferred_element_type=F32, precision=lax.Precision.HIGHEST
        )

    t = packed(t_place_ref, t_ref)
    s = packed(s_place_ref, s_ref)
    gap = s - t
    t_top = jnp.max(t, axis=1, keepdims=True)
    t_lse = t_top + jnp.log(jnp.sum(jnp.exp(t - t_top), axis=1, keepdims=True))
    s_top = jnp.max(s, axis=1, keepdims=True)
    e = jnp.exp(s - s_top)
    total = jnp.sum(e, axis=1, keepdims=True)
    weighted = jnp.sum(e * gap, axis=1, keepdims=True)
    logit_ref[...] = s
    gap_ref[...] = gap
    lane = iota((lanes, 128), 1)
    table = jnp.where(
        lane == 0,
        s_top,
        jnp.where(lane == 1, total, jnp.where(lane == 2, weighted, t_lse)),
    )
    table = table.T[:4]
    for k in range(stat_ref.shape[0]):
        stat_ref[k] = table


def local(t, s, t_place, s_place, lanes, count):
    return pl.pallas_call(
        local_kernel,
        out_shape=[
            jax.ShapeDtypeStruct((lanes, t.shape[1]), F32),
            jax.ShapeDtypeStruct((lanes, t.shape[1]), F32),
            jax.ShapeDtypeStruct((count, 4, lanes), F32),
        ],
        in_specs=[VMEM] * 4,
        out_specs=[VMEM] * 3,
        compiler_params=PARAMS,
    )(t, s, t_place, s_place)


def merged(stat_ref):
    top = stat_ref[:, 0, :]
    high = jnp.max(top, axis=0, keepdims=True)
    scale = jnp.exp(top - high)
    total = jnp.sum(scale * stat_ref[:, 1, :], axis=0, keepdims=True)
    weighted = jnp.sum(scale * stat_ref[:, 2, :], axis=0, keepdims=True)
    t_lse = stat_ref[:, 3, :]
    t_high = jnp.max(t_lse, axis=0, keepdims=True)
    t_lse = t_high + jnp.log(jnp.sum(jnp.exp(t_lse - t_high), axis=0, keepdims=True))
    return high, total, weighted, t_lse


def merge_kernel(stat_ref, out_ref):
    high, total, weighted, t_lse = merged(stat_ref)
    table = jnp.concatenate([high, total, weighted, t_lse], axis=0)
    for k in range(out_ref.shape[0]):
        out_ref[k] = table


def merge(stat, count):
    return pl.pallas_call(
        merge_kernel,
        out_shape=jax.ShapeDtypeStruct((count, *stat.shape[1:]), F32),
        in_specs=[VMEM],
        out_specs=VMEM,
    )(stat)


def gradient_kernel(
    info_ref, stat_ref, logit_ref, gap_ref, head_ref, keep_ref, send_ref, kl_ref, g_ref
):
    @pl.when(pl.program_id(0) == 0)
    def _():
        high, total, weighted, t_lse = merged(stat_ref)
        lanes = high.shape[1]
        mean = weighted / total
        kl = jnp.broadcast_to(mean - (high + jnp.log(total)) + t_lse, (8, lanes))
        kl = pltpu.roll(kl, lax.rem(lanes - info_ref[2], lanes), 1)[:1, :128]
        kl_ref[...] = jnp.where(iota((1, 128), 1) < info_ref[3], kl, 0.0)
        row = iota((128, lanes), 0)
        table = jnp.where(row == 0, high, jnp.where(row == 1, 1.0 / total, mean)).T
        q = jnp.exp(logit_ref[...] - table[:, 0:1]) * table[:, 1:2]
        g = q * (gap_ref[...] - table[:, 2:3])
        g_ref[...] = g[: g_ref.shape[0]].astype(BF16)

    width = keep_ref.shape[2]
    half = keep_ref.shape[1]
    low = info_ref[1] == 0
    for k in range(keep_ref.shape[0]):
        part = lax.dot_general(
            g_ref[...],
            head_ref[k * width : (k + 1) * width, :],
            (((1,), (1,)), ((), ())),
            preferred_element_type=F32,
        ).astype(BF16)
        keep_ref[k] = jnp.where(low, part[:half], part[half:])
        send_ref[k] = jnp.where(low, part[half:], part[:half])


def gradient(info, stat, logit, gap, head, rows, count):
    steps = 4
    width = head.shape[0] // count
    part = jax.ShapeDtypeStruct((count, rows // 2, width), BF16)
    block = pl.BlockSpec((count // steps, rows // 2, width), lambda i: (i, 0, 0))
    whole = lambda a: pl.BlockSpec(a.shape, lambda i: (0,) * a.ndim)
    return pl.pallas_call(
        gradient_kernel,
        grid=(steps,),
        out_shape=[part, part, jax.ShapeDtypeStruct((1, 128), F32)],
        in_specs=[
            SMEM,
            whole(stat),
            whole(logit),
            whole(gap),
            pl.BlockSpec((head.shape[0] // steps, head.shape[1]), lambda i: (i, 0)),
        ],
        out_specs=[block, block, pl.BlockSpec((1, 128), lambda i: (0, 0))],
        scratch_shapes=[pltpu.VMEM((rows, head.shape[1]), BF16)],
        compiler_params=PARAMS,
    )(info, stat, logit, gap, head)


def spread_kernel(info_ref, part_ref, place_ref, out_ref):
    count, pad, width = out_ref.shape
    rows = part_ref.shape[1]
    total = part_ref[0].astype(F32)
    for k in range(1, part_ref.shape[0]):
        total += part_ref[k].astype(F32)
    total = total.astype(BF16)
    slots = place_ref.shape[0]
    target = iota((slots, rows), 1) + info_ref[1] * rows
    pick = (place_ref[:, :rows] == target).astype(F32).astype(BF16)
    for c in range(2):
        found = jnp.dot(
            pick, total[:, c * width : (c + 1) * width], preferred_element_type=F32
        )
        found = found.astype(BF16).reshape(count // 2, pad, width)
        for k in range(count // 2):
            out_ref[2 * k + c] = found[k]


def spread(info, parts, place, pad):
    slots = place.shape[0]
    return pl.pallas_call(
        spread_kernel,
        out_shape=jax.ShapeDtypeStruct(
            (2 * slots // pad, pad, parts.shape[2] // 2), BF16
        ),
        in_specs=[SMEM, VMEM, VMEM],
        out_specs=VMEM,
        compiler_params=PARAMS,
    )(info, parts, place)


def tail(rows, pad, operands):
    info, t, s, t_place, s_place, s_column, student_head = operands
    lanes = -(-rows // 128) * 128
    ring = lax.axis_size("y")
    logit, gap, stat = local(t, s, t_place, s_place, lanes, lax.axis_size(VOCAB))
    stat = merge(exchange(stat, VOCAB), lax.axis_size(GRP))
    stat = exchange(stat, GRP)
    keep, send, kl = gradient(info, stat, logit, gap, student_head, rows, ring)
    came = lax.ppermute(send, "c", ((0, 1), (1, 0)))
    both = (keep.astype(F32) + came.astype(F32)).astype(BF16)
    pieces = spread(info, exchange(both, "y"), s_column, pad)
    pieces = exchange(pieces, OWNER)
    grad = jnp.sum(pieces.astype(F32), axis=0).astype(BF16)
    return kl, grad


def routing_kernel(
    groups, pad, group_ref, core_ref, lengths_ref, owner_ref, t_ref, s_ref, column_ref, info_ref, start_ref
):
    share = lengths_ref.shape[0] // groups

    def total(g):
        return sum(lengths_ref[share * g + k] for k in range(share))

    def owned(j, found):
        g, count = found
        return lax.fori_loop(
            0,
            groups,
            lambda i, f: (
                jnp.where(owner_ref[share * i] == j, i, f[0]),
                jnp.where(owner_ref[share * i] == j, total(i), f[1]),
            ),
            (g, count),
        )

    lane = iota(t_ref.shape, 1)
    column = iota(column_ref.shape, 0)
    zero = jnp.int32(0)

    def place(j, carry):
        t, s, wide, start = carry
        g, count = owned(j, (zero, zero))
        s_step = lane - j * pad
        t_step = lane - g * pad
        down = column - j * pad
        t = jnp.where((t_step >= 0) & (t_step < count), start + t_step, t)
        s = jnp.where((s_step >= 0) & (s_step < count), start + s_step, s)
        wide = jnp.where((down >= 0) & (down < count), start + down, wide)
        start_ref[j] = start
        start_ref[groups + j] = count
        return t, s, wide, start + count

    none = jnp.full(t_ref.shape, -1, jnp.int32)
    t, s, wide, live = lax.fori_loop(
        0, groups, place, (none, none, jnp.full(column_ref.shape, -1, jnp.int32), zero)
    )
    t_ref[...] = t
    s_ref[...] = s
    column_ref[...] = wide
    which = zero
    for c in CAPACITIES[:-1]:
        which += (live > c).astype(jnp.int32)
    info_ref[0] = which
    info_ref[1] = core_ref[0]
    info_ref[2] = start_ref[group_ref[0]]
    info_ref[3] = start_ref[groups + group_ref[0]]


def routing(group, core, lengths, owner, groups, pad):
    slots = groups * pad
    return pl.pallas_call(
        functools.partial(routing_kernel, groups, pad),
        out_shape=[
            jax.ShapeDtypeStruct((1, slots), jnp.int32),
            jax.ShapeDtypeStruct((1, slots), jnp.int32),
            jax.ShapeDtypeStruct((slots, 128), jnp.int32),
            jax.ShapeDtypeStruct((4,), jnp.int32),
        ],
        in_specs=[SMEM] * 4,
        out_specs=[VMEM] * 3 + [SMEM],
        scratch_shapes=[pltpu.SMEM((2 * groups,), jnp.int32)],
        cost_estimate=pl.CostEstimate(flops=10**8, bytes_accessed=10**6, transcendentals=0),
    )(group, core, lengths, owner)


def per_device(teacher_rows, student_rows, teacher_head, student_head, lengths, owner):
    groups = lax.axis_size(GRP)
    pad = student_rows.shape[1]
    group = lax.axis_index(GRP).astype(jnp.int32).reshape(1)
    core = lax.axis_index("c").astype(jnp.int32).reshape(1)
    mine = arrange(group, lengths, teacher_rows, student_rows, groups)
    rows = exchange(mine, GRP).reshape(groups * pad, mine.shape[2])
    rows = lax.all_gather(rows, VOCAB, axis=0, tiled=True)
    rows = rows.reshape(-1, groups * pad, mine.shape[2])
    t_place, s_place, s_column, info = routing(group, core, lengths, owner, groups, pad)
    t_head, s_head = stage(teacher_head, student_head)
    t, s = logits(rows, t_head, s_head, teacher_rows.shape[2])
    operands = (info, t, s, t_place, s_place, s_column, student_head)
    branches = [functools.partial(tail, c, pad) for c in CAPACITIES]
    kl, grad = lax.switch(info[0], branches, operands)
    return kl[:, :pad], grad.reshape(1, pad, grad.shape[1])


def solution(mesh):
    torus = Mesh(mesh.devices.reshape(4, 8, 8, 2), ("x", "z", "y", "c"))
    return jax.shard_map(
        per_device,
        mesh=torus,
        in_specs=(
            P(GRP, None, VOCAB),
            P(GRP, None, VOCAB),
            P(None, (*GRP, *VOCAB)),
            P(None, (*GRP, *VOCAB)),
            P(),
            P(),
        ),
        out_specs=(P(GRP, None), P(GRP, None, VOCAB)),
        check_vma=False,
    )
```

time: 204 us -> 177 us (0.87)
  waiting for transfers between devices: 105 us -> 29.7 us
  blocking collectives: 36.1 us -> 96.1 us
  starting transfers between devices: 22.1 us -> 3.77 us
  Pallas kernels: 11.6 us -> 28.6 us
  local copies, waits for them, and re-layouts: 10.9 us -> 3.65 us
  other arithmetic: 3.1 us -> 0.25 us
    all_to_all x2 -> x5, blocking collectives: 36.1 us -> 96.1 us  [exchange(): return lax.all_to_all(pieces, axes, 0, 0, tiled=True)]
    all_to_all x3 -> x0, waiting for transfers between devices: 57.9 us -> none  [exchange(): return lax.all_to_all(pieces, axes, 0, 0, tiled=True)]
    all_to_all x3 -> x0, starting transfers between devices: 18 us -> none  [exchange(): return lax.all_to_all(pieces, axes, 0, 0, tiled=True)]
    all_gather x1, waiting for transfers between devices: 44.8 us -> 28 us  [per_device(): rows = lax.all_gather(rows, VOCAB, axis=0, tiled=True)]
    pallas_call x1 -> x3, Pallas kernels: 4.51 us -> 20.4 us  [the longest x1 13.4 us: routing(): pl.pallas_call(functools.partial(routing_kernel, groups, pad), out_shape=...]
    all_gather x1 -> x0, local copies, waits for them, and re-layouts: 7.85 us -> none  [per_device(): rows = lax.all_gather(rows, VOCAB)]
    unnamed x8 -> x6, local copies, waits for them, and re-layouts: 1.6 us -> 3.65 us
  transfers between devices with their start and end apart: 5 -> 2, of which waited for: 5 -> 2; matrix products, arithmetic and copies ran while one was open for 1% -> 0% of each run, Pallas kernels for 0% -> 9%
where the time goes in v2:
time: 177 us; the launch traced here: 176 us
  blocking collectives  96.1 us (54%)
  waiting for transfers between devices  29.7 us (17%)
  Pallas kernels  28.6 us (16%)
  between operations  14.1 us (8%)
  starting transfers between devices  3.77 us (2%)
  local copies, waits for them, and re-layouts  3.65 us (2%)
    all_to_all x5, blocking collectives, exchange(): return lax.all_to_all(pieces, axes, 0, 0, tiled=True)  96.1 us
    all_gather x1, waiting for transfers between devices, per_device(): rows = lax.all_gather(rows, VOCAB, axis=0, tiled=True)  28 us
    pallas_call x1, Pallas kernels, routing(): pl.pallas_call(functools.partial(routing_kernel, groups, pad), out_shape=...  13.4 us
    pallas_call x1, Pallas kernels, logits(): pl.pallas_call(functools.partial(logits_step, teacher_width, steps), grid...  5.06 us
    pallas_call x1, Pallas kernels, gradient(): pl.pallas_call(gradient_kernel, grid=(steps,), out_shape=[part, part, jax...  3.77 us
    ppermute x1, starting transfers between devices, tail(): came = lax.ppermute(send, 'c', ((0, 1), (1, 0)))  3.73 us
    unnamed x6, local copies, waits for them, and re-layouts  3.65 us
  transfers between devices with their start and end apart: 2, of which 2 were waited for; matrix products, arithmetic and copies ran while one was open for 0% of the time, Pallas kernels for 9%

profile of v2, /device:TPU:1, one launch (start us, length us, event | category | flops | bytes accessed | tf_op | source)
XLA Modules:
  0.0 176.3 jit_solution(9489473029438667653)
XLA Ops:
  7.2 0.0 all-gather.2.cloned.1.call-start
  7.2 1.5 shard_map.78
  8.7 24.0 %all_to_all.65 = bf16[32,8,640]{2,1,0:T(8,128)(2,1)} all-to-all(bf16[32,8,640]{2,1,0:T(8,128)(2,1)} %shard_map.78), channel_id=1, replica_groups=mesh['x'=4,'z'=8,'y'=8,'c'=2] {'x','z'}, dimensions={0} | all-to-all | bytes 655360 | tf_op jit(solution)/shard_map/all_to_all | solution.py:27
  32.7 0.0 all-gather.2.cloned.1.call-update
  32.7 1.6 copy-done.1
  34.3 1.9 %shard_map.79 = (bf16[4096,256]{1,0:T(8,128)(2,1)S(1)}, bf16[5120,256]{1,0:T(8,128)(2,1)S(1)}) custom-call(bf16[4096,256]{1,0:T(8,128)(2,1)S(1)} %copy-done.1, bf16[5120,256]{1,0:T(8,128)(2,1)} %student_ref.3), custom_call_target="tpu_custom_call" | custom-call | bytes 9437184 | tf_op jit(solution)/shard_map/pallas_call | solution.py:69
  36.2 1.5 copy-done
  37.7 13.4 %shard_map.77 = (s32[1,256]{1,0:T(1,128)S(1)}, s32[1,256]{1,0:T(1,128)S(1)}, s32[256,128]{1,0:T(8,128)S(1)}, s32[4]{0:T(128)S(1)}) custom-call(s32[1]{0:T(128)} %bitcast.3.group_ref, s32[1]{0:T(128)} %bitcast.4.core_ref, s32[64]{0:T(128)} %lengths_ref.3, s32[64]{0:T(128)} %owner_ref.1), custom_call_target="tpu_custom_call" | custom-call | flops 100000000 | bytes 1000000 | tf_op jit(solution)/shard_map/pallas_call | solution.py:371
  51.2 28.0 %all-gather.2.cloned.1.call-done = bf16[4096,640]{1,0:T(8,128)(2,1)} async-done(((bf16[256,640]{1,0:T(8,128)(2,1)}), bf16[4096,640]{1,0:T(8,128)(2,1)}) %all-gather.2.cloned.1.call-update) | async-done | bytes 5242896 | tf_op jit(solution)/shard_map/all_gather | solution.py:393
  79.2 5.1 %shard_map.80 = (f32[256,256]{1,0:T(8,128)S(1)}, f32[256,256]{1,0:T(8,128)S(1)}) custom-call(bf16[16,256,640]{2,1,0:T(8,128)(2,1)} %bitcast.10, bf16[4096,256]{1,0:T(8,128)(2,1)S(1)} %get-tuple-element.95.teacher_ref, bf16[5120,256]{1,0:T(8,128)(2,1)} %copy-done), custom_call_target="tpu_custom_call" | custom-call | tf_op jit(solution)/shard_map/pallas_call | solution.py:126
  84.2 84.6 %conditional.1 = (f32[1,128]{1,0:T(1,128)}, bf16[1,8,320]{2,1,0:T(8,128)(2,1)S(1)}) conditional(s32[]{:T(128)} %bitcast.5, (f32[256,256]{1,0:T(8,128)S(1)}, f32[256,256]{1,0:T(8,128)S(1)}, s32[1,256]{1,0:T(1,128)S(1)}, s32[1,256]{1,0:T(1,128)S(1)}, s32[4]{0:T(128)S(1)}, /*index=5*/bf16[5120,256]{1,0:T(8,128)(2,1)}, ...), branch_computations={%region_0.0_spmd, %region_2.0_spmd, %region_4.0_spmd} | conditional | flops 2782720 | bytes 13177914 | solution.py:400
  84.2 0.7 branch_0_fun.4
  84.9 11.7 %all_to_all.53.stat_ref = f32[16,4,128]{2,1,0:T(4,128)} all-to-all(f32[16,4,128]{2,1,0:T(4,128)S(1)} %get-tuple-element.48), channel_id=1, replica_groups=mesh['x'=4,'z'=8,'y'=8,'c'=2] {'y','c'}, dimensions={0} | all-to-all | bytes 65536 | tf_op jit(solution)/shard_map/cond/branch_0_fun/all_to_all | solution.py:27
  96.7 1.4 branch_0_fun.5
  98.1 18.8 %all_to_all.54.stat_ref = f32[32,4,128]{2,1,0:T(4,128)S(1)} all-to-all(f32[32,4,128]{2,1,0:T(4,128)} %branch_0_fun.5), channel_id=1, replica_groups=mesh['x'=4,'z'=8,'y'=8,'c'=2] {'x','z'}, dimensions={0} | all-to-all | bytes 131072 | tf_op jit(solution)/shard_map/cond/branch_0_fun/all_to_all | solution.py:27
  116.9 3.8 %branch_0_fun.6 = (bf16[8,64,640]{2,1,0:T(8,128)(2,1)S(1)}, bf16[8,64,640]{2,1,0:T(8,128)(2,1)S(1)}, f32[1,128]{1,0:T(1,128)}) custom-call(s32[4]{0:T(128)S(1)} %get-tuple-element.43.info_ref, f32[32,4,128]{2,1,0:T(4,128)S(1)} %all_to_all.54.stat_ref, f32[128,256]{1,0:T(8,128)S(1)} %get-tuple-element.49.logit_ref, f32[128,256]{1,0:T(8,128)S(1)} %get-tuple-element.50.gap_ref, ...), custom_call_target="tpu_custom_call" | custom-call | tf_op jit(solution)/shard_map/cond/branch_0_fun/pallas_call | solution.py:251
  120.6 3.7 %collective-permute-start = (bf16[8,64,640]{2,1,0:T(8,128)(2,1)S(1)}, bf16[8,64,640]{2,1,0:T(8,128)(2,1)S(1)}, u32[]{:S(2)}, u32[]{:S(2)}) collective-permute-start(bf16[8,64,640]{2,1,0:T(8,128)(2,1)S(1)} %get-tuple-element.54), channel_id=1, source_target_pairs={{0,1},{1,0},{2,3},{3,2},{4,5},{5,4},{6,7},{7,6},{8,9},{9,8},{10,11... | collective-permute-start | bytes 1966088 | tf_op jit(solution)/shard_map/cond/branch_0_fun/ppermute | solution.py:308
  124.4 1.7 collective-permute-done
  126.1 0.2 add_convert_fusion
  126.2 23.2 %all_to_all.55.part_ref = bf16[8,64,640]{2,1,0:T(8,128)(2,1)S(1)} all-to-all(bf16[8,64,640]{2,1,0:T(8,128)(2,1)S(1)} %add_convert_fusion), channel_id=1, replica_groups=mesh['x'=4,'z'=8,'y'=8,'c'=2] {'y'}, dimensions={0} | all-to-all | bytes 1310720 | tf_op jit(solution)/shard_map/cond/branch_0_fun/all_to_all | solution.py:27
  149.4 0.9 branch_0_fun.7
  150.3 18.4 %all_to_all.56 = bf16[64,8,320]{2,1,0:T(8,128)(2,1)S(1)} all-to-all(bf16[64,8,320]{2,1,0:T(8,128)(2,1)S(1)} %branch_0_fun.7), channel_id=1, replica_groups=mesh['x'=4,'z'=8,'y'=8,'c'=2] {'x','z','c'}, dimensions={0} | all-to-all | bytes 655360 | tf_op jit(solution)/shard_map/cond/branch_0_fun/all_to_all | solution.py:27
  168.7 0.1 reduce_sum.33
  168.8 0.6 copy-done.2
  (3 shorter events, 0.0 us)
Async XLA Ops:
  7.2 72.0 %all-gather.2.cloned.1.call-start = ((), (), s32[]{:S(2)}) async-start(), calls=%async_computation.13 | async-start | bytes 5570560 | tf_op jit(solution)/shard_map/all_gather | solution.py:393
  32.7 1.6 copy-start.1
  36.2 1.5 copy-start
  120.6 5.4 %collective-permute-start = (bf16[8,64,640]{2,1,0:T(8,128)(2,1)S(1)}, bf16[8,64,640]{2,1,0:T(8,128)(2,1)S(1)}, u32[]{:S(2)}, u32[]{:S(2)}) collective-permute-start(bf16[8,64,640]{2,1,0:T(8,128)(2,1)S(1)} %get-tuple-element.54), channel_id=1, source_target_pairs={{0,1},{1,0},{2,3},{3,2},{4,5},{5,4},{6,7},{7,6},{8,9},{9,8},{10,11... | collective-permute-start | bytes 1966088 | tf_op jit(solution)/shard_map/cond/branch_0_fun/ppermute | solution.py:308
  168.8 0.6 copy-start.2
Sparse Core Ops, SparseCore 0:
  32.8 46.2 all-gather.1

commit v3 on v2

v3 whole, which is shorter than its diff:
```python
import functools

import jax
import jax.numpy as jnp
from jax import lax
from jax.experimental import pallas as pl
from jax.experimental.pallas import tpu as pltpu
from jax.sharding import Mesh
from jax.sharding import PartitionSpec as P

GRP = ("x", "z")
VOCAB = ("y", "c")
CAPACITIES = (128, 256)
F32 = jnp.float32
BF16 = jnp.bfloat16
VMEM = pl.BlockSpec(memory_space=pltpu.VMEM)
SMEM = pl.BlockSpec(memory_space=pltpu.SMEM)
PARAMS = pltpu.CompilerParams(vmem_limit_bytes=20 * 1024 * 1024)


def iota(shape, dim):
    return lax.broadcasted_iota(jnp.int32, shape, dim)


def exchange(pieces, axes):
    return lax.all_to_all(pieces, axes, 0, 0, tiled=True)


def arrange_kernel(group_ref, lengths_ref, teacher_ref, student_ref, out_ref):
    count, pad, _ = out_ref.shape
    width = teacher_ref.shape[2]
    rest = out_ref.shape[2] - width - student_ref.shape[2]
    first = lengths_ref[2 * group_ref[0]]
    upper = teacher_ref[0].astype(F32)
    lower = pltpu.roll(teacher_ref[1].astype(F32), first, 0)
    chosen = jnp.where(iota(upper.shape, 0) < first, upper, lower).astype(BF16)
    for k in range(count):
        out_ref[k, :, :width] = chosen
        out_ref[k, :, width : width + student_ref.shape[2]] = student_ref[0]
        if rest:
            out_ref[k, :, -rest:] = jnp.zeros((pad, rest), BF16)


def arrange(group, lengths, teacher_rows, student_rows, count):
    pad = student_rows.shape[1]
    width = -(-(teacher_rows.shape[2] + student_rows.shape[2]) // 128) * 128
    return pl.pallas_call(
        arrange_kernel,
        out_shape=jax.ShapeDtypeStruct((count, pad, width), BF16),
        in_specs=[SMEM, SMEM, VMEM, VMEM],
        out_specs=VMEM,
    )(group, lengths, teacher_rows, student_rows)


def stage_kernel(teacher_ref, student_ref, t_out_ref, s_out_ref, sems):
    copies = [
        pltpu.make_async_copy(teacher_ref, t_out_ref, sems.at[0]),
        pltpu.make_async_copy(student_ref, s_out_ref, sems.at[1]),
    ]
    for copy in copies:
        copy.start()
    for copy in copies:
        copy.wait()


def stage(teacher_head, student_head):
    size = 2 * (teacher_head.size + student_head.size)
    return pl.pallas_call(
        stage_kernel,
        out_shape=[
            jax.ShapeDtypeStruct(teacher_head.shape, BF16),
            jax.ShapeDtypeStruct(student_head.shape, BF16),
        ],
        in_specs=[pl.BlockSpec(memory_space=pl.ANY)] * 2,
        out_specs=[VMEM] * 2,
        scratch_shapes=[pltpu.SemaphoreType.DMA((2,))],
        compiler_params=PARAMS,
        cost_estimate=pl.CostEstimate(flops=0, bytes_accessed=2 * size, transcendentals=0),
    )(teacher_head, student_head)


def logits_step(teacher_width, steps, rows_ref, teacher_ref, student_ref, t_ref, s_ref):
    @pl.when(pl.program_id(0) == 0)
    def _():
        t_ref[...] = jnp.zeros_like(t_ref)
        s_ref[...] = jnp.zeros_like(s_ref)

    pieces = range(rows_ref.shape[0])
    student_width = student_ref.shape[0] // (steps * len(pieces))
    whole = student_width // 128 * 128
    end = teacher_width + whole
    stop = teacher_width + student_width
    step = pl.program_id(0)
    deep = len(pieces) * teacher_width
    first = pl.multiple_of(step * deep, deep)
    t_ref[...] += jnp.dot(
        jnp.concatenate([rows_ref[k, :, :teacher_width] for k in pieces], axis=1),
        teacher_ref[pl.ds(first, deep), :],
        preferred_element_type=F32,
    )
    base = step * len(pieces) * student_width

    def heads(k, start, count):
        return student_ref[pl.ds(pl.multiple_of(base + k * student_width + start, 64), count), :]

    s_ref[...] += jnp.dot(
        jnp.concatenate(
            [rows_ref[k, :, teacher_width:end] for k in pieces]
            + [rows_ref[k, :, end:stop] for k in pieces],
            axis=1,
        ),
        jnp.concatenate(
            [heads(k, 0, whole) for k in pieces]
            + [heads(k, whole, student_width - whole) for k in pieces],
            axis=0,
        ),
        preferred_element_type=F32,
    )

    @pl.when(step == steps - 1)
    def _():
        t_ref[...] = t_ref[...].T
        s_ref[...] = s_ref[...].T


def logits(rows, teacher_head, student_head, teacher_width):
    count, slots, width = rows.shape
    steps = 4
    vocab = teacher_head.shape[1]
    return pl.pallas_call(
        functools.partial(logits_step, teacher_width, steps),
        grid=(steps,),
        out_shape=[jax.ShapeDtypeStruct((slots, vocab), F32)] * 2,
        in_specs=[
            pl.BlockSpec((count // steps, slots, width), lambda i: (i, 0, 0)),
            VMEM,
            VMEM,
        ],
        out_specs=[pl.BlockSpec((slots, vocab), lambda i: (0, 0))] * 2,
        compiler_params=pltpu.CompilerParams(vmem_limit_bytes=50 * 1024 * 1024),
    )(rows, teacher_head, student_head)


def in_parts(stats, lanes):
    row = iota((16, lanes), 0)
    table = jnp.zeros((16, lanes), F32)
    for k, value in enumerate(stats):
        for part in range(3):
            rounded = value.astype(BF16).astype(F32)
            table = jnp.where(row == 3 * k + part, rounded, table)
            value = value - rounded
    return table


def from_parts(table, lanes):
    rows = [table[k : k + 1, :lanes] for k in range(9)]
    return [rows[k] + rows[k + 1] + rows[k + 2] for k in (0, 3, 6)]


def merged(stats):
    lse, mean, t_lse = zip(*stats)
    high = functools.reduce(jnp.maximum, lse)
    t_high = functools.reduce(jnp.maximum, t_lse)
    scale = [jnp.exp(v - high) for v in lse]
    total = sum(scale[1:], scale[0])
    scale = [v / total for v in scale]
    middle = sum((a * v for a, v in zip(scale[1:], mean[1:])), scale[0] * mean[0])
    t_total = sum((jnp.exp(v - t_high) for v in t_lse[1:]), jnp.exp(t_lse[0] - t_high))
    shift = [v - middle for v in mean]
    return scale, shift, [high + jnp.log(total), middle, t_high + jnp.log(t_total)]


def partial_kernel(
    info_ref, t_ref, s_ref, t_place_ref, s_place_ref, head_ref, keep_ref, send_ref, g_ref, stat_ref
):
    lanes = g_ref.shape[1] // 2

    @pl.when(pl.program_id(0) == 0)
    def _():
        def packed(place_ref, ref):
            slots = place_ref.shape[0]
            pick = (place_ref[:, :1] == iota((slots, lanes), 1)).astype(F32)
            return jnp.dot(
                ref[...], pick, preferred_element_type=F32, precision=lax.Precision.HIGHEST
            )

        t = packed(t_place_ref, t_ref)
        s = packed(s_place_ref, s_ref)
        gap = s - t
        t_top = jnp.max(t, axis=0, keepdims=True)
        t_lse = t_top + jnp.log(jnp.sum(jnp.exp(t - t_top), axis=0, keepdims=True))
        s_top = jnp.max(s, axis=0, keepdims=True)
        p = jnp.exp(s - s_top)
        total = jnp.sum(p, axis=0, keepdims=True)
        p = p / total
        mean = jnp.sum(p * gap, axis=0, keepdims=True)
        g_ref[:, :lanes] = (p * (gap - mean)).astype(BF16)
        g_ref[:, lanes:] = p.astype(BF16)
        table = in_parts([s_top + jnp.log(total), mean, t_lse], lanes)
        stat_ref[...] = jnp.concatenate([table, table], axis=1).astype(BF16)

    half = keep_ref.shape[1] - 16
    low = info_ref[1] == 0
    for k in range(keep_ref.shape[0]):
        part = jnp.dot(
            head_ref[2 * half * k : 2 * half * (k + 1), :],
            g_ref[...],
            preferred_element_type=F32,
        ).astype(BF16)
        keep_ref[k, :half] = jnp.where(low, part[:half], part[half:])
        send_ref[k, :half] = jnp.where(low, part[half:], part[:half])
        keep_ref[k, half:] = stat_ref[...]
        send_ref[k, half:] = stat_ref[...]


def partial(info, t, s, t_place, s_place, head, lanes, count):
    steps = 4
    half = head.shape[0] // count // 2
    part = jax.ShapeDtypeStruct((count, half + 16, 2 * lanes), BF16)
    block = pl.BlockSpec((count // steps, half + 16, 2 * lanes), lambda i: (i, 0, 0))
    whole = lambda a: pl.BlockSpec(a.shape, lambda i: (0,) * a.ndim)
    return pl.pallas_call(
        partial_kernel,
        grid=(steps,),
        out_shape=[part, part],
        in_specs=[
            SMEM,
            whole(t),
            whole(s),
            whole(t_place),
            whole(s_place),
            pl.BlockSpec((head.shape[0] // steps, head.shape[1]), lambda i: (i, 0)),
        ],
        out_specs=[block, block],
        scratch_shapes=[
            pltpu.VMEM((head.shape[1], 2 * lanes), BF16),
            pltpu.VMEM((16, 2 * lanes), BF16),
        ],
        compiler_params=PARAMS,
    )(info, t, s, t_place, s_place, head)


def pair_kernel(info_ref, keep_ref, came_ref, out_ref):
    lanes = out_ref.shape[2] // 2
    half = out_ref.shape[1] - 16
    low = info_ref[1] == 0
    kept = keep_ref[0, half:].astype(F32)
    come = came_ref[0, half:].astype(F32)
    first = jnp.where(low, kept, come)
    second = jnp.where(low, come, kept)
    scale, shift, stats = merged([from_parts(first, lanes), from_parts(second, lanes)])
    table = in_parts(stats, lanes)
    table = jnp.concatenate([table, table], axis=1).astype(BF16)
    own, other = (jnp.where(low, scale[0], scale[1]), jnp.where(low, scale[1], scale[0]))
    own_shift, other_shift = (
        own * jnp.where(low, shift[0], shift[1]),
        other * jnp.where(low, shift[1], shift[0]),
    )
    for k in range(out_ref.shape[0]):
        a = own * keep_ref[k, :half, :lanes].astype(F32)
        a += other * came_ref[k, :half, :lanes].astype(F32)
        b_own = keep_ref[k, :half, lanes:].astype(F32)
        b_other = came_ref[k, :half, lanes:].astype(F32)
        a += own_shift * b_own + other_shift * b_other
        out_ref[k, :half, :lanes] = a.astype(BF16)
        out_ref[k, :half, lanes:] = (own * b_own + other * b_other).astype(BF16)
        out_ref[k, half:] = table


def pair(info, keep, came):
    return pl.pallas_call(
        pair_kernel,
        out_shape=jax.ShapeDtypeStruct(keep.shape, BF16),
        in_specs=[SMEM, VMEM, VMEM],
        out_specs=VMEM,
        compiler_params=PARAMS,
    )(info, keep, came)


def spread_kernel(part_ref, place_ref, out_ref):
    lanes = part_ref.shape[2] // 2
    half = part_ref.shape[1] - 16
    count = part_ref.shape[0]
    groups, rows, width = out_ref.shape
    scale, shift, stats = merged(
        [from_parts(part_ref[k, half:].astype(F32), lanes) for k in range(count)]
    )
    a = jnp.zeros((half, lanes), F32)
    b = jnp.zeros((half, lanes), F32)
    for k in range(count):
        b_one = part_ref[k, :half, lanes:].astype(F32)
        a += scale[k] * part_ref[k, :half, :lanes].astype(F32) + (scale[k] * shift[k]) * b_one
        b += scale[k] * b_one
    rest = jnp.zeros((width - half - 16, lanes), F32)
    table = jnp.concatenate([in_parts(stats, lanes), rest], axis=0)
    slots = place_ref.shape[0]
    pick = (place_ref[:, :1] == iota((slots, lanes), 1)).astype(F32).astype(BF16)

    def found(value):
        value = jnp.concatenate([value, table], axis=0).astype(BF16)
        value = lax.dot_general(
            pick, value, (((1,), (1,)), ((), ())), preferred_element_type=F32
        )
        return value.reshape(groups, rows // 2, width)

    out_ref[...] = jnp.concatenate([found(a), found(b)], axis=1).astype(BF16)


def spread(parts, place, pad):
    groups = place.shape[0] // pad
    width = -(-parts.shape[1] // 128) * 128
    return pl.pallas_call(
        spread_kernel,
        out_shape=jax.ShapeDtypeStruct((groups, 2 * pad, width), BF16),
        in_specs=[VMEM, VMEM],
        out_specs=VMEM,
        compiler_params=PARAMS,
    )(parts, place)


def finish_kernel(info_ref, part_ref, grad_ref, kl_ref):
    _, pad, width = grad_ref.shape
    parts = [part_ref[k].astype(F32) for k in range(part_ref.shape[0])]
    stats = []
    for part in parts:
        column = [part[:pad, width + k : width + k + 1] for k in range(9)]
        stats.append([column[k] + column[k + 1] + column[k + 2] for k in (0, 3, 6)])
    scale, shift, (lse, mean, t_lse) = merged(stats)
    grad = jnp.zeros((pad, width), F32)
    for part, a, b in zip(parts, scale, shift):
        grad += a * (part[:pad, :width] + b * part[pad:, :width])
    grad_ref[0] = grad.astype(BF16)
    kl = jnp.where(iota((pad, 1), 0) < info_ref[3], mean - lse + t_lse, 0.0)
    square = iota((pad, pad), 0) == iota((pad, pad), 1)
    kl_ref[...] = jnp.sum(jnp.where(square, kl, 0.0), axis=0, keepdims=True)


def finish(info, parts, width):
    pad = parts.shape[1] // 2
    return pl.pallas_call(
        finish_kernel,
        out_shape=[
            jax.ShapeDtypeStruct((1, pad, width), BF16),
            jax.ShapeDtypeStruct((1, pad), F32),
        ],
        in_specs=[SMEM, VMEM],
        out_specs=[VMEM, VMEM],
    )(info, parts)


def tail(lanes, pad, operands):
    info, t, s, t_place, s_place, student_head = operands
    ring = lax.axis_size("y")
    keep, send = partial(info, t, s, t_place, s_place, student_head, lanes, ring)
    came = lax.ppermute(send, "c", ((0, 1), (1, 0)))
    both = pair(info, keep, came)
    return exchange(spread(exchange(both, "y"), s_place, pad), GRP)


def routing_kernel(
    groups, pad, group_ref, core_ref, lengths_ref, owner_ref, t_ref, s_ref, info_ref, start_ref
):
    share = lengths_ref.shape[0] // groups

    def total(g):
        return sum(lengths_ref[share * g + k] for k in range(share))

    def owned(j, found):
        g, count = found
        return lax.fori_loop(
            0,
            groups,
            lambda i, f: (
                jnp.where(owner_ref[share * i] == j, i, f[0]),
                jnp.where(owner_ref[share * i] == j, total(i), f[1]),
            ),
            (g, count),
        )

    slot = iota(t_ref.shape, 0)
    zero = jnp.int32(0)

    none = jnp.full(t_ref.shape, -1, jnp.int32)
    t_ref[...] = none
    s_ref[...] = none

    def place(j, start):
        g, count = owned(j, (zero, zero))
        for ref, first in ((t_ref, g * pad), (s_ref, j * pad)):
            step = slot - first
            ref[...] = jnp.where((step >= 0) & (step < count), start + step, ref[...])
        start_ref[j] = start
        start_ref[groups + j] = count
        return start + count

    live = lax.fori_loop(0, groups, place, zero)
    which = zero
    for c in CAPACITIES[:-1]:
        which += (live > c).astype(jnp.int32)
    info_ref[0] = which
    info_ref[1] = core_ref[0]
    info_ref[2] = start_ref[group_ref[0]]
    info_ref[3] = start_ref[groups + group_ref[0]]


def routing(group, core, lengths, owner, groups, pad):
    slots = groups * pad
    return pl.pallas_call(
        functools.partial(routing_kernel, groups, pad),
        out_shape=[
            jax.ShapeDtypeStruct((slots, 128), jnp.int32),
            jax.ShapeDtypeStruct((slots, 128), jnp.int32),
            jax.ShapeDtypeStruct((4,), jnp.int32),
        ],
        in_specs=[SMEM] * 4,
        out_specs=[VMEM] * 2 + [SMEM],
        scratch_shapes=[pltpu.SMEM((2 * groups,), jnp.int32)],
        cost_estimate=pl.CostEstimate(flops=10**8, bytes_accessed=10**6, transcendentals=0),
    )(group, core, lengths, owner)


def per_device(teacher_rows, student_rows, teacher_head, student_head, lengths, owner):
    groups = lax.axis_size(GRP)
    pad = student_rows.shape[1]
    group = lax.axis_index(GRP).astype(jnp.int32).reshape(1)
    core = lax.axis_index("c").astype(jnp.int32).reshape(1)
    mine = arrange(group, lengths, teacher_rows, student_rows, groups)
    rows = exchange(mine, GRP).reshape(groups * pad, mine.shape[2])
    rows = lax.all_gather(rows, VOCAB, axis=0, tiled=True)
    rows = rows.reshape(-1, groups * pad, mine.shape[2])
    t_place, s_place, info = routing(group, core, lengths, owner, groups, pad)
    t_head, s_head = stage(teacher_head, student_head)
    t, s = logits(rows, t_head, s_head, teacher_rows.shape[2])
    operands = (info, t, s, t_place, s_place, student_head)
    branches = [functools.partial(tail, c, pad) for c in CAPACITIES]
    parts = lax.switch(info[0], branches, operands)
    grad, divergence = finish(info, parts, student_rows.shape[2])
    return divergence, grad


def solution(mesh):
    torus = Mesh(mesh.devices.reshape(4, 8, 8, 2), ("x", "z", "y", "c"))
    return jax.shard_map(
        per_device,
        mesh=torus,
        in_specs=(
            P(GRP, None, VOCAB),
            P(GRP, None, VOCAB),
            P(None, (*GRP, *VOCAB)),
            P(None, (*GRP, *VOCAB)),
            P(),
            P(),
        ),
        out_specs=(P(GRP, None), P(GRP, None, VOCAB)),
        check_vma=False,
    )
```

time: 177 us -> 166 us (0.938)
  the two profiles are of different devices: /device:TPU:1 before, /device:TPU:64 now
where the time goes in v3:
time: 166 us; the launch traced here: 165 us
  blocking collectives  91 us (55%)
  Pallas kernels  28.7 us (17%)
  waiting for transfers between devices  26.2 us (16%)
  between operations  14.1 us (8%)
  local copies, waits for them, and re-layouts  3.05 us (2%)
  starting transfers between devices  2.19 us (1%)
    all_to_all x3, blocking collectives, exchange(): return lax.all_to_all(pieces, axes, 0, 0, tiled=True)  91 us
    all_gather x1, waiting for transfers between devices, per_device(): rows = lax.all_gather(rows, VOCAB, axis=0, tiled=True)  23.3 us
    pallas_call x1, Pallas kernels, routing(): pl.pallas_call(functools.partial(routing_kernel, groups, pad), out_shape=...  13.7 us
    pallas_call x1, Pallas kernels, logits(): pl.pallas_call(functools.partial(logits_step, teacher_width, steps), grid...  5.39 us
  transfers between devices with their start and end apart: 2, of which 2 were waited for; matrix products, arithmetic and copies ran while one was open for 0% of the time, Pallas kernels for 9%

profile of v3, /device:TPU:64, one launch (start us, length us, event | category | flops | bytes accessed | tf_op | source)
XLA Modules:
  0.0 165.3 jit_solution(13231042801315065445)
XLA Ops:
  7.2 0.0 all-gather.2.cloned.1.call-start
  7.2 1.5 shard_map.78
  8.7 26.3 %all_to_all.25 = bf16[32,8,640]{2,1,0:T(8,128)(2,1)} all-to-all(bf16[32,8,640]{2,1,0:T(8,128)(2,1)} %shard_map.78), channel_id=1, replica_groups=mesh['x'=4,'z'=8,'y'=8,'c'=2] {'x','z'}, dimensions={0} | all-to-all | bytes 655360 | tf_op jit(solution)/shard_map/all_to_all | solution.py:26
  35.0 0.0 all-gather.2.cloned.1.call-update
  35.0 0.0 copy-start.1
  35.0 1.6 copy-done.1
  36.6 1.9 %shard_map.79 = (bf16[4096,256]{1,0:T(8,128)(2,1)S(1)}, bf16[5120,256]{1,0:T(8,128)(2,1)S(1)}) custom-call(bf16[4096,256]{1,0:T(8,128)(2,1)S(1)} %copy-done.1, bf16[5120,256]{1,0:T(8,128)(2,1)} %student_ref.3), custom_call_target="tpu_custom_call" | custom-call | bytes 9437184 | tf_op jit(solution)/shard_map/pallas_call | solution.py:68
  38.5 0.0 copy-start
  38.5 1.5 copy-done
  40.0 13.7 %shard_map.77 = (s32[256,128]{1,0:T(8,128)S(1)}, s32[256,128]{1,0:T(8,128)S(1)}, s32[4]{0:T(128)S(1)}) custom-call(s32[1]{0:T(128)} %bitcast.group_ref, s32[1]{0:T(128)} %bitcast.1.core_ref, s32[64]{0:T(128)} %lengths_ref.3, s32[64]{0:T(128)} %owner_ref.1), custom_call_target="tpu_custom_call" | custom-call | flops 100000000 | bytes 1000000 | tf_op jit(solution)/shard_map/pallas_call | solution.py:408
  53.7 23.3 %all-gather.2.cloned.1.call-done = bf16[4096,640]{1,0:T(8,128)(2,1)} async-done(((bf16[256,640]{1,0:T(8,128)(2,1)}), bf16[4096,640]{1,0:T(8,128)(2,1)}) %all-gather.2.cloned.1.call-update) | async-done | bytes 5242896 | tf_op jit(solution)/shard_map/all_gather | solution.py:429
  77.0 0.0 copy-start.2
  77.0 5.4 %shard_map.80 = (f32[256,256]{1,0:T(8,128)S(1)}, f32[256,256]{1,0:T(8,128)S(1)}) custom-call(bf16[16,256,640]{2,1,0:T(8,128)(2,1)} %bitcast.6, bf16[4096,256]{1,0:T(8,128)(2,1)S(1)} %get-tuple-element.55.teacher_ref, bf16[5120,256]{1,0:T(8,128)(2,1)} %copy-done), custom_call_target="tpu_custom_call" | custom-call | tf_op jit(solution)/shard_map/pallas_call | solution.py:130
  82.4 0.0 copy-done.2
  82.4 74.5 %conditional.1 = (bf16[32,16,384]{2,1,0:T(8,128)(2,1)S(1)}) conditional(s32[]{:T(128)} %bitcast.2, (s32[4]{0:T(128)S(1)}, f32[256,256]{1,0:T(8,128)S(1)}, f32[256,256]{1,0:T(8,128)S(1)}, s32[256,128]{1,0:T(8,128)S(1)}, s32[256,128]{1,0:T(8,128)S(1)}, /*index=5*/bf16[5120,256]{1,0:T(8,128)(2,1)S(1)}) %tuple.20, (s32[4]{0:T(128)S(1)}, ...), branch_computations={%region_0.0_spmd, %region_1.0_spmd} | conditional | bytes 17301552 | solution.py:436
  82.4 2.7 %branch_0_fun.3 = (bf16[8,336,256]{2,1,0:T(8,128)(2,1)S(1)}, bf16[8,336,256]{2,1,0:T(8,128)(2,1)S(1)}) custom-call(s32[4]{0:T(128)S(1)} %get-tuple-element.17.info_ref, f32[256,256]{1,0:T(8,128)S(1)} %get-tuple-element.28.t_ref, f32[256,256]{1,0:T(8,128)S(1)} %get-tuple-element.29.s_ref, s32[256,128]{1,0:T(8,128)S(1)} %get-tuple-element.30.t_place_ref, ...), custom_call_target="tpu_custom_call" | custom-call | tf_op jit(solution)/shard_map/cond/branch_0_fun/pallas_call | solution.py:222
  85.2 2.1 %collective-permute-start = (bf16[8,336,256]{2,1,0:T(8,128)(2,1)S(1)}, bf16[8,336,256]{2,1,0:T(8,128)(2,1)S(1)}, u32[]{:S(2)}, u32[]{:S(2)}) collective-permute-start(bf16[8,336,256]{2,1,0:T(8,128)(2,1)S(1)} %get-tuple-element.34), channel_id=1, source_target_pairs={{0,1},{1,0},{2,3},{3,2},{4,5},{5,4},{6,7},{7,6},{8,9},{9,8},{10,11... | collective-permute-start | bytes 4128776 | tf_op jit(solution)/shard_map/cond/branch_0_fun/ppermute | solution.py:355
  87.3 2.9 %collective-permute-done.came_ref = bf16[8,336,256]{2,1,0:T(8,128)(2,1)S(1)} collective-permute-done((bf16[8,336,256]{2,1,0:T(8,128)(2,1)S(1)}, bf16[8,336,256]{2,1,0:T(8,128)(2,1)S(1)}, u32[]{:S(2)}, u32[]{:S(2)}) %collective-permute-start) | collective-permute-done | bytes 1376288 | tf_op jit(solution)/shard_map/cond/branch_0_fun/ppermute | solution.py:355
  90.2 1.3 branch_0_fun.4
  91.5 40.3 %all_to_all.21.part_ref = bf16[8,336,256]{2,1,0:T(8,128)(2,1)S(1)} all-to-all(bf16[8,336,256]{2,1,0:T(8,128)(2,1)S(1)} %branch_0_fun.4), channel_id=1, replica_groups=mesh['x'=4,'z'=8,'y'=8,'c'=2] {'y'}, dimensions={0} | all-to-all | bytes 2752512 | tf_op jit(solution)/shard_map/cond/branch_0_fun/all_to_all | solution.py:26
  131.9 0.6 branch_0_fun.5
  132.5 24.4 %all_to_all.22 = bf16[32,16,384]{2,1,0:T(8,128)(2,1)S(1)} all-to-all(bf16[32,16,384]{2,1,0:T(8,128)(2,1)S(1)} %branch_0_fun.5), channel_id=1, replica_groups=mesh['x'=4,'z'=8,'y'=8,'c'=2] {'x','z'}, dimensions={0} | all-to-all | bytes 786432 | tf_op jit(solution)/shard_map/cond/branch_0_fun/all_to_all | solution.py:26
  156.9 1.5 shard_map.81
Async XLA Ops:
  7.2 69.8 %all-gather.2.cloned.1.call-start = ((), (), s32[]{:S(2)}) async-start(), calls=%async_computation.5 | async-start | bytes 5570560 | tf_op jit(solution)/shard_map/all_gather | solution.py:429
  35.0 1.6 copy-start.1
  38.5 1.5 copy-start
  77.0 5.4 %copy-start.2 = (bf16[5120,256]{1,0:T(8,128)(2,1)S(1)}, bf16[5120,256]{1,0:T(8,128)(2,1)}, u32[]{:S(2)}) copy-start(bf16[5120,256]{1,0:T(8,128)(2,1)} %student_ref.3) | copy-start | bytes 7864324
  85.2 5.0 %collective-permute-start = (bf16[8,336,256]{2,1,0:T(8,128)(2,1)S(1)}, bf16[8,336,256]{2,1,0:T(8,128)(2,1)S(1)}, u32[]{:S(2)}, u32[]{:S(2)}) collective-permute-start(bf16[8,336,256]{2,1,0:T(8,128)(2,1)S(1)} %get-tuple-element.34), channel_id=1, source_target_pairs={{0,1},{1,0},{2,3},{3,2},{4,5},{5,4},{6,7},{7,6},{8,9},{9,8},{10,11... | collective-permute-start | bytes 4128776 | tf_op jit(solution)/shard_map/cond/branch_0_fun/ppermute | solution.py:355
Sparse Core Ops, SparseCore 0:
  35.1 41.8 all-gather.1

commit v4 on v3

--- a/solution.py
+++ b/solution.py
@@ -26,11 +26,16 @@
     return lax.all_to_all(pieces, axes, 0, 0, tiled=True)
 
 
-def arrange_kernel(group_ref, lengths_ref, teacher_ref, student_ref, out_ref):
+def arrange_kernel(
+    place_ref, lengths_ref, owner_ref, meta_ref, teacher_ref, student_ref,
+    out_ref, t_place_ref, s_place_ref, info_ref,
+):
     count, pad, _ = out_ref.shape
     width = teacher_ref.shape[2]
     rest = out_ref.shape[2] - width - student_ref.shape[2]
-    first = lengths_ref[2 * group_ref[0]]
+    group = place_ref[0]
+    share = lengths_ref.shape[0] // count
+    first = lengths_ref[share * group]
     upper = teacher_ref[0].astype(F32)
     lower = pltpu.roll(teacher_ref[1].astype(F32), first, 0)
     chosen = jnp.where(iota(upper.shape, 0) < first, upper, lower).astype(BF16)
@@ -40,16 +45,92 @@
         if rest:
             out_ref[k, :, -rest:] = jnp.zeros((pad, rest), BF16)
 
-
-def arrange(group, lengths, teacher_rows, student_rows, count):
+    live = jnp.int32(0)
+    mine = jnp.int32(0)
+    for k in range(lengths_ref.shape[0]):
+        live += lengths_ref[k]
+        mine += jnp.where(owner_ref[k] == group, lengths_ref[k], 0)
+    which = jnp.int32(0)
+    for c in CAPACITIES[:-1]:
+        which += (live > c).astype(jnp.int32)
+    info_ref[0] = which
+    info_ref[1] = place_ref[1]
+    info_ref[2] = mine
+
+    slots = t_place_ref.shape[1]
+    deep = meta_ref.shape[1]
+
+    def column(k):
+        one = jnp.broadcast_to(meta_ref[k : k + 1, :], (128, deep)).T
+        return jnp.concatenate([one] * (slots // 128), axis=1)
+
+    length, owner = column(0), column(1)
+    seq = iota((deep, slots), 0)
+    home = (iota((deep, slots), 1) // pad)
+    zero = jnp.zeros((deep, slots), F32)
+
+    def total(mask, value):
+        return jnp.sum(jnp.where(mask, value, zero), axis=0, keepdims=True)
+
+    home_f = home.astype(F32)
+    step = (iota((1, slots), 1) % pad).astype(F32)
+    t_count = total(seq // share == home, length)
+    t_owner = total(seq == share * home, owner)
+    t_start = total(owner < t_owner, length)
+    s_count = total(owner == home_f, length)
+    s_start = total(owner < home_f, length)
+    t_place = jnp.where(step < t_count, t_start + step, -1.0)
+    s_place = jnp.where(step < s_count, s_start + step, -1.0)
+    t_place_ref[...] = t_place.astype(jnp.int32)
+    s_place_ref[...] = s_place.astype(jnp.int32)
+
+
+def arrange(place, lengths, owner, teacher_rows, student_rows, count):
     pad = student_rows.shape[1]
     width = -(-(teacher_rows.shape[2] + student_rows.shape[2]) // 128) * 128
+    deep = -(-lengths.shape[0] // 128) * 128
+    meta = jnp.stack([lengths, owner]).astype(F32)
+    meta = jnp.pad(meta, ((0, 0), (0, deep - lengths.shape[0])))
     return pl.pallas_call(
         arrange_kernel,
-        out_shape=jax.ShapeDtypeStruct((count, pad, width), BF16),
-        in_specs=[SMEM, SMEM, VMEM, VMEM],
+        out_shape=[
+            jax.ShapeDtypeStruct((count, pad, width), BF16),
+            jax.ShapeDtypeStruct((1, count * pad), jnp.int32),
+            jax.ShapeDtypeStruct((1, count * pad), jnp.int32),
+            jax.ShapeDtypeStruct((3,), jnp.int32),
+        ],
+        in_specs=[SMEM, SMEM, SMEM, VMEM, VMEM, VMEM],
+        out_specs=[VMEM, VMEM, VMEM, SMEM],
+    )(place, lengths, owner, meta, teacher_rows, student_rows)
+
+
+def pack_kernel(rows_ref, t_place_ref, s_place_ref, out_ref):
+    count, half, _ = out_ref.shape
+    slots = rows_ref.shape[0]
+    width = out_ref.shape[2] // 2
+
+    def packed(place_ref, first, stop):
+        pick = (place_ref[...] == iota((2 * half, slots), 0)).astype(F32).astype(BF16)
+        found = jnp.dot(pick, rows_ref[:, first:stop], preferred_element_type=F32)
+        return found[:half], found[half:]
+
+    t = packed(t_place_ref, 0, 256)
+    s = packed(s_place_ref, 256, width)
+    value = jnp.concatenate(
+        [*t, s[0][:, :256], s[1][:, :256], s[0][:, 256:], s[1][:, 256:]], axis=1
+    ).astype(BF16)
+    for k in range(count):
+        out_ref[k] = value
+
+
+def pack(rows, t_place, s_place, lanes, width, count):
+    return pl.pallas_call(
+        pack_kernel,
+        out_shape=jax.ShapeDtypeStruct((count, lanes // 2, 2 * width), BF16),
+        in_specs=[VMEM] * 3,
         out_specs=VMEM,
-    )(group, lengths, teacher_rows, student_rows)
+        compiler_params=PARAMS,
+    )(rows, t_place, s_place)
 
 
 def stage_kernel(teacher_ref, student_ref, t_out_ref, s_out_ref, sems):
@@ -170,37 +251,24 @@
     return scale, shift, [high + jnp.log(total), middle, t_high + jnp.log(t_total)]
 
 
-def partial_kernel(
-    info_ref, t_ref, s_ref, t_place_ref, s_place_ref, head_ref, keep_ref, send_ref, g_ref, stat_ref
-):
+def soften(t, s, g_ref, stat_ref):
     lanes = g_ref.shape[1] // 2
-
-    @pl.when(pl.program_id(0) == 0)
-    def _():
-        def packed(place_ref, ref):
-            slots = place_ref.shape[0]
-            pick = (place_ref[:, :1] == iota((slots, lanes), 1)).astype(F32)
-            return jnp.dot(
-                ref[...], pick, preferred_element_type=F32, precision=lax.Precision.HIGHEST
-            )
-
-        t = packed(t_place_ref, t_ref)
-        s = packed(s_place_ref, s_ref)
-        gap = s - t
-        t_top = jnp.max(t, axis=0, keepdims=True)
-        t_lse = t_top + jnp.log(jnp.sum(jnp.exp(t - t_top), axis=0, keepdims=True))
-        s_top = jnp.max(s, axis=0, keepdims=True)
-        p = jnp.exp(s - s_top)
-        total = jnp.sum(p, axis=0, keepdims=True)
-        p = p / total
-        mean = jnp.sum(p * gap, axis=0, keepdims=True)
-        g_ref[:, :lanes] = (p * (gap - mean)).astype(BF16)
-        g_ref[:, lanes:] = p.astype(BF16)
-        table = in_parts([s_top + jnp.log(total), mean, t_lse], lanes)
-        stat_ref[...] = jnp.concatenate([table, table], axis=1).astype(BF16)
-
+    gap = s - t
+    t_top = jnp.max(t, axis=0, keepdims=True)
+    t_lse = t_top + jnp.log(jnp.sum(jnp.exp(t - t_top), axis=0, keepdims=True))
+    s_top = jnp.max(s, axis=0, keepdims=True)
+    p = jnp.exp(s - s_top)
+    total = jnp.sum(p, axis=0, keepdims=True)
+    p = p / total
+    mean = jnp.sum(p * gap, axis=0, keepdims=True)
+    g_ref[:, :lanes] = (p * (gap - mean)).astype(BF16)
+    g_ref[:, lanes:] = p.astype(BF16)
+    table = in_parts([s_top + jnp.log(total), mean, t_lse], lanes)
+    stat_ref[...] = jnp.concatenate([table, table], axis=1).astype(BF16)
+
+
+def backward(low, head_ref, g_ref, stat_ref, keep_ref, send_ref):
     half = keep_ref.shape[1] - 16
-    low = info_ref[1] == 0
     for k in range(keep_ref.shape[0]):
         part = jnp.dot(
             head_ref[2 * half * k : 2 * half * (k + 1), :],
@@ -213,22 +281,132 @@
         send_ref[k, half:] = stat_ref[...]
 
 
+def partial_kernel(
+    info_ref, t_ref, s_ref, t_place_ref, s_place_ref, head_ref, keep_ref, send_ref, g_ref, stat_ref
+):
+    lanes = g_ref.shape[1] // 2
+
+    @pl.when(pl.program_id(0) == 0)
+    def _():
+        def packed(place_ref, ref):
+            slots = place_ref.shape[1]
+            pick = (place_ref[...] == iota((lanes, slots), 0)).astype(F32).T
+            return jnp.dot(
+                ref[...], pick, preferred_element_type=F32, precision=lax.Precision.HIGHEST
+            )
+
+        soften(packed(t_place_ref, t_ref), packed(s_place_ref, s_ref), g_ref, stat_ref)
+
+    backward(info_ref[1] == 0, head_ref, g_ref, stat_ref, keep_ref, send_ref)
+
+
+def whole_kernel(
+    steps, info_ref, own_ref, other_ref, t_head_ref, s_head_ref, keep_ref, send_ref,
+    t_ref, s_ref, g_ref, stat_ref,
+):
+    step = pl.program_id(0)
+    low = info_ref[1] == 0
+
+    @pl.when(step == 0)
+    def _():
+        t_ref[...] = jnp.zeros_like(t_ref)
+        s_ref[...] = jnp.zeros_like(s_ref)
+
+    @pl.when(step < steps)
+    def _():
+        pieces = []
+        for k in range(own_ref.shape[0]):
+            pieces.append(jnp.where(low, own_ref[k], other_ref[k]))
+            pieces.append(jnp.where(low, other_ref[k], own_ref[k]))
+        t_size = t_head_ref.shape[0] // len(pieces)
+        s_size = s_head_ref.shape[0] // len(pieces)
+        main = s_size // 128 * 128
+        tail_size = s_size - main
+
+        def rows(x, first, size):
+            return jnp.concatenate([x[:, first : first + size], x[:, first + size : first + 2 * size]], axis=0)
+
+        t_ref[...] += jnp.dot(
+            jnp.concatenate([rows(x, 0, t_size) for x in pieces], axis=1),
+            t_head_ref[...],
+            preferred_element_type=F32,
+        )
+        first = 2 * t_size
+        last = first + 2 * main
+        count = len(pieces)
+        s_ref[...] += jnp.dot(
+            jnp.concatenate(
+                [rows(x, first, main) for x in pieces] + [rows(x, last, tail_size) for x in pieces],
+                axis=1,
+            ),
+            jnp.concatenate(
+                [s_head_ref[k * s_size : k * s_size + main, :] for k in range(count)]
+                + [s_head_ref[k * s_size + main : (k + 1) * s_size, :] for k in range(count)],
+                axis=0,
+            ),
+            preferred_element_type=F32,
+        )
+
+    @pl.when(step == steps)
+    def _():
+        soften(t_ref[...].T, s_ref[...].T, g_ref, stat_ref)
+
+    @pl.when(step >= steps)
+    def _():
+        backward(low, s_head_ref, g_ref, stat_ref, keep_ref, send_ref)
+
+
+def whole(info, own, other, t_head, s_head):
+    steps = 4
+    count, half_rows, width = own.shape
+    lanes = 2 * half_rows
+    vocab = s_head.shape[1]
+    half = s_head.shape[0] // count // 2
+    part = jax.ShapeDtypeStruct((count, half + 16, 2 * lanes), BF16)
+    block = pl.BlockSpec(
+        (count // steps, half + 16, 2 * lanes), lambda i: (jnp.maximum(i - steps, 0), 0, 0)
+    )
+    rows = pl.BlockSpec(
+        (count // steps, half_rows, width), lambda i: (jnp.minimum(i, steps - 1), 0, 0)
+    )
+    return pl.pallas_call(
+        functools.partial(whole_kernel, steps),
+        grid=(2 * steps,),
+        out_shape=[part, part],
+        in_specs=[
+            SMEM,
+            rows,
+            rows,
+            pl.BlockSpec((t_head.shape[0] // steps, vocab), lambda i: (jnp.minimum(i, steps - 1), 0)),
+            pl.BlockSpec((s_head.shape[0] // steps, vocab), lambda i: (lax.rem(i, steps), 0)),
+        ],
+        out_specs=[block, block],
+        scratch_shapes=[
+            pltpu.VMEM((lanes, vocab), F32),
+            pltpu.VMEM((lanes, vocab), F32),
+            pltpu.VMEM((vocab, 2 * lanes), BF16),
+            pltpu.VMEM((16, 2 * lanes), BF16),
+        ],
+        compiler_params=PARAMS,
+    )(info, own, other, t_head, s_head)
+
+
 def partial(info, t, s, t_place, s_place, head, lanes, count):
     steps = 4
     half = head.shape[0] // count // 2
     part = jax.ShapeDtypeStruct((count, half + 16, 2 * lanes), BF16)
     block = pl.BlockSpec((count // steps, half + 16, 2 * lanes), lambda i: (i, 0, 0))
-    whole = lambda a: pl.BlockSpec(a.shape, lambda i: (0,) * a.ndim)
+    full = lambda a: pl.BlockSpec(a.shape, lambda i: (0,) * a.ndim)
     return pl.pallas_call(
         partial_kernel,
         grid=(steps,),
         out_shape=[part, part],
         in_specs=[
             SMEM,
-            whole(t),
-            whole(s),
-            whole(t_place),
-            whole(s_place),
+            full(t),
+            full(s),
+            full(t_place),
+            full(s_place),
             pl.BlockSpec((head.shape[0] // steps, head.shape[1]), lambda i: (i, 0)),
         ],
         out_specs=[block, block],
@@ -293,8 +471,8 @@
         b += scale[k] * b_one
     rest = jnp.zeros((width - half - 16, lanes), F32)
     table = jnp.concatenate([in_parts(stats, lanes), rest], axis=0)
-    slots = place_ref.shape[0]
-    pick = (place_ref[:, :1] == iota((slots, lanes), 1)).astype(F32).astype(BF16)
+    slots = place_ref.shape[1]
+    pick = (place_ref[...] == iota((lanes, slots), 0)).astype(F32).T.astype(BF16)
 
     def found(value):
         value = jnp.concatenate([value, table], axis=0).astype(BF16)
@@ -307,7 +485,7 @@
 
 
 def spread(parts, place, pad):
-    groups = place.shape[0] // pad
+    groups = place.shape[1] // pad
     width = -(-parts.shape[1] // 128) * 128
     return pl.pallas_call(
         spread_kernel,
@@ -330,7 +508,7 @@
     for part, a, b in zip(parts, scale, shift):
         grad += a * (part[:pad, :width] + b * part[pad:, :width])
     grad_ref[0] = grad.astype(BF16)
-    kl = jnp.where(iota((pad, 1), 0) < info_ref[3], mean - lse + t_lse, 0.0)
+    kl = jnp.where(iota((pad, 1), 0) < info_ref[2], mean - lse + t_lse, 0.0)
     square = iota((pad, pad), 0) == iota((pad, pad), 1)
     kl_ref[...] = jnp.sum(jnp.where(square, kl, 0.0), axis=0, keepdims=True)
 
@@ -348,93 +526,49 @@
     )(info, parts)
 
 
-def tail(lanes, pad, operands):
-    info, t, s, t_place, s_place, student_head = operands
+def swap(value):
+    return lax.ppermute(value, "c", ((0, 1), (1, 0)))
+
+
+def reduce(info, keep, send, s_place, pad):
+    both = pair(info, keep, swap(send))
+    return exchange(spread(exchange(both, "y"), s_place, pad), GRP)
+
+
+def some_rows(lanes, pad, width, operands):
+    info, rows, t_place, s_place, teacher_head, student_head = operands
     ring = lax.axis_size("y")
+    own = exchange(pack(rows, t_place, s_place, lanes, width, ring), "y")
+    keep, send = whole(info, own, swap(own), teacher_head, student_head)
+    return reduce(info, keep, send, s_place, pad)
+
+
+def all_rows(lanes, pad, t_width, operands):
+    info, rows, t_place, s_place, teacher_head, student_head = operands
+    ring = lax.axis_size("y")
+    full = lax.all_gather(rows, VOCAB, axis=0, tiled=True).reshape(-1, *rows.shape)
+    t_head, s_head = stage(teacher_head, student_head)
+    t, s = logits(full, t_head, s_head, t_width)
     keep, send = partial(info, t, s, t_place, s_place, student_head, lanes, ring)
-    came = lax.ppermute(send, "c", ((0, 1), (1, 0)))
-    both = pair(info, keep, came)
-    return exchange(spread(exchange(both, "y"), s_place, pad), GRP)
-
-
-def routing_kernel(
-    groups, pad, group_ref, core_ref, lengths_ref, owner_ref, t_ref, s_ref, info_ref, start_ref
-):
-    share = lengths_ref.shape[0] // groups
-
-    def total(g):
-        return sum(lengths_ref[share * g + k] for k in range(share))
-
-    def owned(j, found):
-        g, count = found
-        return lax.fori_loop(
-            0,
-            groups,
-            lambda i, f: (
-                jnp.where(owner_ref[share * i] == j, i, f[0]),
-                jnp.where(owner_ref[share * i] == j, total(i), f[1]),
-            ),
-            (g, count),
-        )
-
-    slot = iota(t_ref.shape, 0)
-    zero = jnp.int32(0)
-
-    none = jnp.full(t_ref.shape, -1, jnp.int32)
-    t_ref[...] = none
-    s_ref[...] = none
-
-    def place(j, start):
-        g, count = owned(j, (zero, zero))
-        for ref, first in ((t_ref, g * pad), (s_ref, j * pad)):
-            step = slot - first
-            ref[...] = jnp.where((step >= 0) & (step < count), start + step, ref[...])
-        start_ref[j] = start
-        start_ref[groups + j] = count
-        return start + count
-
-    live = lax.fori_loop(0, groups, place, zero)
-    which = zero
-    for c in CAPACITIES[:-1]:
-        which += (live > c).astype(jnp.int32)
-    info_ref[0] = which
-    info_ref[1] = core_ref[0]
-    info_ref[2] = start_ref[group_ref[0]]
-    info_ref[3] = start_ref[groups + group_ref[0]]
-
-
-def routing(group, core, lengths, owner, groups, pad):
-    slots = groups * pad
-    return pl.pallas_call(
-        functools.partial(routing_kernel, groups, pad),
-        out_shape=[
-            jax.ShapeDtypeStruct((slots, 128), jnp.int32),
-            jax.ShapeDtypeStruct((slots, 128), jnp.int32),
-            jax.ShapeDtypeStruct((4,), jnp.int32),
-        ],
-        in_specs=[SMEM] * 4,
-        out_specs=[VMEM] * 2 + [SMEM],
-        scratch_shapes=[pltpu.SMEM((2 * groups,), jnp.int32)],
-        cost_estimate=pl.CostEstimate(flops=10**8, bytes_accessed=10**6, transcendentals=0),
-    )(group, core, lengths, owner)
+    return reduce(info, keep, send, s_place, pad)
 
 
 def per_device(teacher_rows, student_rows, teacher_head, student_head, lengths, owner):
     groups = lax.axis_size(GRP)
     pad = student_rows.shape[1]
-    group = lax.axis_index(GRP).astype(jnp.int32).reshape(1)
-    core = lax.axis_index("c").astype(jnp.int32).reshape(1)
-    mine = arrange(group, lengths, teacher_rows, student_rows, groups)
+    t_width, s_width = teacher_rows.shape[2], student_rows.shape[2]
+    place = jnp.stack([lax.axis_index(GRP), lax.axis_index("c")]).astype(jnp.int32)
+    mine, t_place, s_place, info = arrange(
+        place, lengths, owner, teacher_rows, student_rows, groups
+    )
     rows = exchange(mine, GRP).reshape(groups * pad, mine.shape[2])
-    rows = lax.all_gather(rows, VOCAB, axis=0, tiled=True)
-    rows = rows.reshape(-1, groups * pad, mine.shape[2])
-    t_place, s_place, info = routing(group, core, lengths, owner, groups, pad)
-    t_head, s_head = stage(teacher_head, student_head)
-    t, s = logits(rows, t_head, s_head, teacher_rows.shape[2])
-    operands = (info, t, s, t_place, s_place, student_head)
-    branches = [functools.partial(tail, c, pad) for c in CAPACITIES]
-    parts = lax.switch(info[0], branches, operands)
-    grad, divergence = finish(info, parts, student_rows.shape[2])
+    operands = (info, rows, t_place, s_place, teacher_head, student_head)
+    few, every = CAPACITIES
+    branches = [
+        functools.partial(some_rows, few, pad, t_width + s_width),
+        functools.partial(all_rows, every, pad, t_width),
+    ]
+    grad, divergence = finish(info, lax.switch(info[0], branches, operands), s_width)
     return divergence, grad
 
 

time: 166 us -> 159 us (0.958)
  the two profiles are of different devices: /device:TPU:64 before, /device:TPU:1 now
where the time goes in v4:
time: 159 us; the launch traced here: 156 us
  blocking collectives  90.4 us (57%)
  starting transfers between devices  24.1 us (15%)
  waiting for transfers between devices  15.3 us (10%)
  between operations  14.1 us (9%)
  Pallas kernels  10.6 us (7%)
    all_to_all x3, blocking collectives, exchange(): return lax.all_to_all(pieces, axes, 0, 0, tiled=True)  90.4 us
    all_to_all x1, starting transfers between devices, exchange(): return lax.all_to_all(pieces, axes, 0, 0, tiled=True)  13.7 us
    ppermute x2, starting transfers between devices, swap(): return lax.ppermute(value, 'c', ((0, 1), (1, 0)))  10.4 us
    all_to_all x1, waiting for transfers between devices, exchange(): return lax.all_to_all(pieces, axes, 0, 0, tiled=True)  10.1 us
    ppermute x2, waiting for transfers between devices, swap(): return lax.ppermute(value, 'c', ((0, 1), (1, 0)))  5.19 us
    pallas_call x1, Pallas kernels, whole(): pl.pallas_call(functools.partial(whole_kernel, steps), grid=(2 * steps,),...  5.01 us
  transfers between devices with their start and end apart: 3, of which 3 were waited for; matrix products, arithmetic and copies ran while one was open for 0% of the time, Pallas kernels for 0%

profile of v4, /device:TPU:1, one launch (start us, length us, event | category | flops | bytes accessed | tf_op | source)
XLA Modules:
  0.0 156.5 jit_solution(12195542690719160628)
XLA Ops:
  7.2 0.6 pad_add_fusion.place_ref
  7.8 0.7 add_convert_fusion
  8.5 0.6 pad.4.meta_ref
  9.1 1.7 %shard_map.77 = (bf16[32,8,640]{2,1,0:T(8,128)(2,1)}, s32[1,256]{1,0:T(1,128)S(1)}, s32[1,256]{1,0:T(1,128)S(1)}, s32[3]{0:T(128)S(1)}) custom-call(s32[2]{0:T(128)} %pad_add_fusion.place_ref, s32[64]{0:T(128)} %lengths_ref.1, s32[64]{0:T(128)} %owner_ref.1, f32[2,128]{1,0:T(2,128)} %pad.4.meta_ref, bf16[2,8,256]{2,1,0:T(8,128)(2,1)} %teacher_ref.1, ...), custom_call_target="tpu_custom_call" | custom-call | tf_op jit(solution)/shard_map/pallas_call | solution.py:94
  10.8 13.7 %all-to-all-start.5 = ((bf16[32,8,640]{2,1,0:T(8,128)(2,1)}), bf16[32,8,640]{2,1,0:T(8,128)(2,1)S(1)}, u32[]{:S(2)}, u32[]{:S(2)}) async-start(bf16[32,8,640]{2,1,0:T(8,128)(2,1)} %get-tuple-element.56), calls=%async_computation.5 | async-start | bytes 655360 | tf_op jit(solution)/shard_map/all_to_all | solution.py:26
  24.5 10.1 %all-to-all-done.5 = bf16[32,8,640]{2,1,0:T(8,128)(2,1)S(1)} async-done(((bf16[32,8,640]{2,1,0:T(8,128)(2,1)}), bf16[32,8,640]{2,1,0:T(8,128)(2,1)S(1)}, u32[]{:S(2)}, u32[]{:S(2)}) %all-to-all-start.5) | async-done | bytes 327712 | tf_op jit(solution)/shard_map/all_to_all | solution.py:26
  34.7 113.4 %conditional.1 = (bf16[32,16,384]{2,1,0:T(8,128)(2,1)S(1)}) conditional(s32[]{:T(128)} %bitcast.5, (bf16[256,640]{1,0:T(8,128)(2,1)S(1)}, s32[1,256]{1,0:T(1,128)S(1)}, s32[1,256]{1,0:T(1,128)S(1)}, s32[3]{0:T(128)S(1)}, bf16[4096,256]{1,0:T(8,128)(2,1)}, /*index=5*/bf16[5120,256]{1,0:T(8,128)(2,1)}) %tuple.21, (bf16[256,640]{1,0:T(8,128)(2,1)S(1)}, ...), branch_computations={%region_0.1_spmd, %region_1.2_spmd} | conditional | bytes 65732780 | solution.py:571
  34.7 0.0 copy-start.1
  34.7 0.3 branch_0_fun.4
  35.0 33.0 %all_to_all.25.own_ref = bf16[8,64,1152]{2,1,0:T(8,128)(2,1)S(1)} all-to-all(bf16[8,64,1152]{2,1,0:T(8,128)(2,1)S(1)} %branch_0_fun.4), channel_id=1, replica_groups=mesh['x'=4,'z'=8,'y'=8,'c'=2] {'y'}, dimensions={0} | all-to-all | bytes 2359296 | tf_op jit(solution)/shard_map/cond/branch_0_fun/all_to_all | solution.py:26
  68.0 8.1 %collective-permute-start = (bf16[8,64,1152]{2,1,0:T(8,128)(2,1)S(1)}, bf16[8,64,1152]{2,1,0:T(8,128)(2,1)S(1)}, u32[]{:S(2)}, u32[]{:S(2)}) collective-permute-start(bf16[8,64,1152]{2,1,0:T(8,128)(2,1)S(1)} %all_to_all.25.own_ref), channel_id=1, source_target_pairs={{0,1},{1,0},{2,3},{3,2},{4,5},{5,4},{6,7},{7,6},{8,9},{9,8},{10,11... | collective-permute-start | bytes 3538952 | tf_op jit(solution)/shard_map/cond/branch_0_fun/ppermute | solution.py:530
  76.2 2.5 %collective-permute-done.other_ref = bf16[8,64,1152]{2,1,0:T(8,128)(2,1)S(1)} collective-permute-done((bf16[8,64,1152]{2,1,0:T(8,128)(2,1)S(1)}, bf16[8,64,1152]{2,1,0:T(8,128)(2,1)S(1)}, u32[]{:S(2)}, u32[]{:S(2)}) %collective-permute-start) | collective-permute-done | bytes 1179680 | tf_op jit(solution)/shard_map/cond/branch_0_fun/ppermute | solution.py:530
  78.6 0.0 copy-done.1
  78.6 5.0 %branch_0_fun.5 = (bf16[8,336,256]{2,1,0:T(8,128)(2,1)S(1)}, bf16[8,336,256]{2,1,0:T(8,128)(2,1)S(1)}) custom-call(s32[3]{0:T(128)S(1)} %get-tuple-element.17.info_ref, bf16[8,64,1152]{2,1,0:T(8,128)(2,1)S(1)} %all_to_all.25.own_ref, bf16[8,64,1152]{2,1,0:T(8,128)(2,1)S(1)} %collective-permute-done.other_ref, ...), custom_call_target="tpu_custom_call" | custom-call | tf_op jit(solution)/shard_map/cond/branch_0_fun/pallas_call | solution.py:372
  83.6 2.3 %collective-permute-start.1 = (bf16[8,336,256]{2,1,0:T(8,128)(2,1)S(1)}, bf16[8,336,256]{2,1,0:T(8,128)(2,1)S(1)}, u32[]{:S(2)}, u32[]{:S(2)}) collective-permute-start(bf16[8,336,256]{2,1,0:T(8,128)(2,1)S(1)} %get-tuple-element.34), channel_id=1, source_target_pairs={{0,1},{1,0},{2,3},{3,2},{4,5},{5,4},{6,7},{7,6},{8,9},{9,8},{10,11... | collective-permute-start | bytes 4128776 | tf_op jit(solution)/shard_map/cond/branch_0_fun/ppermute | solution.py:530
  85.9 2.7 %collective-permute-done.1.came_ref = bf16[8,336,256]{2,1,0:T(8,128)(2,1)S(1)} collective-permute-done((bf16[8,336,256]{2,1,0:T(8,128)(2,1)S(1)}, bf16[8,336,256]{2,1,0:T(8,128)(2,1)S(1)}, u32[]{:S(2)}, u32[]{:S(2)}) %collective-permute-start.1) | collective-permute-done | bytes 1376288 | tf_op jit(solution)/shard_map/cond/branch_0_fun/ppermute | solution.py:530
  88.7 1.3 branch_0_fun.6
  90.0 38.6 %all_to_all.26.part_ref = bf16[8,336,256]{2,1,0:T(8,128)(2,1)S(1)} all-to-all(bf16[8,336,256]{2,1,0:T(8,128)(2,1)S(1)} %branch_0_fun.6), channel_id=1, replica_groups=mesh['x'=4,'z'=8,'y'=8,'c'=2] {'y'}, dimensions={0} | all-to-all | bytes 2752512 | tf_op jit(solution)/shard_map/cond/branch_0_fun/all_to_all | solution.py:26
  128.6 0.6 branch_0_fun.7
  129.3 18.8 %all_to_all.27 = bf16[32,16,384]{2,1,0:T(8,128)(2,1)S(1)} all-to-all(bf16[32,16,384]{2,1,0:T(8,128)(2,1)S(1)} %branch_0_fun.7), channel_id=1, replica_groups=mesh['x'=4,'z'=8,'y'=8,'c'=2] {'x','z'}, dimensions={0} | all-to-all | bytes 786432 | tf_op jit(solution)/shard_map/cond/branch_0_fun/all_to_all | solution.py:26
  148.1 1.5 shard_map.78
Async XLA Ops:
  10.8 23.9 %all-to-all-start.5 = ((bf16[32,8,640]{2,1,0:T(8,128)(2,1)}), bf16[32,8,640]{2,1,0:T(8,128)(2,1)S(1)}, u32[]{:S(2)}, u32[]{:S(2)}) async-start(bf16[32,8,640]{2,1,0:T(8,128)(2,1)} %get-tuple-element.56), calls=%async_computation.5 | async-start | bytes 655360 | tf_op jit(solution)/shard_map/all_to_all | solution.py:26
  34.7 43.9 %copy-start.1 = (bf16[5120,256]{1,0:T(8,128)(2,1)S(1)}, bf16[5120,256]{1,0:T(8,128)(2,1)}, u32[]{:S(2)}) copy-start(bf16[5120,256]{1,0:T(8,128)(2,1)} %get-tuple-element.32.s_head_ref) | copy-start | bytes 7864324 | tf_op jit(solution)/shard_map/cond
  68.0 10.6 %collective-permute-start = (bf16[8,64,1152]{2,1,0:T(8,128)(2,1)S(1)}, bf16[8,64,1152]{2,1,0:T(8,128)(2,1)S(1)}, u32[]{:S(2)}, u32[]{:S(2)}) collective-permute-start(bf16[8,64,1152]{2,1,0:T(8,128)(2,1)S(1)} %all_to_all.25.own_ref), channel_id=1, source_target_pairs={{0,1},{1,0},{2,3},{3,2},{4,5},{5,4},{6,7},{7,6},{8,9},{9,8},{10,11... | collective-permute-start | bytes 3538952 | tf_op jit(solution)/shard_map/cond/branch_0_fun/ppermute | solution.py:530
  83.6 5.0 %collective-permute-start.1 = (bf16[8,336,256]{2,1,0:T(8,128)(2,1)S(1)}, bf16[8,336,256]{2,1,0:T(8,128)(2,1)S(1)}, u32[]{:S(2)}, u32[]{:S(2)}) collective-permute-start(bf16[8,336,256]{2,1,0:T(8,128)(2,1)S(1)} %get-tuple-element.34), channel_id=1, source_target_pairs={{0,1},{1,0},{2,3},{3,2},{4,5},{5,4},{6,7},{7,6},{8,9},{9,8},{10,11... | collective-permute-start | bytes 4128776 | tf_op jit(solution)/shard_map/cond/branch_0_fun/ppermute | solution.py:530

commit v5 on v4

v5 whole, which is shorter than its diff:
```python
import functools

import jax
import jax.numpy as jnp
from jax import lax
from jax.experimental import pallas as pl
from jax.experimental.pallas import tpu as pltpu
from jax.sharding import Mesh
from jax.sharding import PartitionSpec as P

GRP = ("x", "z")
VOCAB = ("y", "c")
CAPACITIES = (128, 256)
F32 = jnp.float32
BF16 = jnp.bfloat16
VMEM = pl.BlockSpec(memory_space=pltpu.VMEM)
SMEM = pl.BlockSpec(memory_space=pltpu.SMEM)
PARAMS = pltpu.CompilerParams(vmem_limit_bytes=20 * 1024 * 1024)


def iota(shape, dim):
    return lax.broadcasted_iota(jnp.int32, shape, dim)


def exchange(pieces, axes):
    return lax.all_to_all(pieces, axes, 0, 0, tiled=True)


def arrange_kernel(
    group_ref, core_ref, lengths_ref, owner_ref, length_row_ref, owner_row_ref, teacher_ref, student_ref,
    out_ref, t_place_ref, s_place_ref, info_ref,
):
    count, pad, _ = out_ref.shape
    width = teacher_ref.shape[2]
    rest = out_ref.shape[2] - width - student_ref.shape[2]
    group = group_ref[0]
    share = lengths_ref.shape[0] // count
    first = lengths_ref[share * group]
    upper = teacher_ref[0].astype(F32)
    lower = pltpu.roll(teacher_ref[1].astype(F32), first, 0)
    chosen = jnp.where(iota(upper.shape, 0) < first, upper, lower).astype(BF16)
    for k in range(count):
        out_ref[k, :, :width] = chosen
        out_ref[k, :, width : width + student_ref.shape[2]] = student_ref[0]
        if rest:
            out_ref[k, :, -rest:] = jnp.zeros((pad, rest), BF16)

    live = jnp.int32(0)
    mine = jnp.int32(0)
    for k in range(lengths_ref.shape[0]):
        live += lengths_ref[k]
        mine += jnp.where(owner_ref[k] == group, lengths_ref[k], 0)
    which = jnp.int32(0)
    for c in CAPACITIES[:-1]:
        which += (live > c).astype(jnp.int32)
    info_ref[0] = which
    info_ref[1] = core_ref[0]
    info_ref[2] = mine

    slots = t_place_ref.shape[1]
    deep = length_row_ref.shape[1]

    def column(ref):
        one = jnp.broadcast_to(ref[...].astype(F32), (deep, deep)).T
        return jnp.broadcast_to(one[:, :1], (deep, slots))

    length, owner = column(length_row_ref), column(owner_row_ref)
    seq = iota((deep, slots), 0)
    home = (iota((deep, slots), 1) // pad)
    zero = jnp.zeros((deep, slots), F32)

    def total(mask, value):
        return jnp.sum(jnp.where(mask, value, zero), axis=0, keepdims=True)

    home_f = home.astype(F32)
    step = (iota((1, slots), 1) % pad).astype(F32)
    t_count = total(seq // share == home, length)
    t_owner = total(seq == share * home, owner)
    t_start = total(owner < t_owner, length)
    s_count = total(owner == home_f, length)
    s_start = total(owner < home_f, length)
    t_place = jnp.where(step < t_count, t_start + step, -1.0)
    s_place = jnp.where(step < s_count, s_start + step, -1.0)
    t_place_ref[...] = t_place.astype(jnp.int32)
    s_place_ref[...] = s_place.astype(jnp.int32)


def arrange(group, core, lengths, owner, teacher_rows, student_rows, count):
    pad = student_rows.shape[1]
    width = -(-(teacher_rows.shape[2] + student_rows.shape[2]) // 128) * 128
    return pl.pallas_call(
        arrange_kernel,
        out_shape=[
            jax.ShapeDtypeStruct((count, pad, width), BF16),
            jax.ShapeDtypeStruct((1, count * pad), jnp.int32),
            jax.ShapeDtypeStruct((1, count * pad), jnp.int32),
            jax.ShapeDtypeStruct((3,), jnp.int32),
        ],
        in_specs=[SMEM] * 4 + [VMEM] * 4,
        out_specs=[VMEM, VMEM, VMEM, SMEM],
    )(
        group,
        core,
        lengths,
        owner,
        lengths.reshape(1, -1),
        owner.reshape(1, -1),
        teacher_rows,
        student_rows,
    )


def pack_kernel(t_width, rows_ref, t_place_ref, s_place_ref, out_ref):
    count, half, _ = out_ref.shape
    slots = rows_ref.shape[0]
    width = out_ref.shape[2] // 2

    def packed(place_ref, first, stop):
        pick = (place_ref[...] == iota((2 * half, slots), 0)).astype(F32).astype(BF16)
        found = jnp.dot(pick, rows_ref[:, first:stop], preferred_element_type=F32)
        return found[:half], found[half:]

    main = (width - t_width) // 128 * 128
    t = packed(t_place_ref, 0, t_width)
    low, high = packed(s_place_ref, t_width, width)
    value = jnp.concatenate(
        [*t, low[:, :main], high[:, :main], low[:, main:], high[:, main:]], axis=1
    ).astype(BF16)
    for k in range(count):
        out_ref[k] = value


def pack(rows, t_place, s_place, lanes, t_width, width, count):
    return pl.pallas_call(
        functools.partial(pack_kernel, t_width),
        out_shape=jax.ShapeDtypeStruct((count, lanes // 2, 2 * width), BF16),
        in_specs=[VMEM] * 3,
        out_specs=VMEM,
        compiler_params=PARAMS,
    )(rows, t_place, s_place)


def in_parts(stats, lanes):
    row = iota((16, lanes), 0)
    table = jnp.zeros((16, lanes), F32)
    for k, value in enumerate(stats):
        for part in range(3):
            rounded = value.astype(BF16).astype(F32)
            table = jnp.where(row == 3 * k + part, rounded, table)
            value = value - rounded
    return table


def from_parts(table, lanes):
    rows = [table[k : k + 1, :lanes] for k in range(9)]
    return [rows[k] + rows[k + 1] + rows[k + 2] for k in (0, 3, 6)]


def merged(stats):
    lse, mean, t_lse = zip(*stats)
    high = functools.reduce(jnp.maximum, lse)
    t_high = functools.reduce(jnp.maximum, t_lse)
    scale = [jnp.exp(v - high) for v in lse]
    total = sum(scale[1:], scale[0])
    scale = [v / total for v in scale]
    middle = sum((a * v for a, v in zip(scale[1:], mean[1:])), scale[0] * mean[0])
    t_total = sum((jnp.exp(v - t_high) for v in t_lse[1:]), jnp.exp(t_lse[0] - t_high))
    shift = [v - middle for v in mean]
    return scale, shift, [high + jnp.log(total), middle, t_high + jnp.log(t_total)]


def soften(t, s, g_ref, stat_ref):
    lanes = g_ref.shape[1] // 2
    gap = s - t
    t_top = jnp.max(t, axis=0, keepdims=True)
    t_lse = t_top + jnp.log(jnp.sum(jnp.exp(t - t_top), axis=0, keepdims=True))
    s_top = jnp.max(s, axis=0, keepdims=True)
    p = jnp.exp(s - s_top)
    total = jnp.sum(p, axis=0, keepdims=True)
    p = p / total
    mean = jnp.sum(p * gap, axis=0, keepdims=True)
    g_ref[:, :lanes] = (p * (gap - mean)).astype(BF16)
    g_ref[:, lanes:] = p.astype(BF16)
    table = in_parts([s_top + jnp.log(total), mean, t_lse], lanes)
    stat_ref[...] = jnp.concatenate([table, table], axis=1).astype(BF16)


def product(rows_ref, t_head_ref, s_head_ref, t, s):
    t_size, s_size = t_head_ref.shape[1], s_head_ref.shape[1]
    main = s_size // 128 * 128

    def rows(k, first, size):
        low = rows_ref[k, :, first : first + size]
        high = rows_ref[k, :, first + size : first + 2 * size]
        return jnp.concatenate([low, high], axis=0)

    count = rows_ref.shape[0]
    batch = 4
    for start in range(0, count, batch):
        ids = range(start, start + batch)
        t += jnp.dot(
            jnp.concatenate([rows(k, 0, t_size) for k in ids], axis=1),
            jnp.concatenate([t_head_ref[k] for k in ids], axis=0),
            preferred_element_type=F32,
        )
        s += jnp.dot(
            jnp.concatenate(
                [rows(k, 2 * t_size, main) for k in ids]
                + [rows(k, 2 * (t_size + main), s_size - main) for k in ids],
                axis=1,
            ),
            jnp.concatenate(
                [s_head_ref[k, :main] for k in ids] + [s_head_ref[k, main:] for k in ids],
                axis=0,
            ),
            preferred_element_type=F32,
        )
    return t, s


def first_kernel(
    info_ref, own_ref, t_head_ref, s_head_ref, t_ref, s_ref,
    s_own_ref, t_other_ref, s_other_ref, t_own_ref, sems,
):
    core = info_ref[1]
    copies = [
        pltpu.make_async_copy(head.at[:, c], to, sems.at[k])
        for k, (head, c, to) in enumerate(
            (
                (t_head_ref, core, t_own_ref),
                (s_head_ref, core, s_own_ref),
                (t_head_ref, 1 - core, t_other_ref),
                (s_head_ref, 1 - core, s_other_ref),
            )
        )
    ]
    for copy in copies:
        copy.start()
    copies[0].wait()
    copies[1].wait()
    zero = jnp.zeros(t_ref.shape, F32)
    t, s = product(own_ref, t_own_ref, s_own_ref, zero, zero)
    t_ref[...] = t
    s_ref[...] = s
    copies[2].wait()
    copies[3].wait()


def first(info, own, t_head, s_head):
    count, half_rows, width = own.shape
    vocab = t_head.shape[1]
    t_head = t_head.reshape(count, 2, -1, vocab)
    s_head = s_head.reshape(count, 2, -1, vocab)
    logit = jax.ShapeDtypeStruct((2 * half_rows, vocab), F32)
    t_part = (count, *t_head.shape[2:])
    s_part = (count, *s_head.shape[2:])
    return pl.pallas_call(
        first_kernel,
        out_shape=[
            logit,
            logit,
            jax.ShapeDtypeStruct(s_part, BF16),
            jax.ShapeDtypeStruct(t_part, BF16),
            jax.ShapeDtypeStruct(s_part, BF16),
        ],
        in_specs=[SMEM, VMEM] + [pl.BlockSpec(memory_space=pl.ANY)] * 2,
        out_specs=[VMEM] * 5,
        scratch_shapes=[pltpu.VMEM(t_part, BF16), pltpu.SemaphoreType.DMA((4,))],
        compiler_params=PARAMS,
        cost_estimate=pl.CostEstimate(
            flops=2 * own.size * vocab, bytes_accessed=4 * (t_head.size + s_head.size), transcendentals=0
        ),
    )(info, own, t_head, s_head)


def second_kernel(
    other_ref, t_ref, s_ref, s_own_ref, t_other_ref, s_other_ref, keep_ref, send_ref, g_ref, stat_ref
):
    t, s = product(other_ref, t_other_ref, s_other_ref, t_ref[...], s_ref[...])
    soften(t.T, s.T, g_ref, stat_ref)
    half = s_own_ref.shape[1]
    for k in range(keep_ref.shape[0]):
        for head_ref, out_ref in ((s_own_ref, keep_ref), (s_other_ref, send_ref)):
            out_ref[k, :half] = jnp.dot(
                head_ref[k], g_ref[...], preferred_element_type=F32
            ).astype(BF16)
            out_ref[k, half:] = stat_ref[...]


def second(other, t, s, s_own, t_other, s_other):
    lanes, vocab = t.shape
    count, half, _ = s_own.shape
    part = jax.ShapeDtypeStruct((count, half + 16, 2 * lanes), BF16)
    return pl.pallas_call(
        second_kernel,
        out_shape=[part, part],
        in_specs=[VMEM] * 6,
        out_specs=[VMEM] * 2,
        scratch_shapes=[
            pltpu.VMEM((vocab, 2 * lanes), BF16),
            pltpu.VMEM((16, 2 * lanes), BF16),
        ],
        compiler_params=PARAMS,
    )(other, t, s, s_own, t_other, s_other)


def pair_kernel(info_ref, keep_ref, came_ref, out_ref):
    lanes = out_ref.shape[2] // 2
    half = out_ref.shape[1] - 16
    low = info_ref[1] == 0
    kept = keep_ref[0, half:].astype(F32)
    come = came_ref[0, half:].astype(F32)
    first = jnp.where(low, kept, come)
    second = jnp.where(low, come, kept)
    scale, shift, stats = merged([from_parts(first, lanes), from_parts(second, lanes)])
    table = in_parts(stats, lanes)
    table = jnp.concatenate([table, table], axis=1).astype(BF16)
    own, other = (jnp.where(low, scale[0], scale[1]), jnp.where(low, scale[1], scale[0]))
    own_shift, other_shift = (
        own * jnp.where(low, shift[0], shift[1]),
        other * jnp.where(low, shift[1], shift[0]),
    )
    for k in range(out_ref.shape[0]):
        a = own * keep_ref[k, :half, :lanes].astype(F32)
        a += other * came_ref[k, :half, :lanes].astype(F32)
        b_own = keep_ref[k, :half, lanes:].astype(F32)
        b_other = came_ref[k, :half, lanes:].astype(F32)
        a += own_shift * b_own + other_shift * b_other
        out_ref[k, :half, :lanes] = a.astype(BF16)
        out_ref[k, :half, lanes:] = (own * b_own + other * b_other).astype(BF16)
        out_ref[k, half:] = table


def pair(info, keep, came):
    return pl.pallas_call(
        pair_kernel,
        out_shape=jax.ShapeDtypeStruct(keep.shape, BF16),
        in_specs=[SMEM, VMEM, VMEM],
        out_specs=VMEM,
        compiler_params=PARAMS,
    )(info, keep, came)


def spread_kernel(part_ref, place_ref, out_ref):
    lanes = part_ref.shape[2] // 2
    half = part_ref.shape[1] - 16
    count = part_ref.shape[0]
    groups, rows, width = out_ref.shape
    scale, shift, stats = merged(
        [from_parts(part_ref[k, half:].astype(F32), lanes) for k in range(count)]
    )
    a = jnp.zeros((half, lanes), F32)
    b = jnp.zeros((half, lanes), F32)
    for k in range(count):
        b_one = part_ref[k, :half, lanes:].astype(F32)
        a += scale[k] * part_ref[k, :half, :lanes].astype(F32) + (scale[k] * shift[k]) * b_one
        b += scale[k] * b_one
    rest = jnp.zeros((width - half - 16, lanes), F32)
    table = jnp.concatenate([in_parts(stats, lanes), rest], axis=0)
    slots = place_ref.shape[1]
    pick = (place_ref[...] == iota((lanes, slots), 0)).astype(F32).T.astype(BF16)

    def found(value):
        value = jnp.concatenate([value, table], axis=0).astype(BF16)
        value = lax.dot_general(
            pick, value, (((1,), (1,)), ((), ())), preferred_element_type=F32
        )
        return value.reshape(groups, rows // 2, width)

    out_ref[...] = jnp.concatenate([found(a), found(b)], axis=1).astype(BF16)


def spread(parts, place, pad):
    groups = place.shape[1] // pad
    width = -(-parts.shape[1] // 128) * 128
    return pl.pallas_call(
        spread_kernel,
        out_shape=jax.ShapeDtypeStruct((groups, 2 * pad, width), BF16),
        in_specs=[VMEM, VMEM],
        out_specs=VMEM,
        compiler_params=PARAMS,
    )(parts, place)


def finish_kernel(info_ref, part_ref, grad_ref, kl_ref):
    _, pad, width = grad_ref.shape
    parts = [part_ref[k].astype(F32) for k in range(part_ref.shape[0])]
    stats = []
    for part in parts:
        column = [part[:pad, width + k : width + k + 1] for k in range(9)]
        stats.append([column[k] + column[k + 1] + column[k + 2] for k in (0, 3, 6)])
    scale, shift, (lse, mean, t_lse) = merged(stats)
    grad = jnp.zeros((pad, width), F32)
    for part, a, b in zip(parts, scale, shift):
        grad += a * (part[:pad, :width] + b * part[pad:, :width])
    grad_ref[0] = grad.astype(BF16)
    kl = jnp.where(iota((pad, 1), 0) < info_ref[2], mean - lse + t_lse, 0.0)
    square = iota((pad, pad), 0) == iota((pad, pad), 1)
    kl_ref[...] = jnp.sum(jnp.where(square, kl, 0.0), axis=0, keepdims=True)


def finish(info, parts, width):
    pad = parts.shape[1] // 2
    return pl.pallas_call(
        finish_kernel,
        out_shape=[
            jax.ShapeDtypeStruct((1, pad, width), BF16),
            jax.ShapeDtypeStruct((1, pad), F32),
        ],
        in_specs=[SMEM, VMEM],
        out_specs=[VMEM, VMEM],
    )(info, parts)


def swap(value):
    return lax.ppermute(value, "c", ((0, 1), (1, 0)))


def some_rows(lanes, pad, t_width, width, operands):
    info, rows, t_place, s_place, teacher_head, student_head = operands
    ring = lax.axis_size("y")
    own = exchange(pack(rows, t_place, s_place, lanes, t_width, width, ring), "y")
    other = swap(own)
    t, s, *heads = first(info, own, teacher_head, student_head)
    keep, send = second(other, t, s, *heads)
    both = pair(info, keep, swap(send))
    return exchange(spread(exchange(both, "y"), s_place, pad), GRP)


def per_device(teacher_rows, student_rows, teacher_head, student_head, lengths, owner):
    groups = lax.axis_size(GRP)
    pad = student_rows.shape[1]
    t_width, s_width = teacher_rows.shape[2], student_rows.shape[2]
    group = lax.axis_index(GRP).astype(jnp.int32).reshape(1)
    core = lax.axis_index("c").astype(jnp.int32).reshape(1)
    mine, t_place, s_place, info = arrange(
        group, core, lengths, owner, teacher_rows, student_rows, groups
    )
    rows = exchange(mine, GRP).reshape(groups * pad, mine.shape[2])
    operands = (info, rows, t_place, s_place, teacher_head, student_head)
    branches = [functools.partial(some_rows, c, pad, t_width, t_width + s_width) for c in CAPACITIES]
    grad, divergence = finish(info, lax.switch(info[0], branches, operands), s_width)
    return divergence, grad


def solution(mesh):
    torus = Mesh(mesh.devices.reshape(4, 8, 8, 2), ("x", "z", "y", "c"))
    return jax.shard_map(
        per_device,
        mesh=torus,
        in_specs=(
            P(GRP, None, VOCAB),
            P(GRP, None, VOCAB),
            P(None, (*GRP, *VOCAB)),
            P(None, (*GRP, *VOCAB)),
            P(),
            P(),
        ),
        out_specs=(P(GRP, None), P(GRP, None, VOCAB)),
        check_vma=False,
    )
```

time: 159 us -> 140 us (0.88)
  between operations: 14.1 us -> 0.69 us
  waiting for transfers between devices: 15.3 us -> 13 us
    ppermute x2, waiting for transfers between devices: 5.19 us -> 2.88 us  [swap(): return lax.ppermute(value, 'c', ((0, 1), (1, 0)))]
    pallas_call x2 -> x3, Pallas kernels: 5.32 us -> 4.13 us  [the longest x1 2.29 us: first(): pl.pallas_call(first_kernel, out_shape=[logit, logit, jax.ShapeDtypeStruc...]
  transfers between devices with their start and end apart: 3 -> 3, of which waited for: 3 -> 3; matrix products, arithmetic and copies ran while one was open for 0% -> 0% of each run, Pallas kernels for 0% -> 2%
where the time goes in v5:
time: 140 us; the launch traced here: 138 us
  blocking collectives  90.4 us (65%)
  starting transfers between devices  24.1 us (17%)
  waiting for transfers between devices  13 us (9%)
  Pallas kernels  9.26 us (7%)
    all_to_all x3, blocking collectives, exchange(): return lax.all_to_all(pieces, axes, 0, 0, tiled=True)  90.4 us
    all_to_all x1, starting transfers between devices, exchange(): return lax.all_to_all(pieces, axes, 0, 0, tiled=True)  13.7 us
    ppermute x2, starting transfers between devices, swap(): return lax.ppermute(value, 'c', ((0, 1), (1, 0)))  10.4 us
    all_to_all x1, waiting for transfers between devices, exchange(): return lax.all_to_all(pieces, axes, 0, 0, tiled=True)  10.1 us
    ppermute x2, waiting for transfers between devices, swap(): return lax.ppermute(value, 'c', ((0, 1), (1, 0)))  2.88 us
  transfers between devices with their start and end apart: 3, of which 3 were waited for; matrix products, arithmetic and copies ran while one was open for 0% of the time, Pallas kernels for 2%

profile of v5, /device:TPU:1, one launch (start us, length us, event | category | flops | bytes accessed | tf_op | source)
XLA Modules:
  0.0 137.6 jit_solution(17607192525108642255)
XLA Ops:
  0.6 1.6 %shard_map.77 = (bf16[32,8,640]{2,1,0:T(8,128)(2,1)}, s32[1,256]{1,0:T(1,128)S(1)}, s32[1,256]{1,0:T(1,128)S(1)}, s32[3]{0:T(128)S(1)}) custom-call(s32[1]{0:T(128)} %bitcast.4.group_ref, s32[1]{0:T(128)} %bitcast.5.core_ref, s32[64]{0:T(128)} %lengths_ref.1, s32[64]{0:T(128)} %owner_ref.1, s32[1,64]{1,0:T(1,128)} %bitcast.18, s32[1,64]{1,0:T(1,128)} %bitcast.19, ...), custom_call_target="tpu_custom_call" | custom-call | tf_op jit(solution)/shard_map/pallas_call | solution.py:91
  2.3 13.7 %all-to-all-start.6 = ((bf16[32,8,640]{2,1,0:T(8,128)(2,1)}), bf16[32,8,640]{2,1,0:T(8,128)(2,1)S(1)}, u32[]{:S(2)}, u32[]{:S(2)}) async-start(bf16[32,8,640]{2,1,0:T(8,128)(2,1)} %get-tuple-element.62), calls=%async_computation.6 | async-start | bytes 655360 | tf_op jit(solution)/shard_map/all_to_all | solution.py:26
  16.0 10.1 %all-to-all-done.6 = bf16[32,8,640]{2,1,0:T(8,128)(2,1)S(1)} async-done(((bf16[32,8,640]{2,1,0:T(8,128)(2,1)}), bf16[32,8,640]{2,1,0:T(8,128)(2,1)S(1)}, u32[]{:S(2)}, u32[]{:S(2)}) %all-to-all-start.6) | async-done | bytes 327712 | tf_op jit(solution)/shard_map/all_to_all | solution.py:26
  26.2 109.9 %conditional.1 = (bf16[32,16,384]{2,1,0:T(8,128)(2,1)S(1)}) conditional(s32[]{:T(128)} %bitcast.8, (bf16[256,640]{1,0:T(8,128)(2,1)S(1)}, s32[1,256]{1,0:T(1,128)S(1)}, s32[1,256]{1,0:T(1,128)S(1)}, bf16[4096,256]{1,0:T(8,128)(2,1)}, bf16[5120,256]{1,0:T(8,128)(2,1)}, /*index=5*/s32[3]{0:T(128)S(1)}) %tuple.18, (bf16[256,640]{1,0:T(8,128)(2,1)S(1)}, ...), branch_computations={%region_0.0_spmd, %region_1.0_spmd} | conditional | flops 603979776 | bytes 59768976 | solution.py:442
  26.2 0.0 copy-start
  26.2 0.3 branch_0_fun.5
  26.5 33.0 %all_to_all.29.own_ref = bf16[8,64,1152]{2,1,0:T(8,128)(2,1)S(1)} all-to-all(bf16[8,64,1152]{2,1,0:T(8,128)(2,1)S(1)} %branch_0_fun.5), channel_id=1, replica_groups=mesh['x'=4,'z'=8,'y'=8,'c'=2] {'y'}, dimensions={0} | all-to-all | bytes 2359296 | tf_op jit(solution)/shard_map/cond/branch_0_fun/all_to_all | solution.py:26
  59.5 8.1 %collective-permute-start = (bf16[8,64,1152]{2,1,0:T(8,128)(2,1)S(1)}, bf16[8,64,1152]{2,1,0:T(8,128)(2,1)S(1)}, u32[]{:S(2)}, u32[]{:S(2)}) collective-permute-start(bf16[8,64,1152]{2,1,0:T(8,128)(2,1)S(1)} %all_to_all.29.own_ref), channel_id=1, source_target_pairs={{0,1},{1,0},{2,3},{3,2},{4,5},{5,4},{6,7},{7,6},{8,9},{9,8},{10,11... | collective-permute-start | bytes 3538952 | tf_op jit(solution)/shard_map/cond/branch_0_fun/ppermute | solution.py:416
  67.6 0.0 copy-done
  67.6 2.3 %branch_0_fun.6 = (f32[128,256]{1,0:T(8,128)S(1)}, f32[128,256]{1,0:T(8,128)S(1)}, bf16[8,320,256]{2,1,0:T(8,128)(2,1)S(1)}, bf16[8,256,256]{2,1,0:T(8,128)(2,1)S(1)}, bf16[8,320,256]{2,1,0:T(8,128)(2,1)S(1)}) custom-call(s32[3]{0:T(128)S(1)} %get-tuple-element.17.info_ref, bf16[8,64,1152]{2,1,0:T(8,128)(2,1)S(1)} %all_to_all.29.own_ref, ...), custom_call_target="tpu_custom_call" | custom-call | flops 301989888 | bytes 9437184 | tf_op jit(solution)/shard_map/cond/branch_0_fun/pallas_call | solution.py:257
  69.9 0.1 collective-permute-done.other_ref
  70.1 1.5 %branch_0_fun.7 = (bf16[8,336,256]{2,1,0:T(8,128)(2,1)S(1)}, bf16[8,336,256]{2,1,0:T(8,128)(2,1)S(1)}) custom-call(bf16[8,64,1152]{2,1,0:T(8,128)(2,1)S(1)} %collective-permute-done.other_ref, f32[128,256]{1,0:T(8,128)S(1)} %get-tuple-element.33.t_ref, f32[128,256]{1,0:T(8,128)S(1)} %get-tuple-element.34.s_ref, ...), custom_call_target="tpu_custom_call" | custom-call | tf_op jit(solution)/shard_map/cond/branch_0_fun/pallas_call | solution.py:294
  71.6 2.3 %collective-permute-start.1 = (bf16[8,336,256]{2,1,0:T(8,128)(2,1)S(1)}, bf16[8,336,256]{2,1,0:T(8,128)(2,1)S(1)}, u32[]{:S(2)}, u32[]{:S(2)}) collective-permute-start(bf16[8,336,256]{2,1,0:T(8,128)(2,1)S(1)} %get-tuple-element.39), channel_id=1, source_target_pairs={{0,1},{1,0},{2,3},{3,2},{4,5},{5,4},{6,7},{7,6},{8,9},{9,8},{10,11... | collective-permute-start | bytes 4128776 | tf_op jit(solution)/shard_map/cond/branch_0_fun/ppermute | solution.py:416
  73.9 2.7 %collective-permute-done.1.came_ref = bf16[8,336,256]{2,1,0:T(8,128)(2,1)S(1)} collective-permute-done((bf16[8,336,256]{2,1,0:T(8,128)(2,1)S(1)}, bf16[8,336,256]{2,1,0:T(8,128)(2,1)S(1)}, u32[]{:S(2)}, u32[]{:S(2)}) %collective-permute-start.1) | collective-permute-done | bytes 1376288 | tf_op jit(solution)/shard_map/cond/branch_0_fun/ppermute | solution.py:416
  76.6 1.3 branch_0_fun.8
  78.0 38.6 %all_to_all.30.part_ref = bf16[8,336,256]{2,1,0:T(8,128)(2,1)S(1)} all-to-all(bf16[8,336,256]{2,1,0:T(8,128)(2,1)S(1)} %branch_0_fun.8), channel_id=1, replica_groups=mesh['x'=4,'z'=8,'y'=8,'c'=2] {'y'}, dimensions={0} | all-to-all | bytes 2752512 | tf_op jit(solution)/shard_map/cond/branch_0_fun/all_to_all | solution.py:26
  116.6 0.6 branch_0_fun.9
  117.3 18.8 %all_to_all.31 = bf16[32,16,384]{2,1,0:T(8,128)(2,1)S(1)} all-to-all(bf16[32,16,384]{2,1,0:T(8,128)(2,1)S(1)} %branch_0_fun.9), channel_id=1, replica_groups=mesh['x'=4,'z'=8,'y'=8,'c'=2] {'x','z'}, dimensions={0} | all-to-all | bytes 786432 | tf_op jit(solution)/shard_map/cond/branch_0_fun/all_to_all | solution.py:26
  136.0 1.5 %shard_map.78 = (bf16[1,8,320]{2,1,0:T(8,128)(2,1)}, f32[1,8]{1,0:T(1,128)}) custom-call(s32[3]{0:T(128)S(1)} %get-tuple-element.61.info_ref, bf16[32,16,384]{2,1,0:T(8,128)(2,1)S(1)} %get-tuple-element.67.part_ref), custom_call_target="tpu_custom_call" | custom-call | tf_op jit(solution)/shard_map/pallas_call | solution.py:404
Async XLA Ops:
  2.3 23.9 %all-to-all-start.6 = ((bf16[32,8,640]{2,1,0:T(8,128)(2,1)}), bf16[32,8,640]{2,1,0:T(8,128)(2,1)S(1)}, u32[]{:S(2)}, u32[]{:S(2)}) async-start(bf16[32,8,640]{2,1,0:T(8,128)(2,1)} %get-tuple-element.62), calls=%async_computation.6 | async-start | bytes 655360 | tf_op jit(solution)/shard_map/all_to_all | solution.py:26
  26.2 41.5 %copy-start = (bf16[5120,256]{1,0:T(8,128)(2,1)S(1)}, bf16[5120,256]{1,0:T(8,128)(2,1)}, u32[]{:S(2)}) copy-start(bf16[5120,256]{1,0:T(8,128)(2,1)} %get-tuple-element.32) | copy-start | bytes 7864324 | tf_op jit(solution)/shard_map/cond
  59.5 10.6 %collective-permute-start = (bf16[8,64,1152]{2,1,0:T(8,128)(2,1)S(1)}, bf16[8,64,1152]{2,1,0:T(8,128)(2,1)S(1)}, u32[]{:S(2)}, u32[]{:S(2)}) collective-permute-start(bf16[8,64,1152]{2,1,0:T(8,128)(2,1)S(1)} %all_to_all.29.own_ref), channel_id=1, source_target_pairs={{0,1},{1,0},{2,3},{3,2},{4,5},{5,4},{6,7},{7,6},{8,9},{9,8},{10,11... | collective-permute-start | bytes 3538952 | tf_op jit(solution)/shard_map/cond/branch_0_fun/ppermute | solution.py:416
  71.6 5.0 %collective-permute-start.1 = (bf16[8,336,256]{2,1,0:T(8,128)(2,1)S(1)}, bf16[8,336,256]{2,1,0:T(8,128)(2,1)S(1)}, u32[]{:S(2)}, u32[]{:S(2)}) collective-permute-start(bf16[8,336,256]{2,1,0:T(8,128)(2,1)S(1)} %get-tuple-element.39), channel_id=1, source_target_pairs={{0,1},{1,0},{2,3},{3,2},{4,5},{5,4},{6,7},{7,6},{8,9},{9,8},{10,11... | collective-permute-start | bytes 4128776 | tf_op jit(solution)/shard_map/cond/branch_0_fun/ppermute | solution.py:416

commit v6 on v5

--- a/solution.py
+++ b/solution.py
@@ -9,7 +9,10 @@
 from jax.sharding import PartitionSpec as P
 
 GRP = ("x", "z")
-VOCAB = ("y", "c")
+Y = ("yh", "yl")
+VOCAB = ("yh", "yl", "c")
+NEAR = ("x", "yl")
+REST = ("yh", "x", "z")
 CAPACITIES = (128, 256)
 F32 = jnp.float32
 BF16 = jnp.bfloat16
@@ -304,9 +307,9 @@
     )(other, t, s, s_own, t_other, s_other)
 
 
-def pair_kernel(info_ref, keep_ref, came_ref, out_ref):
+def pair_kernel(parts, info_ref, keep_ref, came_ref, out_ref):
     lanes = out_ref.shape[2] // 2
-    half = out_ref.shape[1] - 16
+    half = keep_ref.shape[1] - 16
     low = info_ref[1] == 0
     kept = keep_ref[0, half:].astype(F32)
     come = came_ref[0, half:].astype(F32)
@@ -320,21 +323,30 @@
         own * jnp.where(low, shift[0], shift[1]),
         other * jnp.where(low, shift[1], shift[0]),
     )
-    for k in range(out_ref.shape[0]):
+    per = half // parts
+    near = out_ref.shape[0] // parts
+    last = out_ref.shape[1] - 16
+    for k in range(keep_ref.shape[0]):
         a = own * keep_ref[k, :half, :lanes].astype(F32)
         a += other * came_ref[k, :half, :lanes].astype(F32)
         b_own = keep_ref[k, :half, lanes:].astype(F32)
         b_other = came_ref[k, :half, lanes:].astype(F32)
         a += own_shift * b_own + other_shift * b_other
-        out_ref[k, :half, :lanes] = a.astype(BF16)
-        out_ref[k, :half, lanes:] = (own * b_own + other * b_other).astype(BF16)
-        out_ref[k, half:] = table
-
-
-def pair(info, keep, came):
-    return pl.pallas_call(
-        pair_kernel,
-        out_shape=jax.ShapeDtypeStruct(keep.shape, BF16),
+        both = jnp.concatenate([a, own * b_own + other * b_other], axis=1).astype(BF16)
+        first = k // near * per
+        for q in range(parts):
+            piece = both[q * per : (q + 1) * per]
+            out_ref[q * near + k % near, first : first + per] = piece
+    for k in range(out_ref.shape[0]):
+        out_ref[k, last:] = table
+
+
+def pair(info, keep, came, parts, near):
+    ring, deep, width = keep.shape
+    deep = (deep - 16) // parts * (ring // near) + 16
+    return pl.pallas_call(
+        functools.partial(pair_kernel, parts),
+        out_shape=jax.ShapeDtypeStruct((parts * near, deep, width), BF16),
         in_specs=[SMEM, VMEM, VMEM],
         out_specs=VMEM,
         compiler_params=PARAMS,
@@ -345,7 +357,12 @@
     lanes = part_ref.shape[2] // 2
     half = part_ref.shape[1] - 16
     count = part_ref.shape[0]
-    groups, rows, width = out_ref.shape
+    slots = place_ref.shape[1]
+    pad = out_ref.shape[1] // 2
+    width = out_ref.shape[2]
+    groups = slots // pad
+    far = out_ref.shape[0] // groups
+    per = half // far
     scale, shift, stats = merged(
         [from_parts(part_ref[k, half:].astype(F32), lanes) for k in range(count)]
     )
@@ -355,54 +372,72 @@
         b_one = part_ref[k, :half, lanes:].astype(F32)
         a += scale[k] * part_ref[k, :half, :lanes].astype(F32) + (scale[k] * shift[k]) * b_one
         b += scale[k] * b_one
-    rest = jnp.zeros((width - half - 16, lanes), F32)
+    rest = jnp.zeros((width - per - 16, lanes), F32)
     table = jnp.concatenate([in_parts(stats, lanes), rest], axis=0)
-    slots = place_ref.shape[1]
     pick = (place_ref[...] == iota((lanes, slots), 0)).astype(F32).T.astype(BF16)
 
     def found(value):
-        value = jnp.concatenate([value, table], axis=0).astype(BF16)
-        value = lax.dot_general(
-            pick, value, (((1,), (1,)), ((), ())), preferred_element_type=F32
+        pieces = []
+        for k in range(far):
+            pieces += [value[k * per : (k + 1) * per], table]
+        return lax.dot_general(
+            pick,
+            jnp.concatenate(pieces, axis=0).astype(BF16),
+            (((1,), (1,)), ((), ())),
+            preferred_element_type=F32,
         )
-        return value.reshape(groups, rows // 2, width)
-
-    out_ref[...] = jnp.concatenate([found(a), found(b)], axis=1).astype(BF16)
-
-
-def spread(parts, place, pad):
+
+    a, b = found(a), found(b)
+    for k in range(far):
+        both = [v[:, k * width : (k + 1) * width].reshape(groups, pad, width) for v in (a, b)]
+        out_ref[k * groups : (k + 1) * groups] = jnp.concatenate(both, axis=1).astype(BF16)
+
+
+def spread(parts, place, pad, far):
     groups = place.shape[1] // pad
-    width = -(-parts.shape[1] // 128) * 128
+    per = (parts.shape[1] - 16) // far
+    width = -(-(per + 16) // 128) * 128
     return pl.pallas_call(
         spread_kernel,
-        out_shape=jax.ShapeDtypeStruct((groups, 2 * pad, width), BF16),
+        out_shape=jax.ShapeDtypeStruct((far * groups, 2 * pad, width), BF16),
         in_specs=[VMEM, VMEM],
         out_specs=VMEM,
         compiler_params=PARAMS,
     )(parts, place)
 
 
-def finish_kernel(info_ref, part_ref, grad_ref, kl_ref):
+def finish_kernel(far, near, info_ref, part_ref, grad_ref, kl_ref):
     _, pad, width = grad_ref.shape
-    parts = [part_ref[k].astype(F32) for k in range(part_ref.shape[0])]
+    per = width // near
+    groups = part_ref.shape[0] // far
+    share = groups // near
+
+    def source(q):
+        return [f * groups + q * share + k for f in range(far) for k in range(share)]
+
     stats = []
-    for part in parts:
-        column = [part[:pad, width + k : width + k + 1] for k in range(9)]
-        stats.append([column[k] + column[k + 1] + column[k + 2] for k in (0, 3, 6)])
+    for k in source(0):
+        part = part_ref[k].astype(F32)[:pad]
+        column = [part[:, per + j : per + j + 1] for j in range(9)]
+        stats.append([column[j] + column[j + 1] + column[j + 2] for j in (0, 3, 6)])
     scale, shift, (lse, mean, t_lse) = merged(stats)
-    grad = jnp.zeros((pad, width), F32)
-    for part, a, b in zip(parts, scale, shift):
-        grad += a * (part[:pad, :width] + b * part[pad:, :width])
-    grad_ref[0] = grad.astype(BF16)
+    pieces = []
+    for q in range(near):
+        grad = jnp.zeros((pad, part_ref.shape[2]), F32)
+        for k, a, b in zip(source(q), scale, shift):
+            part = part_ref[k].astype(F32)
+            grad += a * (part[:pad] + b * part[pad:])
+        pieces.append(grad[:, :per])
+    grad_ref[0] = jnp.concatenate(pieces, axis=1).astype(BF16)
     kl = jnp.where(iota((pad, 1), 0) < info_ref[2], mean - lse + t_lse, 0.0)
     square = iota((pad, pad), 0) == iota((pad, pad), 1)
     kl_ref[...] = jnp.sum(jnp.where(square, kl, 0.0), axis=0, keepdims=True)
 
 
-def finish(info, parts, width):
+def finish(info, parts, width, far, near):
     pad = parts.shape[1] // 2
     return pl.pallas_call(
-        finish_kernel,
+        functools.partial(finish_kernel, far, near),
         out_shape=[
             jax.ShapeDtypeStruct((1, pad, width), BF16),
             jax.ShapeDtypeStruct((1, pad), F32),
@@ -418,13 +453,12 @@
 
 def some_rows(lanes, pad, t_width, width, operands):
     info, rows, t_place, s_place, teacher_head, student_head = operands
-    ring = lax.axis_size("y")
-    own = exchange(pack(rows, t_place, s_place, lanes, t_width, width, ring), "y")
+    own = exchange(pack(rows, t_place, s_place, lanes, t_width, width, lax.axis_size(Y)), Y)
     other = swap(own)
     t, s, *heads = first(info, own, teacher_head, student_head)
     keep, send = second(other, t, s, *heads)
-    both = pair(info, keep, swap(send))
-    return exchange(spread(exchange(both, "y"), s_place, pad), GRP)
+    both = pair(info, keep, swap(send), lax.axis_size("x"), lax.axis_size("yl"))
+    return exchange(spread(exchange(both, NEAR), s_place, pad, lax.axis_size("yh")), REST)
 
 
 def per_device(teacher_rows, student_rows, teacher_head, student_head, lengths, owner):
@@ -439,12 +473,13 @@
     rows = exchange(mine, GRP).reshape(groups * pad, mine.shape[2])
     operands = (info, rows, t_place, s_place, teacher_head, student_head)
     branches = [functools.partial(some_rows, c, pad, t_width, t_width + s_width) for c in CAPACITIES]
-    grad, divergence = finish(info, lax.switch(info[0], branches, operands), s_width)
+    parts = lax.switch(info[0], branches, operands)
+    grad, divergence = finish(info, parts, s_width, lax.axis_size("yh"), lax.axis_size("x"))
     return divergence, grad
 
 
 def solution(mesh):
-    torus = Mesh(mesh.devices.reshape(4, 8, 8, 2), ("x", "z", "y", "c"))
+    torus = Mesh(mesh.devices.reshape(4, 8, 4, 2, 2), ("x", "z", "yh", "yl", "c"))
     return jax.shard_map(
         per_device,
         mesh=torus,

time: 140 us -> 178 us (1.27)
  the two profiles are of different devices: /device:TPU:1 before, /device:TPU:8 now
where the time goes in v6:
time: 178 us
  blocking collectives  127 us (71%)
  waiting for transfers between devices  21.1 us (12%)
  starting transfers between devices  17.3 us (10%)
  Pallas kernels  11 us (6%)
    all_to_all x3, blocking collectives, exchange(): return lax.all_to_all(pieces, axes, 0, 0, tiled=True)  127 us
    all_to_all x1, waiting for transfers between devices, exchange(): return lax.all_to_all(pieces, axes, 0, 0, tiled=True)  13.5 us
    all_to_all x1, starting transfers between devices, exchange(): return lax.all_to_all(pieces, axes, 0, 0, tiled=True)  13.2 us
    ppermute x2, waiting for transfers between devices, swap(): return lax.ppermute(value, 'c', ((0, 1), (1, 0)))  7.55 us
    ppermute x2, starting transfers between devices, swap(): return lax.ppermute(value, 'c', ((0, 1), (1, 0)))  4.13 us
  transfers between devices with their start and end apart: 3, of which 3 were waited for; matrix products, arithmetic and copies ran while one was open for 0% of the time, Pallas kernels for 1%

profile of v6, /device:TPU:8, one launch (start us, length us, event | category | flops | bytes accessed | tf_op | source)
XLA Modules:
  0.0 177.6 jit_solution(722822521863738555)
XLA Ops:
  0.6 1.6 shard_map.77
  2.3 13.2 %all-to-all-start.6 = ((bf16[32,8,640]{2,1,0:T(8,128)(2,1)}), bf16[32,8,640]{2,1,0:T(8,128)(2,1)S(1)}, u32[]{:S(2)}, u32[]{:S(2)}) async-start(bf16[32,8,640]{2,1,0:T(8,128)(2,1)} %get-tuple-element.62), calls=%async_computation.6 | async-start | bytes 655360 | tf_op jit(solution)/shard_map/all_to_all | solution.py:29
  15.5 13.5 %all-to-all-done.6 = bf16[32,8,640]{2,1,0:T(8,128)(2,1)S(1)} async-done(((bf16[32,8,640]{2,1,0:T(8,128)(2,1)}), bf16[32,8,640]{2,1,0:T(8,128)(2,1)S(1)}, u32[]{:S(2)}, u32[]{:S(2)}) %all-to-all-start.6) | async-done | bytes 327712 | tf_op jit(solution)/shard_map/all_to_all | solution.py:29
  29.0 147.0 %conditional.1 = (bf16[128,16,128]{2,1,0:T(8,128)(2,1)S(1)}) conditional(s32[]{:T(128)} %bitcast.8, (bf16[256,640]{1,0:T(8,128)(2,1)S(1)}, s32[1,256]{1,0:T(1,128)S(1)}, s32[1,256]{1,0:T(1,128)S(1)}, bf16[4096,256]{1,0:T(8,128)(2,1)}, bf16[5120,256]{1,0:T(8,128)(2,1)}, /*index=5*/s32[3]{0:T(128)S(1)}) %tuple.18, (bf16[256,640]{1,0:T(8,128)(2,1)S(1)}, ...), branch_computations={%region_0.0_spmd, %region_1.0_spmd} | conditional | flops 603979776 | bytes 60031120 | solution.py:476
  29.0 0.5 branch_1_fun.5
  29.5 0.0 copy-start.1
  29.5 0.0 copy-start.2
  29.5 59.3 %all_to_all.32.own_ref = bf16[8,128,1152]{2,1,0:T(8,128)(2,1)S(1)} all-to-all(bf16[8,128,1152]{2,1,0:T(8,128)(2,1)S(1)} %branch_1_fun.5), channel_id=1, replica_groups=mesh['x'=4,'z'=8,'yh'=4,'yl'=2,'c'=2] {'yh','yl'}, dimensions={0} | all-to-all | bytes 4718592 | tf_op jit(solution)/shard_map/cond/branch_1_fun/all_to_all | solution.py:29
  88.8 1.9 %collective-permute-start.2 = (bf16[8,128,1152]{2,1,0:T(8,128)(2,1)S(1)}, bf16[8,128,1152]{2,1,0:T(8,128)(2,1)S(1)}, u32[]{:S(2)}, u32[]{:S(2)}) collective-permute-start(bf16[8,128,1152]{2,1,0:T(8,128)(2,1)S(1)} %all_to_all.32.own_ref), channel_id=1, source_target_pairs={{0,1},{1,0},{2,3},{3,2},{4,5},{5,4},{6,7},{7,6},{8,9},{9,8},{10,11... | collective-permute-start | bytes 7077896 | tf_op jit(solution)/shard_map/cond/branch_1_fun/ppermute | solution.py:451
  90.7 0.0 copy-done.1
  90.7 0.0 copy-done.2
  90.7 1.7 branch_1_fun.6
  92.4 2.8 %collective-permute-done.2.other_ref = bf16[8,128,1152]{2,1,0:T(8,128)(2,1)S(1)} collective-permute-done((bf16[8,128,1152]{2,1,0:T(8,128)(2,1)S(1)}, bf16[8,128,1152]{2,1,0:T(8,128)(2,1)S(1)}, u32[]{:S(2)}, u32[]{:S(2)}) %collective-permute-start.2) | collective-permute-done | bytes 2359328 | tf_op jit(solution)/shard_map/cond/branch_1_fun/ppermute | solution.py:451
  95.2 2.7 %branch_1_fun.7 = (bf16[8,336,512]{2,1,0:T(8,128)(2,1)S(1)}, bf16[8,336,512]{2,1,0:T(8,128)(2,1)S(1)}) custom-call(bf16[8,128,1152]{2,1,0:T(8,128)(2,1)S(1)} %collective-permute-done.2.other_ref, f32[256,256]{1,0:T(8,128)S(1)} %get-tuple-element.46.t_ref, f32[256,256]{1,0:T(8,128)S(1)} %get-tuple-element.47.s_ref, ...), custom_call_target="tpu_custom_call" | custom-call | tf_op jit(solution)/shard_map/cond/branch_1_fun/pallas_call | solution.py:297
  97.9 2.2 %collective-permute-start.3 = (bf16[8,336,512]{2,1,0:T(8,128)(2,1)S(1)}, bf16[8,336,512]{2,1,0:T(8,128)(2,1)S(1)}, u32[]{:S(2)}, u32[]{:S(2)}) collective-permute-start(bf16[8,336,512]{2,1,0:T(8,128)(2,1)S(1)} %get-tuple-element.52), channel_id=1, source_target_pairs={{0,1},{1,0},{2,3},{3,2},{4,5},{5,4},{6,7},{7,6},{8,9},{9,8},{10,11... | collective-permute-start | bytes 8257544 | tf_op jit(solution)/shard_map/cond/branch_1_fun/ppermute | solution.py:451
  100.1 4.8 %collective-permute-done.3.came_ref = bf16[8,336,512]{2,1,0:T(8,128)(2,1)S(1)} collective-permute-done((bf16[8,336,512]{2,1,0:T(8,128)(2,1)S(1)}, bf16[8,336,512]{2,1,0:T(8,128)(2,1)S(1)}, u32[]{:S(2)}, u32[]{:S(2)}) %collective-permute-start.3) | collective-permute-done | bytes 2752544 | tf_op jit(solution)/shard_map/cond/branch_1_fun/ppermute | solution.py:451
  104.9 1.9 %branch_1_fun.8 = bf16[8,336,512]{2,1,0:T(8,128)(2,1)S(1)} custom-call(s32[3]{0:T(128)S(1)} %get-tuple-element.40.info_ref, bf16[8,336,512]{2,1,0:T(8,128)(2,1)S(1)} %get-tuple-element.51.keep_ref, bf16[8,336,512]{2,1,0:T(8,128)(2,1)S(1)} %collective-permute-done.3.came_ref), custom_call_target="tpu_custom_call" | custom-call | tf_op jit(solution)/shard_map/cond/branch_1_fun/pallas_call | solution.py:347
  106.8 37.7 %all_to_all.33.part_ref = bf16[8,336,512]{2,1,0:T(8,128)(2,1)S(1)} all-to-all(bf16[8,336,512]{2,1,0:T(8,128)(2,1)S(1)} %branch_1_fun.8), channel_id=1, replica_groups=mesh['x'=4,'z'=8,'yh'=4,'yl'=2,'c'=2] {'x','yl'}, dimensions={0} | all-to-all | bytes 5505024 | tf_op jit(solution)/shard_map/cond/branch_1_fun/all_to_all | solution.py:29
  144.5 1.1 branch_1_fun.9
  145.6 30.4 %all_to_all.34 = bf16[128,16,128]{2,1,0:T(8,128)(2,1)S(1)} all-to-all(bf16[128,16,128]{2,1,0:T(8,128)(2,1)S(1)} %branch_1_fun.9), channel_id=1, replica_groups=mesh['x'=4,'z'=8,'yh'=4,'yl'=2,'c'=2] {'yh','x','z'}, dimensions={0} | all-to-all | bytes 1048576 | tf_op jit(solution)/shard_map/cond/branch_1_fun/all_to_all | solution.py:29
  176.0 1.6 shard_map.78
Async XLA Ops:
  2.3 26.7 %all-to-all-start.6 = ((bf16[32,8,640]{2,1,0:T(8,128)(2,1)}), bf16[32,8,640]{2,1,0:T(8,128)(2,1)S(1)}, u32[]{:S(2)}, u32[]{:S(2)}) async-start(bf16[32,8,640]{2,1,0:T(8,128)(2,1)} %get-tuple-element.62), calls=%async_computation.6 | async-start | bytes 655360 | tf_op jit(solution)/shard_map/all_to_all | solution.py:29
  29.5 61.2 %copy-start.1 = (bf16[5120,256]{1,0:T(8,128)(2,1)S(1)}, bf16[5120,256]{1,0:T(8,128)(2,1)}, u32[]{:S(2)}) copy-start(bf16[5120,256]{1,0:T(8,128)(2,1)} %get-tuple-element.45) | copy-start | bytes 7864324 | tf_op jit(solution)/shard_map/cond
  29.5 61.2 %copy-start.2 = (bf16[4096,256]{1,0:T(8,128)(2,1)S(1)}, bf16[4096,256]{1,0:T(8,128)(2,1)}, u32[]{:S(2)}) copy-start(bf16[4096,256]{1,0:T(8,128)(2,1)} %get-tuple-element.44) | copy-start | bytes 6291460 | tf_op jit(solution)/shard_map/cond
  88.8 6.4 %collective-permute-start.2 = (bf16[8,128,1152]{2,1,0:T(8,128)(2,1)S(1)}, bf16[8,128,1152]{2,1,0:T(8,128)(2,1)S(1)}, u32[]{:S(2)}, u32[]{:S(2)}) collective-permute-start(bf16[8,128,1152]{2,1,0:T(8,128)(2,1)S(1)} %all_to_all.32.own_ref), channel_id=1, source_target_pairs={{0,1},{1,0},{2,3},{3,2},{4,5},{5,4},{6,7},{7,6},{8,9},{9,8},{10,11... | collective-permute-start | bytes 7077896 | tf_op jit(solution)/shard_map/cond/branch_1_fun/ppermute | solution.py:451
  97.9 7.0 %collective-permute-start.3 = (bf16[8,336,512]{2,1,0:T(8,128)(2,1)S(1)}, bf16[8,336,512]{2,1,0:T(8,128)(2,1)S(1)}, u32[]{:S(2)}, u32[]{:S(2)}) collective-permute-start(bf16[8,336,512]{2,1,0:T(8,128)(2,1)S(1)} %get-tuple-element.52), channel_id=1, source_target_pairs={{0,1},{1,0},{2,3},{3,2},{4,5},{5,4},{6,7},{7,6},{8,9},{9,8},{10,11... | collective-permute-start | bytes 8257544 | tf_op jit(solution)/shard_map/cond/branch_1_fun/ppermute | solution.py:451

commit v7 on v6

--- a/solution.py
+++ b/solution.py
@@ -13,7 +13,7 @@
 VOCAB = ("yh", "yl", "c")
 NEAR = ("x", "yl")
 REST = ("yh", "x", "z")
-CAPACITIES = (128, 256)
+CAPACITIES = ((128, 128), (160, 192), (256, 256))
 F32 = jnp.float32
 BF16 = jnp.bfloat16
 VMEM = pl.BlockSpec(memory_space=pltpu.VMEM)
@@ -29,16 +29,12 @@
     return lax.all_to_all(pieces, axes, 0, 0, tiled=True)
 
 
-def arrange_kernel(
-    group_ref, core_ref, lengths_ref, owner_ref, length_row_ref, owner_row_ref, teacher_ref, student_ref,
-    out_ref, t_place_ref, s_place_ref, info_ref,
-):
+def arrange_kernel(group_ref, lengths_ref, teacher_ref, student_ref, out_ref):
     count, pad, _ = out_ref.shape
     width = teacher_ref.shape[2]
     rest = out_ref.shape[2] - width - student_ref.shape[2]
-    group = group_ref[0]
     share = lengths_ref.shape[0] // count
-    first = lengths_ref[share * group]
+    first = lengths_ref[share * group_ref[0]]
     upper = teacher_ref[0].astype(F32)
     lower = pltpu.roll(teacher_ref[1].astype(F32), first, 0)
     chosen = jnp.where(iota(upper.shape, 0) < first, upper, lower).astype(BF16)
@@ -48,13 +44,30 @@
         if rest:
             out_ref[k, :, -rest:] = jnp.zeros((pad, rest), BF16)
 
+
+def arrange(group, lengths, teacher_rows, student_rows, count):
+    pad = student_rows.shape[1]
+    width = -(-(teacher_rows.shape[2] + student_rows.shape[2]) // 128) * 128
+    return pl.pallas_call(
+        arrange_kernel,
+        out_shape=jax.ShapeDtypeStruct((count, pad, width), BF16),
+        in_specs=[SMEM] * 2 + [VMEM] * 2,
+        out_specs=VMEM,
+    )(group, lengths, teacher_rows, student_rows)
+
+
+def routing_kernel(
+    pad, group_ref, core_ref, lengths_ref, owner_ref, length_row_ref, owner_row_ref,
+    t_place_ref, s_place_ref, info_ref,
+):
+    group = group_ref[0]
     live = jnp.int32(0)
     mine = jnp.int32(0)
     for k in range(lengths_ref.shape[0]):
         live += lengths_ref[k]
         mine += jnp.where(owner_ref[k] == group, lengths_ref[k], 0)
     which = jnp.int32(0)
-    for c in CAPACITIES[:-1]:
+    for c, _ in CAPACITIES[:-1]:
         which += (live > c).astype(jnp.int32)
     info_ref[0] = which
     info_ref[1] = core_ref[0]
@@ -62,6 +75,7 @@
 
     slots = t_place_ref.shape[1]
     deep = length_row_ref.shape[1]
+    share = deep * pad // slots
 
     def column(ref):
         one = jnp.broadcast_to(ref[...].astype(F32), (deep, deep)).T
@@ -69,7 +83,7 @@
 
     length, owner = column(length_row_ref), column(owner_row_ref)
     seq = iota((deep, slots), 0)
-    home = (iota((deep, slots), 1) // pad)
+    home = iota((deep, slots), 1) // pad
     zero = jnp.zeros((deep, slots), F32)
 
     def total(mask, value):
@@ -88,29 +102,18 @@
     s_place_ref[...] = s_place.astype(jnp.int32)
 
 
-def arrange(group, core, lengths, owner, teacher_rows, student_rows, count):
-    pad = student_rows.shape[1]
-    width = -(-(teacher_rows.shape[2] + student_rows.shape[2]) // 128) * 128
-    return pl.pallas_call(
-        arrange_kernel,
+def routing(group, core, lengths, owner, slots, pad):
+    return pl.pallas_call(
+        functools.partial(routing_kernel, pad),
         out_shape=[
-            jax.ShapeDtypeStruct((count, pad, width), BF16),
-            jax.ShapeDtypeStruct((1, count * pad), jnp.int32),
-            jax.ShapeDtypeStruct((1, count * pad), jnp.int32),
+            jax.ShapeDtypeStruct((1, slots), jnp.int32),
+            jax.ShapeDtypeStruct((1, slots), jnp.int32),
             jax.ShapeDtypeStruct((3,), jnp.int32),
         ],
-        in_specs=[SMEM] * 4 + [VMEM] * 4,
-        out_specs=[VMEM, VMEM, VMEM, SMEM],
-    )(
-        group,
-        core,
-        lengths,
-        owner,
-        lengths.reshape(1, -1),
-        owner.reshape(1, -1),
-        teacher_rows,
-        student_rows,
-    )
+        in_specs=[SMEM] * 4 + [VMEM] * 2,
+        out_specs=[VMEM, VMEM, SMEM],
+        cost_estimate=pl.CostEstimate(flops=10**6, bytes_accessed=10**6, transcendentals=0),
+    )(group, core, lengths, owner, lengths.reshape(1, -1), owner.reshape(1, -1))
 
 
 def pack_kernel(t_width, rows_ref, t_place_ref, s_place_ref, out_ref):
@@ -182,8 +185,7 @@
     total = jnp.sum(p, axis=0, keepdims=True)
     p = p / total
     mean = jnp.sum(p * gap, axis=0, keepdims=True)
-    g_ref[:, :lanes] = (p * (gap - mean)).astype(BF16)
-    g_ref[:, lanes:] = p.astype(BF16)
+    g_ref[...] = jnp.concatenate([p * (gap - mean), p], axis=1).astype(BF16)
     table = in_parts([s_top + jnp.log(total), mean, t_lse], lanes)
     stat_ref[...] = jnp.concatenate([table, table], axis=1).astype(BF16)
 
@@ -280,7 +282,15 @@
     other_ref, t_ref, s_ref, s_own_ref, t_other_ref, s_other_ref, keep_ref, send_ref, g_ref, stat_ref
 ):
     t, s = product(other_ref, t_other_ref, s_other_ref, t_ref[...], s_ref[...])
-    soften(t.T, s.T, g_ref, stat_ref)
+    count, lanes = t.shape[0], g_ref.shape[1] // 2
+
+    def turned(value):
+        rest = -count % 128
+        if rest:
+            value = jnp.concatenate([value, jnp.zeros((rest, value.shape[1]), F32)], axis=0)
+        return value.T[:, :lanes]
+
+    soften(turned(t), turned(s), g_ref, stat_ref)
     half = s_own_ref.shape[1]
     for k in range(keep_ref.shape[0]):
         for head_ref, out_ref in ((s_own_ref, keep_ref), (s_other_ref, send_ref)):
@@ -290,8 +300,8 @@
             out_ref[k, half:] = stat_ref[...]
 
 
-def second(other, t, s, s_own, t_other, s_other):
-    lanes, vocab = t.shape
+def second(other, t, s, s_own, t_other, s_other, lanes):
+    vocab = t.shape[1]
     count, half, _ = s_own.shape
     part = jax.ShapeDtypeStruct((count, half + 16, 2 * lanes), BF16)
     return pl.pallas_call(
@@ -327,10 +337,9 @@
     near = out_ref.shape[0] // parts
     last = out_ref.shape[1] - 16
     for k in range(keep_ref.shape[0]):
-        a = own * keep_ref[k, :half, :lanes].astype(F32)
-        a += other * came_ref[k, :half, :lanes].astype(F32)
-        b_own = keep_ref[k, :half, lanes:].astype(F32)
-        b_other = came_ref[k, :half, lanes:].astype(F32)
+        kept, come = keep_ref[k, :half].astype(F32), came_ref[k, :half].astype(F32)
+        a = own * kept[:, :lanes] + other * come[:, :lanes]
+        b_own, b_other = kept[:, lanes:], come[:, lanes:]
         a += own_shift * b_own + other_shift * b_other
         both = jnp.concatenate([a, own * b_own + other * b_other], axis=1).astype(BF16)
         first = k // near * per
@@ -369,12 +378,14 @@
     a = jnp.zeros((half, lanes), F32)
     b = jnp.zeros((half, lanes), F32)
     for k in range(count):
-        b_one = part_ref[k, :half, lanes:].astype(F32)
-        a += scale[k] * part_ref[k, :half, :lanes].astype(F32) + (scale[k] * shift[k]) * b_one
+        one = part_ref[k, :half].astype(F32)
+        b_one = one[:, lanes:]
+        a += scale[k] * one[:, :lanes] + (scale[k] * shift[k]) * b_one
         b += scale[k] * b_one
     rest = jnp.zeros((width - per - 16, lanes), F32)
     table = jnp.concatenate([in_parts(stats, lanes), rest], axis=0)
-    pick = (place_ref[...] == iota((lanes, slots), 0)).astype(F32).T.astype(BF16)
+    tall = -(-lanes // 128) * 128
+    pick = (place_ref[...] == iota((tall, slots), 0)).astype(F32).T[:, :lanes].astype(BF16)
 
     def found(value):
         pieces = []
@@ -415,12 +426,24 @@
     def source(q):
         return [f * groups + q * share + k for f in range(far) for k in range(share)]
 
-    stats = []
+    wide = part_ref.shape[2]
+
+    def moved(value, by):
+        return pltpu.roll(value, by % wide, 1)
+
+    tables = []
     for k in source(0):
         part = part_ref[k].astype(F32)[:pad]
-        column = [part[:, per + j : per + j + 1] for j in range(9)]
-        stats.append([column[j] + column[j + 1] + column[j + 2] for j in (0, 3, 6)])
-    scale, shift, (lse, mean, t_lse) = merged(stats)
+        tables.append(part + moved(part, -1) + moved(part, -2))
+    high = functools.reduce(jnp.maximum, tables)
+    weight = [jnp.exp(v - high) for v in tables]
+    total = functools.reduce(jnp.add, weight)
+    weight = [w / total for w in weight]
+    mean = functools.reduce(jnp.add, [moved(w, 3) * v for w, v in zip(weight, tables)])
+    scale = [w[:, per : per + 1] for w in weight]
+    shift = [(v - mean)[:, per + 3 : per + 4] for v in tables]
+    lse = high + jnp.log(total)
+    lse, t_lse, mean = lse[:, per : per + 1], lse[:, per + 6 : per + 7], mean[:, per + 3 : per + 4]
     pieces = []
     for q in range(near):
         grad = jnp.zeros((pad, part_ref.shape[2]), F32)
@@ -451,12 +474,12 @@
     return lax.ppermute(value, "c", ((0, 1), (1, 0)))
 
 
-def some_rows(lanes, pad, t_width, width, operands):
+def some_rows(count, lanes, pad, t_width, width, operands):
     info, rows, t_place, s_place, teacher_head, student_head = operands
-    own = exchange(pack(rows, t_place, s_place, lanes, t_width, width, lax.axis_size(Y)), Y)
+    own = exchange(pack(rows, t_place, s_place, count, t_width, width, lax.axis_size(Y)), Y)
     other = swap(own)
     t, s, *heads = first(info, own, teacher_head, student_head)
-    keep, send = second(other, t, s, *heads)
+    keep, send = second(other, t, s, *heads, lanes)
     both = pair(info, keep, swap(send), lax.axis_size("x"), lax.axis_size("yl"))
     return exchange(spread(exchange(both, NEAR), s_place, pad, lax.axis_size("yh")), REST)
 
@@ -467,12 +490,11 @@
     t_width, s_width = teacher_rows.shape[2], student_rows.shape[2]
     group = lax.axis_index(GRP).astype(jnp.int32).reshape(1)
     core = lax.axis_index("c").astype(jnp.int32).reshape(1)
-    mine, t_place, s_place, info = arrange(
-        group, core, lengths, owner, teacher_rows, student_rows, groups
-    )
+    mine = arrange(group, lengths, teacher_rows, student_rows, groups)
+    t_place, s_place, info = routing(group, core, lengths, owner, groups * pad, pad)
     rows = exchange(mine, GRP).reshape(groups * pad, mine.shape[2])
     operands = (info, rows, t_place, s_place, teacher_head, student_head)
-    branches = [functools.partial(some_rows, c, pad, t_width, t_width + s_width) for c in CAPACITIES]
+    branches = [functools.partial(some_rows, *c, pad, t_width, t_width + s_width) for c in CAPACITIES]
     parts = lax.switch(info[0], branches, operands)
     grad, divergence = finish(info, parts, s_width, lax.axis_size("yh"), lax.axis_size("x"))
     return divergence, grad

time: 178 us -> 132 us (0.74)
  blocking collectives: 127 us -> 87.4 us
  waiting for transfers between devices: 21.1 us -> 15.5 us
    all_to_all x3, blocking collectives: 127 us -> 87.4 us  [exchange(): return lax.all_to_all(pieces, axes, 0, 0, tiled=True)]
    ppermute x2, waiting for transfers between devices: 7.55 us -> 3.48 us  [swap(): return lax.ppermute(value, 'c', ((0, 1), (1, 0)))]
  transfers between devices with their start and end apart: 3 -> 3, of which waited for: 3 -> 3; matrix products, arithmetic and copies ran while one was open for 0% -> 0% of each run, Pallas kernels for 1% -> 3%
where the time goes in v7:
time: 132 us; the launch traced here: 131 us
  blocking collectives  87.4 us (66%)
  starting transfers between devices  17.1 us (13%)
  waiting for transfers between devices  15.5 us (12%)
  Pallas kernels  10.6 us (8%)
    all_to_all x3, blocking collectives, exchange(): return lax.all_to_all(pieces, axes, 0, 0, tiled=True)  87.4 us
    all_to_all x1, starting transfers between devices, exchange(): return lax.all_to_all(pieces, axes, 0, 0, tiled=True)  13.2 us
    all_to_all x1, waiting for transfers between devices, exchange(): return lax.all_to_all(pieces, axes, 0, 0, tiled=True)  12 us
    ppermute x2, starting transfers between devices, swap(): return lax.ppermute(value, 'c', ((0, 1), (1, 0)))  3.95 us
    ppermute x2, waiting for transfers between devices, swap(): return lax.ppermute(value, 'c', ((0, 1), (1, 0)))  3.48 us
  transfers between devices with their start and end apart: 3, of which 3 were waited for; matrix products, arithmetic and copies ran while one was open for 0% of the time, Pallas kernels for 3%

profile of v7, /device:TPU:8, one launch (start us, length us, event | category | flops | bytes accessed | tf_op | source)
XLA Modules:
  0.0 131.4 jit_solution(10984391367507499461)
XLA Ops:
  0.6 1.5 %shard_map.78 = bf16[32,8,640]{2,1,0:T(8,128)(2,1)} custom-call(s32[1]{0:T(128)} %bitcast.6.group_ref, s32[64]{0:T(128)} %lengths_ref.3, bf16[2,8,256]{2,1,0:T(8,128)(2,1)} %teacher_ref.1, bf16[1,8,320]{2,1,0:T(8,128)(2,1)} %student_ref.1), custom_call_target="tpu_custom_call" | custom-call | tf_op jit(solution)/shard_map/pallas_call | solution.py:51
  2.1 13.2 %all-to-all-start.9 = ((bf16[32,8,640]{2,1,0:T(8,128)(2,1)}), bf16[32,8,640]{2,1,0:T(8,128)(2,1)S(1)}, u32[]{:S(2)}, u32[]{:S(2)}) async-start(bf16[32,8,640]{2,1,0:T(8,128)(2,1)} %shard_map.78), calls=%async_computation.9 | async-start | bytes 655360 | tf_op jit(solution)/shard_map/all_to_all | solution.py:29
  15.3 1.5 %shard_map.77 = (s32[1,256]{1,0:T(1,128)S(1)}, s32[1,256]{1,0:T(1,128)S(1)}, s32[3]{0:T(128)S(1)}) custom-call(s32[1]{0:T(128)} %bitcast.6.group_ref, s32[1]{0:T(128)} %bitcast.7.core_ref, s32[64]{0:T(128)} %lengths_ref.3, s32[64]{0:T(128)} %owner_ref.1, s32[1,64]{1,0:T(1,128)} %bitcast.23, s32[1,64]{1,0:T(1,128)} %bitcast.24), custom_call_target="tpu_custom_call" | custom-call | flops 1000000 | bytes 1000000 | tf_op jit(solution)/shard_map/pallas_call | solution.py:106
  16.8 12.0 %all-to-all-done.9 = bf16[32,8,640]{2,1,0:T(8,128)(2,1)S(1)} async-done(((bf16[32,8,640]{2,1,0:T(8,128)(2,1)}), bf16[32,8,640]{2,1,0:T(8,128)(2,1)S(1)}, u32[]{:S(2)}, u32[]{:S(2)}) %all-to-all-start.9) | async-done | bytes 327712 | tf_op jit(solution)/shard_map/all_to_all | solution.py:29
  28.9 100.9 %conditional.1 = (bf16[128,16,128]{2,1,0:T(8,128)(2,1)S(1)}) conditional(s32[]{:T(128)} %bitcast.10, (bf16[256,640]{1,0:T(8,128)(2,1)S(1)}, s32[1,256]{1,0:T(1,128)S(1)}, s32[1,256]{1,0:T(1,128)S(1)}, bf16[4096,256]{1,0:T(8,128)(2,1)}, bf16[5120,256]{1,0:T(8,128)(2,1)}, /*index=5*/s32[3]{0:T(128)S(1)}) %tuple.22, ...), branch_computations={%region_0.0_spmd, %region_1.0_spmd, %region_2.0_spmd} | conditional | flops 603979776 | bytes 60031120 | solution.py:498
  28.9 0.0 copy-start
  28.9 0.3 branch_0_fun.5
  29.2 33.9 %all_to_all.41.own_ref = bf16[8,64,1152]{2,1,0:T(8,128)(2,1)S(1)} all-to-all(bf16[8,64,1152]{2,1,0:T(8,128)(2,1)S(1)} %branch_0_fun.5), channel_id=1, replica_groups=mesh['x'=4,'z'=8,'yh'=4,'yl'=2,'c'=2] {'yh','yl'}, dimensions={0} | all-to-all | bytes 2359296 | tf_op jit(solution)/shard_map/cond/branch_0_fun/all_to_all | solution.py:29
  63.1 1.9 %collective-permute-start = (bf16[8,64,1152]{2,1,0:T(8,128)(2,1)S(1)}, bf16[8,64,1152]{2,1,0:T(8,128)(2,1)S(1)}, u32[]{:S(2)}, u32[]{:S(2)}) collective-permute-start(bf16[8,64,1152]{2,1,0:T(8,128)(2,1)S(1)} %all_to_all.41.own_ref), channel_id=1, source_target_pairs={{0,1},{1,0},{2,3},{3,2},{4,5},{5,4},{6,7},{7,6},{8,9},{9,8},{10,11... | collective-permute-start | bytes 3538952 | tf_op jit(solution)/shard_map/cond/branch_0_fun/ppermute | solution.py:474
  65.0 0.0 copy-done
  65.0 2.3 %branch_0_fun.6 = (f32[128,256]{1,0:T(8,128)S(1)}, f32[128,256]{1,0:T(8,128)S(1)}, bf16[8,320,256]{2,1,0:T(8,128)(2,1)S(1)}, bf16[8,256,256]{2,1,0:T(8,128)(2,1)S(1)}, bf16[8,320,256]{2,1,0:T(8,128)(2,1)S(1)}) custom-call(s32[3]{0:T(128)S(1)} %get-tuple-element.28.info_ref, bf16[8,64,1152]{2,1,0:T(8,128)(2,1)S(1)} %all_to_all.41.own_ref, ...), custom_call_target="tpu_custom_call" | custom-call | flops 301989888 | bytes 9437184 | tf_op jit(solution)/shard_map/cond/branch_0_fun/pallas_call | solution.py:262
  67.3 0.5 collective-permute-done.other_ref
  67.8 1.5 %branch_0_fun.7 = (bf16[8,336,256]{2,1,0:T(8,128)(2,1)S(1)}, bf16[8,336,256]{2,1,0:T(8,128)(2,1)S(1)}) custom-call(bf16[8,64,1152]{2,1,0:T(8,128)(2,1)S(1)} %collective-permute-done.other_ref, f32[128,256]{1,0:T(8,128)S(1)} %get-tuple-element.46.t_ref, f32[128,256]{1,0:T(8,128)S(1)} %get-tuple-element.47.s_ref, ...), custom_call_target="tpu_custom_call" | custom-call | tf_op jit(solution)/shard_map/cond/branch_0_fun/pallas_call | solution.py:307
  69.3 2.0 %collective-permute-start.1 = (bf16[8,336,256]{2,1,0:T(8,128)(2,1)S(1)}, bf16[8,336,256]{2,1,0:T(8,128)(2,1)S(1)}, u32[]{:S(2)}, u32[]{:S(2)}) collective-permute-start(bf16[8,336,256]{2,1,0:T(8,128)(2,1)S(1)} %get-tuple-element.52), channel_id=1, source_target_pairs={{0,1},{1,0},{2,3},{3,2},{4,5},{5,4},{6,7},{7,6},{8,9},{9,8},{10,11... | collective-permute-start | bytes 4128776 | tf_op jit(solution)/shard_map/cond/branch_0_fun/ppermute | solution.py:474
  71.4 3.0 %collective-permute-done.1.came_ref = bf16[8,336,256]{2,1,0:T(8,128)(2,1)S(1)} collective-permute-done((bf16[8,336,256]{2,1,0:T(8,128)(2,1)S(1)}, bf16[8,336,256]{2,1,0:T(8,128)(2,1)S(1)}, u32[]{:S(2)}, u32[]{:S(2)}) %collective-permute-start.1) | collective-permute-done | bytes 1376288 | tf_op jit(solution)/shard_map/cond/branch_0_fun/ppermute | solution.py:474
  74.3 1.2 branch_0_fun.8
  75.6 22.9 %all_to_all.42.part_ref = bf16[8,336,256]{2,1,0:T(8,128)(2,1)S(1)} all-to-all(bf16[8,336,256]{2,1,0:T(8,128)(2,1)S(1)} %branch_0_fun.8), channel_id=1, replica_groups=mesh['x'=4,'z'=8,'yh'=4,'yl'=2,'c'=2] {'x','yl'}, dimensions={0} | all-to-all | bytes 2752512 | tf_op jit(solution)/shard_map/cond/branch_0_fun/all_to_all | solution.py:29
  98.5 0.7 branch_0_fun.9
  99.2 30.6 %all_to_all.43 = bf16[128,16,128]{2,1,0:T(8,128)(2,1)S(1)} all-to-all(bf16[128,16,128]{2,1,0:T(8,128)(2,1)S(1)} %branch_0_fun.9), channel_id=1, replica_groups=mesh['x'=4,'z'=8,'yh'=4,'yl'=2,'c'=2] {'yh','x','z'}, dimensions={0} | all-to-all | bytes 1048576 | tf_op jit(solution)/shard_map/cond/branch_0_fun/all_to_all | solution.py:29
  129.8 1.6 %shard_map.79 = (bf16[1,8,320]{2,1,0:T(8,128)(2,1)}, f32[1,8]{1,0:T(1,128)}) custom-call(s32[3]{0:T(128)S(1)} %get-tuple-element.86.info_ref, bf16[128,16,128]{2,1,0:T(8,128)(2,1)S(1)} %get-tuple-element.91.part_ref), custom_call_target="tpu_custom_call" | custom-call | tf_op jit(solution)/shard_map/pallas_call | solution.py:462
Async XLA Ops:
  2.1 26.7 %all-to-all-start.9 = ((bf16[32,8,640]{2,1,0:T(8,128)(2,1)}), bf16[32,8,640]{2,1,0:T(8,128)(2,1)S(1)}, u32[]{:S(2)}, u32[]{:S(2)}) async-start(bf16[32,8,640]{2,1,0:T(8,128)(2,1)} %shard_map.78), calls=%async_computation.9 | async-start | bytes 655360 | tf_op jit(solution)/shard_map/all_to_all | solution.py:29
  28.9 36.1 %copy-start = (bf16[5120,256]{1,0:T(8,128)(2,1)S(1)}, bf16[5120,256]{1,0:T(8,128)(2,1)}, u32[]{:S(2)}) copy-start(bf16[5120,256]{1,0:T(8,128)(2,1)} %get-tuple-element.45) | copy-start | bytes 7864324 | tf_op jit(solution)/shard_map/cond
  63.1 4.7 %collective-permute-start = (bf16[8,64,1152]{2,1,0:T(8,128)(2,1)S(1)}, bf16[8,64,1152]{2,1,0:T(8,128)(2,1)S(1)}, u32[]{:S(2)}, u32[]{:S(2)}) collective-permute-start(bf16[8,64,1152]{2,1,0:T(8,128)(2,1)S(1)} %all_to_all.41.own_ref), channel_id=1, source_target_pairs={{0,1},{1,0},{2,3},{3,2},{4,5},{5,4},{6,7},{7,6},{8,9},{9,8},{10,11... | collective-permute-start | bytes 3538952 | tf_op jit(solution)/shard_map/cond/branch_0_fun/ppermute | solution.py:474
  69.3 5.0 %collective-permute-start.1 = (bf16[8,336,256]{2,1,0:T(8,128)(2,1)S(1)}, bf16[8,336,256]{2,1,0:T(8,128)(2,1)S(1)}, u32[]{:S(2)}, u32[]{:S(2)}) collective-permute-start(bf16[8,336,256]{2,1,0:T(8,128)(2,1)S(1)} %get-tuple-element.52), channel_id=1, source_target_pairs={{0,1},{1,0},{2,3},{3,2},{4,5},{5,4},{6,7},{7,6},{8,9},{9,8},{10,11... | collective-permute-start | bytes 4128776 | tf_op jit(solution)/shard_map/cond/branch_0_fun/ppermute | solution.py:474

commit v8 on v7

--- a/solution.py
+++ b/solution.py
@@ -9,10 +9,7 @@
 from jax.sharding import PartitionSpec as P
 
 GRP = ("x", "z")
-Y = ("yh", "yl")
-VOCAB = ("yh", "yl", "c")
-NEAR = ("x", "yl")
-REST = ("yh", "x", "z")
+VOCAB = ("y", "c")
 CAPACITIES = ((128, 128), (160, 192), (256, 256))
 F32 = jnp.float32
 BF16 = jnp.bfloat16
@@ -334,7 +331,6 @@
         other * jnp.where(low, shift[1], shift[0]),
     )
     per = half // parts
-    near = out_ref.shape[0] // parts
     last = out_ref.shape[1] - 16
     for k in range(keep_ref.shape[0]):
         kept, come = keep_ref[k, :half].astype(F32), came_ref[k, :half].astype(F32)
@@ -342,89 +338,105 @@
         b_own, b_other = kept[:, lanes:], come[:, lanes:]
         a += own_shift * b_own + other_shift * b_other
         both = jnp.concatenate([a, own * b_own + other * b_other], axis=1).astype(BF16)
-        first = k // near * per
         for q in range(parts):
-            piece = both[q * per : (q + 1) * per]
-            out_ref[q * near + k % near, first : first + per] = piece
+            out_ref[q, k * per : (k + 1) * per] = both[q * per : (q + 1) * per]
     for k in range(out_ref.shape[0]):
         out_ref[k, last:] = table
 
 
-def pair(info, keep, came, parts, near):
+def pair(info, keep, came, parts):
     ring, deep, width = keep.shape
-    deep = (deep - 16) // parts * (ring // near) + 16
+    deep = (deep - 16) // parts * ring + 16
     return pl.pallas_call(
         functools.partial(pair_kernel, parts),
-        out_shape=jax.ShapeDtypeStruct((parts * near, deep, width), BF16),
+        out_shape=jax.ShapeDtypeStruct((parts, deep, width), BF16),
         in_specs=[SMEM, VMEM, VMEM],
         out_specs=VMEM,
         compiler_params=PARAMS,
     )(info, keep, came)
 
 
+def gathered(part_ref, lanes, half):
+    count = part_ref.shape[0]
+    scale, shift, stats = merged(
+        [from_parts(part_ref[k, half:].astype(F32), lanes) for k in range(count)]
+    )
+    shift = [a * b for a, b in zip(scale, shift)]
+
+    def piece(first, size):
+        a = jnp.zeros((size, lanes), F32)
+        b = jnp.zeros((size, lanes), F32)
+        for k in range(count):
+            one = part_ref[k, first : first + size].astype(F32)
+            a += scale[k] * one[:, :lanes] + shift[k] * one[:, lanes:]
+            b += scale[k] * one[:, lanes:]
+        return a, b
+
+    return piece, in_parts(stats, lanes)
+
+
+def fold_kernel(part_ref, out_ref):
+    lanes = part_ref.shape[2] // 2
+    per = out_ref.shape[1] - 16
+    piece, table = gathered(part_ref, lanes, part_ref.shape[1] - 16)
+    table = jnp.concatenate([table, table], axis=1).astype(BF16)
+    for k in range(out_ref.shape[0]):
+        out_ref[k, :per] = jnp.concatenate(piece(k * per, per), axis=1).astype(BF16)
+        out_ref[k, per:] = table
+
+
+def fold(parts, count):
+    _, deep, width = parts.shape
+    return pl.pallas_call(
+        fold_kernel,
+        out_shape=jax.ShapeDtypeStruct((count, (deep - 16) // count + 16, width), BF16),
+        in_specs=[VMEM],
+        out_specs=VMEM,
+        compiler_params=PARAMS,
+    )(parts)
+
+
 def spread_kernel(part_ref, place_ref, out_ref):
     lanes = part_ref.shape[2] // 2
     half = part_ref.shape[1] - 16
-    count = part_ref.shape[0]
+    groups, rows, width = out_ref.shape
     slots = place_ref.shape[1]
-    pad = out_ref.shape[1] // 2
-    width = out_ref.shape[2]
-    groups = slots // pad
-    far = out_ref.shape[0] // groups
-    per = half // far
-    scale, shift, stats = merged(
-        [from_parts(part_ref[k, half:].astype(F32), lanes) for k in range(count)]
-    )
-    a = jnp.zeros((half, lanes), F32)
-    b = jnp.zeros((half, lanes), F32)
-    for k in range(count):
-        one = part_ref[k, :half].astype(F32)
-        b_one = one[:, lanes:]
-        a += scale[k] * one[:, :lanes] + (scale[k] * shift[k]) * b_one
-        b += scale[k] * b_one
-    rest = jnp.zeros((width - per - 16, lanes), F32)
-    table = jnp.concatenate([in_parts(stats, lanes), rest], axis=0)
+    piece, table = gathered(part_ref, lanes, half)
+    rest = jnp.zeros((width - half - 16, lanes), F32)
     tall = -(-lanes // 128) * 128
     pick = (place_ref[...] == iota((tall, slots), 0)).astype(F32).T[:, :lanes].astype(BF16)
 
     def found(value):
-        pieces = []
-        for k in range(far):
-            pieces += [value[k * per : (k + 1) * per], table]
-        return lax.dot_general(
+        value = lax.dot_general(
             pick,
-            jnp.concatenate(pieces, axis=0).astype(BF16),
+            jnp.concatenate([value, table, rest], axis=0).astype(BF16),
             (((1,), (1,)), ((), ())),
             preferred_element_type=F32,
         )
-
-    a, b = found(a), found(b)
-    for k in range(far):
-        both = [v[:, k * width : (k + 1) * width].reshape(groups, pad, width) for v in (a, b)]
-        out_ref[k * groups : (k + 1) * groups] = jnp.concatenate(both, axis=1).astype(BF16)
-
-
-def spread(parts, place, pad, far):
-    groups = place.shape[1] // pad
-    per = (parts.shape[1] - 16) // far
-    width = -(-(per + 16) // 128) * 128
+        return value.reshape(groups, rows // 2, width)
+
+    both = [found(value) for value in piece(0, half)]
+    out_ref[...] = jnp.concatenate(both, axis=1).astype(BF16)
+
+
+def spread(parts, place, pad):
+    width = -(-parts.shape[1] // 128) * 128
     return pl.pallas_call(
         spread_kernel,
-        out_shape=jax.ShapeDtypeStruct((far * groups, 2 * pad, width), BF16),
+        out_shape=jax.ShapeDtypeStruct((place.shape[1] // pad, 2 * pad, width), BF16),
         in_specs=[VMEM, VMEM],
         out_specs=VMEM,
         compiler_params=PARAMS,
     )(parts, place)
 
 
-def finish_kernel(far, near, info_ref, part_ref, grad_ref, kl_ref):
+def finish_kernel(near, info_ref, part_ref, grad_ref, kl_ref):
     _, pad, width = grad_ref.shape
     per = width // near
-    groups = part_ref.shape[0] // far
-    share = groups // near
+    share = part_ref.shape[0] // near
 
     def source(q):
-        return [f * groups + q * share + k for f in range(far) for k in range(share)]
+        return range(q * share, (q + 1) * share)
 
     wide = part_ref.shape[2]
 
@@ -457,10 +469,10 @@
     kl_ref[...] = jnp.sum(jnp.where(square, kl, 0.0), axis=0, keepdims=True)
 
 
-def finish(info, parts, width, far, near):
+def finish(info, parts, width, near):
     pad = parts.shape[1] // 2
     return pl.pallas_call(
-        functools.partial(finish_kernel, far, near),
+        functools.partial(finish_kernel, near),
         out_shape=[
             jax.ShapeDtypeStruct((1, pad, width), BF16),
             jax.ShapeDtypeStruct((1, pad), F32),
@@ -476,12 +488,13 @@
 
 def some_rows(count, lanes, pad, t_width, width, operands):
     info, rows, t_place, s_place, teacher_head, student_head = operands
-    own = exchange(pack(rows, t_place, s_place, count, t_width, width, lax.axis_size(Y)), Y)
+    own = exchange(pack(rows, t_place, s_place, count, t_width, width, lax.axis_size("y")), "y")
     other = swap(own)
     t, s, *heads = first(info, own, teacher_head, student_head)
     keep, send = second(other, t, s, *heads, lanes)
-    both = pair(info, keep, swap(send), lax.axis_size("x"), lax.axis_size("yl"))
-    return exchange(spread(exchange(both, NEAR), s_place, pad, lax.axis_size("yh")), REST)
+    both = exchange(pair(info, keep, swap(send), lax.axis_size("x")), "x")
+    both = exchange(fold(both, lax.axis_size("y")), "y")
+    return exchange(spread(both, s_place, pad), GRP)
 
 
 def per_device(teacher_rows, student_rows, teacher_head, student_head, lengths, owner):
@@ -496,12 +509,12 @@
     operands = (info, rows, t_place, s_place, teacher_head, student_head)
     branches = [functools.partial(some_rows, *c, pad, t_width, t_width + s_width) for c in CAPACITIES]
     parts = lax.switch(info[0], branches, operands)
-    grad, divergence = finish(info, parts, s_width, lax.axis_size("yh"), lax.axis_size("x"))
+    grad, divergence = finish(info, parts, s_width, lax.axis_size("x"))
     return divergence, grad
 
 
 def solution(mesh):
-    torus = Mesh(mesh.devices.reshape(4, 8, 4, 2, 2), ("x", "z", "yh", "yl", "c"))
+    torus = Mesh(mesh.devices.reshape(4, 8, 8, 2), ("x", "z", "y", "c"))
     return jax.shard_map(
         per_device,
         mesh=torus,

time: 132 us -> 133 us (level)
  the two profiles are of different devices: /device:TPU:8 before, /device:TPU:1 now
where the time goes in v8:
time: 133 us; the launch traced here: 131 us
  blocking collectives  84.3 us (63%)
  starting transfers between devices  24.1 us (18%)
  waiting for transfers between devices  11.5 us (9%)
  Pallas kernels  10.5 us (8%)
    all_to_all x4, blocking collectives, exchange(): return lax.all_to_all(pieces, axes, 0, 0, tiled=True)  84.3 us
    all_to_all x1, starting transfers between devices, exchange(): return lax.all_to_all(pieces, axes, 0, 0, tiled=True)  13.7 us
    ppermute x2, starting transfers between devices, swap(): return lax.ppermute(value, 'c', ((0, 1), (1, 0)))  10.4 us
    all_to_all x1, waiting for transfers between devices, exchange(): return lax.all_to_all(pieces, axes, 0, 0, tiled=True)  8.64 us
    ppermute x2, waiting for transfers between devices, swap(): return lax.ppermute(value, 'c', ((0, 1), (1, 0)))  2.88 us
  transfers between devices with their start and end apart: 3, of which 3 were waited for; matrix products, arithmetic and copies ran while one was open for 0% of the time, Pallas kernels for 3%

profile of v8, /device:TPU:1, one launch (start us, length us, event | category | flops | bytes accessed | tf_op | source)
XLA Modules:
  0.0 131.2 jit_solution(12587582469455332581)
XLA Ops:
  0.6 1.5 %shard_map.78 = bf16[32,8,640]{2,1,0:T(8,128)(2,1)} custom-call(s32[1]{0:T(128)} %bitcast.6.group_ref, s32[64]{0:T(128)} %lengths_ref.3, bf16[2,8,256]{2,1,0:T(8,128)(2,1)} %teacher_ref.1, bf16[1,8,320]{2,1,0:T(8,128)(2,1)} %student_ref.1), custom_call_target="tpu_custom_call" | custom-call | tf_op jit(solution)/shard_map/pallas_call | solution.py:48
  2.1 13.7 %all-to-all-start.12 = ((bf16[32,8,640]{2,1,0:T(8,128)(2,1)}), bf16[32,8,640]{2,1,0:T(8,128)(2,1)S(1)}, u32[]{:S(2)}, u32[]{:S(2)}) async-start(bf16[32,8,640]{2,1,0:T(8,128)(2,1)} %shard_map.78), calls=%async_computation.12 | async-start | bytes 655360 | tf_op jit(solution)/shard_map/all_to_all | solution.py:26
  15.8 1.5 %shard_map.77 = (s32[1,256]{1,0:T(1,128)S(1)}, s32[1,256]{1,0:T(1,128)S(1)}, s32[3]{0:T(128)S(1)}) custom-call(s32[1]{0:T(128)} %bitcast.6.group_ref, s32[1]{0:T(128)} %bitcast.7.core_ref, s32[64]{0:T(128)} %lengths_ref.3, s32[64]{0:T(128)} %owner_ref.1, s32[1,64]{1,0:T(1,128)} %bitcast.23, s32[1,64]{1,0:T(1,128)} %bitcast.24), custom_call_target="tpu_custom_call" | custom-call | flops 1000000 | bytes 1000000 | tf_op jit(solution)/shard_map/pallas_call | solution.py:103
  17.4 8.6 %all-to-all-done.12 = bf16[32,8,640]{2,1,0:T(8,128)(2,1)S(1)} async-done(((bf16[32,8,640]{2,1,0:T(8,128)(2,1)}), bf16[32,8,640]{2,1,0:T(8,128)(2,1)S(1)}, u32[]{:S(2)}, u32[]{:S(2)}) %all-to-all-start.12) | async-done | bytes 327712 | tf_op jit(solution)/shard_map/all_to_all | solution.py:26
  26.0 103.7 %conditional.1 = (bf16[32,16,128]{2,1,0:T(8,128)(2,1)S(1)}) conditional(s32[]{:T(128)} %bitcast.10, (bf16[256,640]{1,0:T(8,128)(2,1)S(1)}, s32[1,256]{1,0:T(1,128)S(1)}, s32[1,256]{1,0:T(1,128)S(1)}, bf16[4096,256]{1,0:T(8,128)(2,1)}, bf16[5120,256]{1,0:T(8,128)(2,1)}, /*index=5*/s32[3]{0:T(128)S(1)}) %tuple.22, ...), branch_computations={%region_0.0_spmd, %region_1.0_spmd, %region_2.0_spmd} | conditional | flops 603979776 | bytes 60686480 | solution.py:511
  26.0 0.0 copy-start
  26.0 0.3 branch_0_fun.6
  26.3 33.0 %all_to_all.53.own_ref = bf16[8,64,1152]{2,1,0:T(8,128)(2,1)S(1)} all-to-all(bf16[8,64,1152]{2,1,0:T(8,128)(2,1)S(1)} %branch_0_fun.6), channel_id=1, replica_groups=mesh['x'=4,'z'=8,'y'=8,'c'=2] {'y'}, dimensions={0} | all-to-all | bytes 2359296 | tf_op jit(solution)/shard_map/cond/branch_0_fun/all_to_all | solution.py:26
  59.4 8.1 %collective-permute-start = (bf16[8,64,1152]{2,1,0:T(8,128)(2,1)S(1)}, bf16[8,64,1152]{2,1,0:T(8,128)(2,1)S(1)}, u32[]{:S(2)}, u32[]{:S(2)}) collective-permute-start(bf16[8,64,1152]{2,1,0:T(8,128)(2,1)S(1)} %all_to_all.53.own_ref), channel_id=1, source_target_pairs={{0,1},{1,0},{2,3},{3,2},{4,5},{5,4},{6,7},{7,6},{8,9},{9,8},{10,11... | collective-permute-start | bytes 3538952 | tf_op jit(solution)/shard_map/cond/branch_0_fun/ppermute | solution.py:486
  67.5 0.0 copy-done
  67.5 2.3 %branch_0_fun.7 = (f32[128,256]{1,0:T(8,128)S(1)}, f32[128,256]{1,0:T(8,128)S(1)}, bf16[8,320,256]{2,1,0:T(8,128)(2,1)S(1)}, bf16[8,256,256]{2,1,0:T(8,128)(2,1)S(1)}, bf16[8,320,256]{2,1,0:T(8,128)(2,1)S(1)}) custom-call(s32[3]{0:T(128)S(1)} %get-tuple-element.28.info_ref, bf16[8,64,1152]{2,1,0:T(8,128)(2,1)S(1)} %all_to_all.53.own_ref, ...), custom_call_target="tpu_custom_call" | custom-call | flops 301989888 | bytes 9437184 | tf_op jit(solution)/shard_map/cond/branch_0_fun/pallas_call | solution.py:259
  69.8 0.1 collective-permute-done.other_ref
  69.9 1.5 %branch_0_fun.8 = (bf16[8,336,256]{2,1,0:T(8,128)(2,1)S(1)}, bf16[8,336,256]{2,1,0:T(8,128)(2,1)S(1)}) custom-call(bf16[8,64,1152]{2,1,0:T(8,128)(2,1)S(1)} %collective-permute-done.other_ref, f32[128,256]{1,0:T(8,128)S(1)} %get-tuple-element.46.t_ref, f32[128,256]{1,0:T(8,128)S(1)} %get-tuple-element.47.s_ref, ...), custom_call_target="tpu_custom_call" | custom-call | tf_op jit(solution)/shard_map/cond/branch_0_fun/pallas_call | solution.py:304
  71.5 2.3 %collective-permute-start.1 = (bf16[8,336,256]{2,1,0:T(8,128)(2,1)S(1)}, bf16[8,336,256]{2,1,0:T(8,128)(2,1)S(1)}, u32[]{:S(2)}, u32[]{:S(2)}) collective-permute-start(bf16[8,336,256]{2,1,0:T(8,128)(2,1)S(1)} %get-tuple-element.52), channel_id=1, source_target_pairs={{0,1},{1,0},{2,3},{3,2},{4,5},{5,4},{6,7},{7,6},{8,9},{9,8},{10,11... | collective-permute-start | bytes 4128776 | tf_op jit(solution)/shard_map/cond/branch_0_fun/ppermute | solution.py:486
  73.8 2.7 %collective-permute-done.1.came_ref = bf16[8,336,256]{2,1,0:T(8,128)(2,1)S(1)} collective-permute-done((bf16[8,336,256]{2,1,0:T(8,128)(2,1)S(1)}, bf16[8,336,256]{2,1,0:T(8,128)(2,1)S(1)}, u32[]{:S(2)}, u32[]{:S(2)}) %collective-permute-start.1) | collective-permute-done | bytes 1376288 | tf_op jit(solution)/shard_map/cond/branch_0_fun/ppermute | solution.py:486
  76.5 1.2 branch_0_fun.9
  77.7 20.5 %all_to_all.54.part_ref = bf16[4,656,256]{2,1,0:T(8,128)(2,1)S(1)} all-to-all(bf16[4,656,256]{2,1,0:T(8,128)(2,1)S(1)} %branch_0_fun.9), channel_id=1, replica_groups=mesh['x'=4,'z'=8,'y'=8,'c'=2] {'x'}, dimensions={0} | all-to-all | bytes 2686976 | tf_op jit(solution)/shard_map/cond/branch_0_fun/all_to_all | solution.py:26
  98.3 0.4 branch_0_fun.10
  98.7 15.4 %all_to_all.55.part_ref = bf16[8,96,256]{2,1,0:T(8,128)(2,1)S(1)} all-to-all(bf16[8,96,256]{2,1,0:T(8,128)(2,1)S(1)} %branch_0_fun.10), channel_id=1, replica_groups=mesh['x'=4,'z'=8,'y'=8,'c'=2] {'y'}, dimensions={0} | all-to-all | bytes 786432 | tf_op jit(solution)/shard_map/cond/branch_0_fun/all_to_all | solution.py:26
  114.1 0.3 branch_0_fun.11
  114.4 15.3 %all_to_all.56 = bf16[32,16,128]{2,1,0:T(8,128)(2,1)S(1)} all-to-all(bf16[32,16,128]{2,1,0:T(8,128)(2,1)S(1)} %branch_0_fun.11), channel_id=1, replica_groups=mesh['x'=4,'z'=8,'y'=8,'c'=2] {'x','z'}, dimensions={0} | all-to-all | bytes 262144 | tf_op jit(solution)/shard_map/cond/branch_0_fun/all_to_all | solution.py:26
  129.7 1.5 %shard_map.79 = (bf16[1,8,320]{2,1,0:T(8,128)(2,1)}, f32[1,8]{1,0:T(1,128)}) custom-call(s32[3]{0:T(128)S(1)} %get-tuple-element.86.info_ref, bf16[32,16,128]{2,1,0:T(8,128)(2,1)S(1)} %get-tuple-element.91.part_ref), custom_call_target="tpu_custom_call" | custom-call | tf_op jit(solution)/shard_map/pallas_call | solution.py:474
Async XLA Ops:
  2.1 23.9 %all-to-all-start.12 = ((bf16[32,8,640]{2,1,0:T(8,128)(2,1)}), bf16[32,8,640]{2,1,0:T(8,128)(2,1)S(1)}, u32[]{:S(2)}, u32[]{:S(2)}) async-start(bf16[32,8,640]{2,1,0:T(8,128)(2,1)} %shard_map.78), calls=%async_computation.12 | async-start | bytes 655360 | tf_op jit(solution)/shard_map/all_to_all | solution.py:26
  26.0 41.5 %copy-start = (bf16[5120,256]{1,0:T(8,128)(2,1)S(1)}, bf16[5120,256]{1,0:T(8,128)(2,1)}, u32[]{:S(2)}) copy-start(bf16[5120,256]{1,0:T(8,128)(2,1)} %get-tuple-element.45) | copy-start | bytes 7864324 | tf_op jit(solution)/shard_map/cond
  59.4 10.6 %collective-permute-start = (bf16[8,64,1152]{2,1,0:T(8,128)(2,1)S(1)}, bf16[8,64,1152]{2,1,0:T(8,128)(2,1)S(1)}, u32[]{:S(2)}, u32[]{:S(2)}) collective-permute-start(bf16[8,64,1152]{2,1,0:T(8,128)(2,1)S(1)} %all_to_all.53.own_ref), channel_id=1, source_target_pairs={{0,1},{1,0},{2,3},{3,2},{4,5},{5,4},{6,7},{7,6},{8,9},{9,8},{10,11... | collective-permute-start | bytes 3538952 | tf_op jit(solution)/shard_map/cond/branch_0_fun/ppermute | solution.py:486
  71.5 5.0 %collective-permute-start.1 = (bf16[8,336,256]{2,1,0:T(8,128)(2,1)S(1)}, bf16[8,336,256]{2,1,0:T(8,128)(2,1)S(1)}, u32[]{:S(2)}, u32[]{:S(2)}) collective-permute-start(bf16[8,336,256]{2,1,0:T(8,128)(2,1)S(1)} %get-tuple-element.52), channel_id=1, source_target_pairs={{0,1},{1,0},{2,3},{3,2},{4,5},{5,4},{6,7},{7,6},{8,9},{9,8},{10,11... | collective-permute-start | bytes 4128776 | tf_op jit(solution)/shard_map/cond/branch_0_fun/ppermute | solution.py:486

commit v9 on v7

--- a/solution.py
+++ b/solution.py
@@ -278,11 +278,9 @@
     )(info, own, t_head, s_head)
 
 
-def second_kernel(
-    other_ref, t_ref, s_ref, s_own_ref, t_other_ref, s_other_ref, keep_ref, send_ref, g_ref, stat_ref
-):
+def second_kernel(other_ref, t_ref, s_ref, t_other_ref, s_other_ref, out_ref):
     t, s = product(other_ref, t_other_ref, s_other_ref, t_ref[...], s_ref[...])
-    count, lanes = t.shape[0], g_ref.shape[1] // 2
+    count, lanes = t.shape[0], out_ref.shape[1] // 2
 
     def turned(value):
         rest = -count % 128
@@ -290,76 +288,65 @@
             value = jnp.concatenate([value, jnp.zeros((rest, value.shape[1]), F32)], axis=0)
         return value.T[:, :lanes]
 
-    soften(turned(t), turned(s), g_ref, stat_ref)
-    half = s_own_ref.shape[1]
-    for k in range(keep_ref.shape[0]):
-        for head_ref, out_ref in ((s_own_ref, keep_ref), (s_other_ref, send_ref)):
-            out_ref[k, :half] = jnp.dot(
-                head_ref[k], g_ref[...], preferred_element_type=F32
-            ).astype(BF16)
-            out_ref[k, half:] = stat_ref[...]
-
-
-def second(other, t, s, s_own, t_other, s_other, lanes):
     vocab = t.shape[1]
-    count, half, _ = s_own.shape
-    part = jax.ShapeDtypeStruct((count, half + 16, 2 * lanes), BF16)
+    soften(turned(t), turned(s), out_ref.at[:vocab], out_ref.at[vocab:])
+
+
+def second(other, t, s, t_other, s_other, lanes):
     return pl.pallas_call(
         second_kernel,
-        out_shape=[part, part],
-        in_specs=[VMEM] * 6,
-        out_specs=[VMEM] * 2,
-        scratch_shapes=[
-            pltpu.VMEM((vocab, 2 * lanes), BF16),
-            pltpu.VMEM((16, 2 * lanes), BF16),
-        ],
+        out_shape=jax.ShapeDtypeStruct((t.shape[1] + 16, 2 * lanes), BF16),
+        in_specs=[VMEM] * 5,
+        out_specs=VMEM,
         compiler_params=PARAMS,
-    )(other, t, s, s_own, t_other, s_other)
-
-
-def pair_kernel(parts, info_ref, keep_ref, came_ref, out_ref):
-    lanes = out_ref.shape[2] // 2
-    half = keep_ref.shape[1] - 16
-    low = info_ref[1] == 0
-    kept = keep_ref[0, half:].astype(F32)
-    come = came_ref[0, half:].astype(F32)
-    first = jnp.where(low, kept, come)
-    second = jnp.where(low, come, kept)
+    )(other, t, s, t_other, s_other)
+
+
+def third_kernel(parts, info_ref, own_ref, came_ref, s_own_ref, cross_ref, out_ref):
+    lanes = own_ref.shape[1] // 2
+    vocab = own_ref.shape[0] - 16
+    core = info_ref[1]
+    low = core == 0
+    own = own_ref[...].astype(F32)
+    came = came_ref[...].astype(F32)
+    first = jnp.where(low, own[vocab:], came[vocab:])
+    second = jnp.where(low, came[vocab:], own[vocab:])
     scale, shift, stats = merged([from_parts(first, lanes), from_parts(second, lanes)])
-    table = in_parts(stats, lanes)
-    table = jnp.concatenate([table, table], axis=1).astype(BF16)
-    own, other = (jnp.where(low, scale[0], scale[1]), jnp.where(low, scale[1], scale[0]))
-    own_shift, other_shift = (
-        own * jnp.where(low, shift[0], shift[1]),
-        other * jnp.where(low, shift[1], shift[0]),
-    )
+
+    def scaled(value, k):
+        a = jnp.where(low, scale[k], scale[1 - k])
+        d = a * jnp.where(low, shift[k], shift[1 - k])
+        top, plain = value[:vocab, :lanes], value[:vocab, lanes:]
+        return jnp.concatenate([a * top + d * plain, a * plain], axis=1).astype(BF16)
+
+    g = jnp.concatenate([scaled(own, 0), scaled(came, 1)], axis=0)
+    ring, half, _ = s_own_ref.shape
     per = half // parts
     near = out_ref.shape[0] // parts
     last = out_ref.shape[1] - 16
-    for k in range(keep_ref.shape[0]):
-        kept, come = keep_ref[k, :half].astype(F32), came_ref[k, :half].astype(F32)
-        a = own * kept[:, :lanes] + other * come[:, :lanes]
-        b_own, b_other = kept[:, lanes:], come[:, lanes:]
-        a += own_shift * b_own + other_shift * b_other
-        both = jnp.concatenate([a, own * b_own + other * b_other], axis=1).astype(BF16)
-        first = k // near * per
+    for k in range(ring):
+        head = jnp.concatenate([s_own_ref[k], cross_ref[k, core]], axis=1)
+        both = jnp.dot(head, g, preferred_element_type=F32).astype(BF16)
+        start = k // near * per
         for q in range(parts):
             piece = both[q * per : (q + 1) * per]
-            out_ref[q * near + k % near, first : first + per] = piece
+            out_ref[q * near + k % near, start : start + per] = piece
+    table = in_parts(stats, lanes)
+    table = jnp.concatenate([table, table], axis=1).astype(BF16)
     for k in range(out_ref.shape[0]):
         out_ref[k, last:] = table
 
 
-def pair(info, keep, came, parts, near):
-    ring, deep, width = keep.shape
-    deep = (deep - 16) // parts * (ring // near) + 16
-    return pl.pallas_call(
-        functools.partial(pair_kernel, parts),
-        out_shape=jax.ShapeDtypeStruct((parts * near, deep, width), BF16),
-        in_specs=[SMEM, VMEM, VMEM],
+def third(info, own, came, s_own, cross, parts, near):
+    ring, half, _ = s_own.shape
+    deep = half // parts * (ring // near) + 16
+    return pl.pallas_call(
+        functools.partial(third_kernel, parts),
+        out_shape=jax.ShapeDtypeStruct((parts * near, deep, own.shape[1]), BF16),
+        in_specs=[SMEM] + [VMEM] * 4,
         out_specs=VMEM,
         compiler_params=PARAMS,
-    )(info, keep, came)
+    )(info, own, came, s_own, cross.reshape(ring, 2, half, -1))
 
 
 def spread_kernel(part_ref, place_ref, out_ref):
@@ -475,12 +462,12 @@
 
 
 def some_rows(count, lanes, pad, t_width, width, operands):
-    info, rows, t_place, s_place, teacher_head, student_head = operands
+    info, rows, t_place, s_place, teacher_head, student_head, cross = operands
     own = exchange(pack(rows, t_place, s_place, count, t_width, width, lax.axis_size(Y)), Y)
     other = swap(own)
-    t, s, *heads = first(info, own, teacher_head, student_head)
-    keep, send = second(other, t, s, *heads, lanes)
-    both = pair(info, keep, swap(send), lax.axis_size("x"), lax.axis_size("yl"))
+    t, s, s_own, t_other, s_other = first(info, own, teacher_head, student_head)
+    g = second(other, t, s, t_other, s_other, lanes)
+    both = third(info, g, swap(g), s_own, cross, lax.axis_size("x"), lax.axis_size("yl"))
     return exchange(spread(exchange(both, NEAR), s_place, pad, lax.axis_size("yh")), REST)
 
 
@@ -492,8 +479,10 @@
     core = lax.axis_index("c").astype(jnp.int32).reshape(1)
     mine = arrange(group, lengths, teacher_rows, student_rows, groups)
     t_place, s_place, info = routing(group, core, lengths, owner, groups * pad, pad)
+    mine, outgoing = lax.optimization_barrier((mine, student_head))
+    cross = swap(outgoing)
     rows = exchange(mine, GRP).reshape(groups * pad, mine.shape[2])
-    operands = (info, rows, t_place, s_place, teacher_head, student_head)
+    operands = (info, rows, t_place, s_place, teacher_head, student_head, cross)
     branches = [functools.partial(some_rows, *c, pad, t_width, t_width + s_width) for c in CAPACITIES]
     parts = lax.switch(info[0], branches, operands)
     grad, divergence = finish(info, parts, s_width, lax.axis_size("yh"), lax.axis_size("x"))

time: 132 us -> 133 us (level)
  starting transfers between devices: 17.1 us -> 19.2 us
  waiting for transfers between devices: 15.5 us -> 13.6 us
  blocking collectives: 87.4 us -> 88.9 us
    ppermute x2 -> x3, starting transfers between devices: 3.95 us -> 5.99 us  [swap(): return lax.ppermute(value, 'c', ((0, 1), (1, 0)))]
    ppermute x2 -> x3, waiting for transfers between devices: 3.48 us -> 1.71 us  [swap(): return lax.ppermute(value, 'c', ((0, 1), (1, 0)))]
    all_to_all x3, blocking collectives: 87.4 us -> 88.9 us  [exchange(): return lax.all_to_all(pieces, axes, 0, 0, tiled=True)]
  transfers between devices with their start and end apart: 3 -> 4, of which waited for: 3 -> 3; matrix products, arithmetic and copies ran while one was open for 0% -> 0% of each run, Pallas kernels for 3% -> 3%
where the time goes in v9:
time: 133 us
  blocking collectives  88.9 us (67%)
  starting transfers between devices  19.2 us (14%)
  waiting for transfers between devices  13.6 us (10%)
  Pallas kernels  10 us (8%)
    all_to_all x3, blocking collectives, exchange(): return lax.all_to_all(pieces, axes, 0, 0, tiled=True)  88.9 us
    all_to_all x1, starting transfers between devices, exchange(): return lax.all_to_all(pieces, axes, 0, 0, tiled=True)  13.2 us
    all_to_all x1, waiting for transfers between devices, exchange(): return lax.all_to_all(pieces, axes, 0, 0, tiled=True)  11.9 us
    ppermute x3, starting transfers between devices, swap(): return lax.ppermute(value, 'c', ((0, 1), (1, 0)))  5.99 us
  transfers between devices with their start and end apart: 4, of which 3 were waited for; matrix products, arithmetic and copies ran while one was open for 0% of the time, Pallas kernels for 3%

profile of v9, /device:TPU:8, one launch (start us, length us, event | category | flops | bytes accessed | tf_op | source)
XLA Modules:
  0.0 132.5 jit_solution(16332121897363898271)
XLA Ops:
  0.6 1.5 %shard_map.78 = bf16[32,8,640]{2,1,0:T(8,128)(2,1)} custom-call(s32[1]{0:T(128)} %bitcast.9.group_ref, s32[64]{0:T(128)} %lengths_ref.3, bf16[2,8,256]{2,1,0:T(8,128)(2,1)} %teacher_ref.1, bf16[1,8,320]{2,1,0:T(8,128)(2,1)} %student_ref.1), custom_call_target="tpu_custom_call" | custom-call | tf_op jit(solution)/shard_map/pallas_call | solution.py:51
  2.1 1.9 %collective-permute-start.6 = (bf16[5120,256]{1,0:T(8,128)(2,1)}, bf16[5120,256]{1,0:T(8,128)(2,1)}, u32[]{:S(2)}, u32[]{:S(2)}) collective-permute-start(bf16[5120,256]{1,0:T(8,128)(2,1)} %param.12), channel_id=1, source_target_pairs={{0,1},{1,0},{2,3},{3,2},{4,5},{5,4},{6,7},{7,6},{8,9},{9,8},{10,11... | collective-permute-start | bytes 7864328 | tf_op jit(solution)/shard_map/ppermute | solution.py:461
  4.1 13.2 %all-to-all-start.9 = ((bf16[32,8,640]{2,1,0:T(8,128)(2,1)}), bf16[32,8,640]{2,1,0:T(8,128)(2,1)S(1)}, u32[]{:S(2)}, u32[]{:S(2)}) async-start(bf16[32,8,640]{2,1,0:T(8,128)(2,1)} %shard_map.78), calls=%async_computation.9 | async-start | bytes 655360 | tf_op jit(solution)/shard_map/all_to_all | solution.py:29
  17.2 1.5 %shard_map.77 = (s32[1,256]{1,0:T(1,128)S(1)}, s32[1,256]{1,0:T(1,128)S(1)}, s32[3]{0:T(128)S(1)}) custom-call(s32[1]{0:T(128)} %bitcast.9.group_ref, s32[1]{0:T(128)} %bitcast.10.core_ref, s32[64]{0:T(128)} %lengths_ref.3, s32[64]{0:T(128)} %owner_ref.1, s32[1,64]{1,0:T(1,128)} %bitcast.29, s32[1,64]{1,0:T(1,128)} %bitcast.30), custom_call_target="tpu_custom_call" | custom-call | flops 1000000 | bytes 1000000 | tf_op jit(solution)/shard_map/pallas_call | solution.py:106
  18.8 11.9 %all-to-all-done.9 = bf16[32,8,640]{2,1,0:T(8,128)(2,1)S(1)} async-done(((bf16[32,8,640]{2,1,0:T(8,128)(2,1)}), bf16[32,8,640]{2,1,0:T(8,128)(2,1)S(1)}, u32[]{:S(2)}, u32[]{:S(2)}) %all-to-all-start.9) | async-done | bytes 327712 | tf_op jit(solution)/shard_map/all_to_all | solution.py:29
  30.7 0.0 collective-permute-done.6
  30.7 100.2 %conditional.1 = (bf16[128,16,128]{2,1,0:T(8,128)(2,1)S(1)}) conditional(s32[]{:T(128)} %bitcast.13, (bf16[256,640]{1,0:T(8,128)(2,1)S(1)}, s32[1,256]{1,0:T(1,128)S(1)}, s32[1,256]{1,0:T(1,128)S(1)}, bf16[4096,256]{1,0:T(8,128)(2,1)}, bf16[5120,256]{1,0:T(8,128)(2,1)}, /*index=5*/s32[3]{0:T(128)S(1)}, ...), branch_computations={%region_0.0_spmd, %region_1.0_spmd, %region_2.0_spmd} | conditional | flops 603979776 | bytes 60620972 | solution.py:487
  30.7 0.0 copy-start
  30.7 0.3 branch_0_fun.5
  31.0 35.8 %all_to_all.41.own_ref = bf16[8,64,1152]{2,1,0:T(8,128)(2,1)S(1)} all-to-all(bf16[8,64,1152]{2,1,0:T(8,128)(2,1)S(1)} %branch_0_fun.5), channel_id=1, replica_groups=mesh['x'=4,'z'=8,'yh'=4,'yl'=2,'c'=2] {'yh','yl'}, dimensions={0} | all-to-all | bytes 2359296 | tf_op jit(solution)/shard_map/cond/branch_0_fun/all_to_all | solution.py:29
  66.8 1.9 %collective-permute-start = (bf16[8,64,1152]{2,1,0:T(8,128)(2,1)S(1)}, bf16[8,64,1152]{2,1,0:T(8,128)(2,1)S(1)}, u32[]{:S(2)}, u32[]{:S(2)}) collective-permute-start(bf16[8,64,1152]{2,1,0:T(8,128)(2,1)S(1)} %all_to_all.41.own_ref), channel_id=1, source_target_pairs={{0,1},{1,0},{2,3},{3,2},{4,5},{5,4},{6,7},{7,6},{8,9},{9,8},{10,11... | collective-permute-start | bytes 3538952 | tf_op jit(solution)/shard_map/cond/branch_0_fun/ppermute | solution.py:461
  68.7 0.0 copy-done
  68.7 2.3 %branch_0_fun.6 = (f32[128,256]{1,0:T(8,128)S(1)}, f32[128,256]{1,0:T(8,128)S(1)}, bf16[8,320,256]{2,1,0:T(8,128)(2,1)S(1)}, bf16[8,256,256]{2,1,0:T(8,128)(2,1)S(1)}, bf16[8,320,256]{2,1,0:T(8,128)(2,1)S(1)}) custom-call(s32[3]{0:T(128)S(1)} %get-tuple-element.33.info_ref, bf16[8,64,1152]{2,1,0:T(8,128)(2,1)S(1)} %all_to_all.41.own_ref, ...), custom_call_target="tpu_custom_call" | custom-call | flops 301989888 | bytes 9437184 | tf_op jit(solution)/shard_map/cond/branch_0_fun/pallas_call | solution.py:262
  71.0 0.5 collective-permute-done.other_ref
  71.5 0.0 copy-start.3
  71.5 0.7 branch_0_fun.7.own_ref
  72.2 2.2 %collective-permute-start.1 = (bf16[272,256]{1,0:T(8,128)(2,1)S(1)}, bf16[272,256]{1,0:T(8,128)(2,1)S(1)}, u32[]{:S(2)}, u32[]{:S(2)}) collective-permute-start(bf16[272,256]{1,0:T(8,128)(2,1)S(1)} %branch_0_fun.7.own_ref), channel_id=1, source_target_pairs={{0,1},{1,0},{2,3},{3,2},{4,5},{5,4},{6,7},{7,6},{8,9},{9,8},{10,11... | collective-permute-start | bytes 417800 | tf_op jit(solution)/shard_map/cond/branch_0_fun/ppermute | solution.py:461
  74.4 1.2 collective-permute-done.1.came_ref
  75.6 0.0 copy-done.3
  75.6 1.4 %branch_0_fun.8 = bf16[8,336,256]{2,1,0:T(8,128)(2,1)S(1)} custom-call(s32[3]{0:T(128)S(1)} %get-tuple-element.33.info_ref, bf16[272,256]{1,0:T(8,128)(2,1)S(1)} %branch_0_fun.7.own_ref, bf16[272,256]{1,0:T(8,128)(2,1)S(1)} %collective-permute-done.1.came_ref, bf16[8,320,256]{2,1,0:T(8,128)(2,1)S(1)} %get-tuple-element.56.s_own_ref, ...), custom_call_target="tpu_custom_call" | custom-call | tf_op jit(solution)/shard_map/cond/branch_0_fun/pallas_call | solution.py:343
  77.1 23.3 %all_to_all.42.part_ref = bf16[8,336,256]{2,1,0:T(8,128)(2,1)S(1)} all-to-all(bf16[8,336,256]{2,1,0:T(8,128)(2,1)S(1)} %branch_0_fun.8), channel_id=1, replica_groups=mesh['x'=4,'z'=8,'yh'=4,'yl'=2,'c'=2] {'x','yl'}, dimensions={0} | all-to-all | bytes 2752512 | tf_op jit(solution)/shard_map/cond/branch_0_fun/all_to_all | solution.py:29
  100.4 0.7 branch_0_fun.9
  101.0 29.9 %all_to_all.43 = bf16[128,16,128]{2,1,0:T(8,128)(2,1)S(1)} all-to-all(bf16[128,16,128]{2,1,0:T(8,128)(2,1)S(1)} %branch_0_fun.9), channel_id=1, replica_groups=mesh['x'=4,'z'=8,'yh'=4,'yl'=2,'c'=2] {'yh','x','z'}, dimensions={0} | all-to-all | bytes 1048576 | tf_op jit(solution)/shard_map/cond/branch_0_fun/all_to_all | solution.py:29
  130.9 1.6 %shard_map.79 = (bf16[1,8,320]{2,1,0:T(8,128)(2,1)}, f32[1,8]{1,0:T(1,128)}) custom-call(s32[3]{0:T(128)S(1)} %get-tuple-element.91.info_ref, bf16[128,16,128]{2,1,0:T(8,128)(2,1)S(1)} %get-tuple-element.98.part_ref), custom_call_target="tpu_custom_call" | custom-call | tf_op jit(solution)/shard_map/pallas_call | solution.py:449
Async XLA Ops:
  2.1 28.6 %collective-permute-start.6 = (bf16[5120,256]{1,0:T(8,128)(2,1)}, bf16[5120,256]{1,0:T(8,128)(2,1)}, u32[]{:S(2)}, u32[]{:S(2)}) collective-permute-start(bf16[5120,256]{1,0:T(8,128)(2,1)} %param.12), channel_id=1, source_target_pairs={{0,1},{1,0},{2,3},{3,2},{4,5},{5,4},{6,7},{7,6},{8,9},{9,8},{10,11... | collective-permute-start | bytes 7864328 | tf_op jit(solution)/shard_map/ppermute | solution.py:461
  4.1 26.7 %all-to-all-start.9 = ((bf16[32,8,640]{2,1,0:T(8,128)(2,1)}), bf16[32,8,640]{2,1,0:T(8,128)(2,1)S(1)}, u32[]{:S(2)}, u32[]{:S(2)}) async-start(bf16[32,8,640]{2,1,0:T(8,128)(2,1)} %shard_map.78), calls=%async_computation.9 | async-start | bytes 655360 | tf_op jit(solution)/shard_map/all_to_all | solution.py:29
  30.7 38.0 %copy-start = (bf16[5120,256]{1,0:T(8,128)(2,1)S(1)}, bf16[5120,256]{1,0:T(8,128)(2,1)}, u32[]{:S(2)}) copy-start(bf16[5120,256]{1,0:T(8,128)(2,1)} %get-tuple-element.51) | copy-start | bytes 7864324 | tf_op jit(solution)/shard_map/cond
  66.8 4.7 %collective-permute-start = (bf16[8,64,1152]{2,1,0:T(8,128)(2,1)S(1)}, bf16[8,64,1152]{2,1,0:T(8,128)(2,1)S(1)}, u32[]{:S(2)}, u32[]{:S(2)}) collective-permute-start(bf16[8,64,1152]{2,1,0:T(8,128)(2,1)S(1)} %all_to_all.41.own_ref), channel_id=1, source_target_pairs={{0,1},{1,0},{2,3},{3,2},{4,5},{5,4},{6,7},{7,6},{8,9},{9,8},{10,11... | collective-permute-start | bytes 3538952 | tf_op jit(solution)/shard_map/cond/branch_0_fun/ppermute | solution.py:461
  71.5 4.1 %copy-start.3 = (bf16[5120,256]{1,0:T(8,128)(2,1)S(1)}, bf16[5120,256]{1,0:T(8,128)(2,1)}, u32[]{:S(2)}) copy-start(bf16[5120,256]{1,0:T(8,128)(2,1)} %get-tuple-element.57) | copy-start | bytes 7864324 | tf_op jit(solution)/shard_map/cond
  72.2 3.4 %collective-permute-start.1 = (bf16[272,256]{1,0:T(8,128)(2,1)S(1)}, bf16[272,256]{1,0:T(8,128)(2,1)S(1)}, u32[]{:S(2)}, u32[]{:S(2)}) collective-permute-start(bf16[272,256]{1,0:T(8,128)(2,1)S(1)} %branch_0_fun.7.own_ref), channel_id=1, source_target_pairs={{0,1},{1,0},{2,3},{3,2},{4,5},{5,4},{6,7},{7,6},{8,9},{9,8},{10,11... | collective-permute-start | bytes 417800 | tf_op jit(solution)/shard_map/cond/branch_0_fun/ppermute | solution.py:461

commit v10 on v9

--- a/solution.py
+++ b/solution.py
@@ -479,8 +479,7 @@
     core = lax.axis_index("c").astype(jnp.int32).reshape(1)
     mine = arrange(group, lengths, teacher_rows, student_rows, groups)
     t_place, s_place, info = routing(group, core, lengths, owner, groups * pad, pad)
-    mine, outgoing = lax.optimization_barrier((mine, student_head))
-    cross = swap(outgoing)
+    cross = swap(student_head)
     rows = exchange(mine, GRP).reshape(groups * pad, mine.shape[2])
     operands = (info, rows, t_place, s_place, teacher_head, student_head, cross)
     branches = [functools.partial(some_rows, *c, pad, t_width, t_width + s_width) for c in CAPACITIES]

time: 133 us -> 133 us (level)
  transfers between devices with their start and end apart: 4 -> 4, of which waited for: 3 -> 3; matrix products, arithmetic and copies ran while one was open for 0% -> 0% of each run, Pallas kernels for 3% -> 4%
where the time goes in v10:
time: 133 us
  blocking collectives  88.9 us (67%)
  starting transfers between devices  19.2 us (14%)
  waiting for transfers between devices  13.6 us (10%)
  Pallas kernels  10 us (8%)
    all_to_all x3, blocking collectives, exchange(): return lax.all_to_all(pieces, axes, 0, 0, tiled=True)  88.9 us
    all_to_all x1, starting transfers between devices, exchange(): return lax.all_to_all(pieces, axes, 0, 0, tiled=True)  13.2 us
    all_to_all x1, waiting for transfers between devices, exchange(): return lax.all_to_all(pieces, axes, 0, 0, tiled=True)  11.9 us
    ppermute x3, starting transfers between devices, swap(): return lax.ppermute(value, 'c', ((0, 1), (1, 0)))  6.01 us
  transfers between devices with their start and end apart: 4, of which 3 were waited for; matrix products, arithmetic and copies ran while one was open for 0% of the time, Pallas kernels for 4%

profile of v10, /device:TPU:8, one launch (start us, length us, event | category | flops | bytes accessed | tf_op | source)
XLA Modules:
  0.0 132.5 jit_solution(12749683788205848298)
XLA Ops:
  0.6 1.9 %collective-permute-start.6 = (bf16[5120,256]{1,0:T(8,128)(2,1)}, bf16[5120,256]{1,0:T(8,128)(2,1)}, u32[]{:S(2)}, u32[]{:S(2)}) collective-permute-start(bf16[5120,256]{1,0:T(8,128)(2,1)} %param.12), channel_id=1, source_target_pairs={{0,1},{1,0},{2,3},{3,2},{4,5},{5,4},{6,7},{7,6},{8,9},{9,8},{10,11... | collective-permute-start | bytes 7864328 | tf_op jit(solution)/shard_map/ppermute | solution.py:461
  2.6 1.5 %shard_map.78 = bf16[32,8,640]{2,1,0:T(8,128)(2,1)} custom-call(s32[1]{0:T(128)} %bitcast.9.group_ref, s32[64]{0:T(128)} %lengths_ref.3, bf16[2,8,256]{2,1,0:T(8,128)(2,1)} %teacher_ref.1, bf16[1,8,320]{2,1,0:T(8,128)(2,1)} %student_ref.1), custom_call_target="tpu_custom_call" | custom-call | tf_op jit(solution)/shard_map/pallas_call | solution.py:51
  4.1 13.2 %all-to-all-start.9 = ((bf16[32,8,640]{2,1,0:T(8,128)(2,1)}), bf16[32,8,640]{2,1,0:T(8,128)(2,1)S(1)}, u32[]{:S(2)}, u32[]{:S(2)}) async-start(bf16[32,8,640]{2,1,0:T(8,128)(2,1)} %shard_map.78), calls=%async_computation.9 | async-start | bytes 655360 | tf_op jit(solution)/shard_map/all_to_all | solution.py:29
  17.2 1.5 %shard_map.77 = (s32[1,256]{1,0:T(1,128)S(1)}, s32[1,256]{1,0:T(1,128)S(1)}, s32[3]{0:T(128)S(1)}) custom-call(s32[1]{0:T(128)} %bitcast.9.group_ref, s32[1]{0:T(128)} %bitcast.10.core_ref, s32[64]{0:T(128)} %lengths_ref.3, s32[64]{0:T(128)} %owner_ref.1, s32[1,64]{1,0:T(1,128)} %bitcast.29, s32[1,64]{1,0:T(1,128)} %bitcast.30), custom_call_target="tpu_custom_call" | custom-call | flops 1000000 | bytes 1000000 | tf_op jit(solution)/shard_map/pallas_call | solution.py:106
  18.8 11.9 %all-to-all-done.9 = bf16[32,8,640]{2,1,0:T(8,128)(2,1)S(1)} async-done(((bf16[32,8,640]{2,1,0:T(8,128)(2,1)}), bf16[32,8,640]{2,1,0:T(8,128)(2,1)S(1)}, u32[]{:S(2)}, u32[]{:S(2)}) %all-to-all-start.9) | async-done | bytes 327712 | tf_op jit(solution)/shard_map/all_to_all | solution.py:29
  30.7 0.0 collective-permute-done.6
  30.7 100.2 %conditional.1 = (bf16[128,16,128]{2,1,0:T(8,128)(2,1)S(1)}) conditional(s32[]{:T(128)} %bitcast.13, (bf16[256,640]{1,0:T(8,128)(2,1)S(1)}, s32[1,256]{1,0:T(1,128)S(1)}, s32[1,256]{1,0:T(1,128)S(1)}, bf16[4096,256]{1,0:T(8,128)(2,1)}, bf16[5120,256]{1,0:T(8,128)(2,1)}, /*index=5*/s32[3]{0:T(128)S(1)}, ...), branch_computations={%region_0.0_spmd, %region_1.0_spmd, %region_2.0_spmd} | conditional | flops 603979776 | bytes 60620972 | solution.py:486
  30.7 0.0 copy-start
  30.7 0.3 branch_0_fun.5
  31.0 35.8 %all_to_all.41.own_ref = bf16[8,64,1152]{2,1,0:T(8,128)(2,1)S(1)} all-to-all(bf16[8,64,1152]{2,1,0:T(8,128)(2,1)S(1)} %branch_0_fun.5), channel_id=1, replica_groups=mesh['x'=4,'z'=8,'yh'=4,'yl'=2,'c'=2] {'yh','yl'}, dimensions={0} | all-to-all | bytes 2359296 | tf_op jit(solution)/shard_map/cond/branch_0_fun/all_to_all | solution.py:29
  66.8 1.9 %collective-permute-start = (bf16[8,64,1152]{2,1,0:T(8,128)(2,1)S(1)}, bf16[8,64,1152]{2,1,0:T(8,128)(2,1)S(1)}, u32[]{:S(2)}, u32[]{:S(2)}) collective-permute-start(bf16[8,64,1152]{2,1,0:T(8,128)(2,1)S(1)} %all_to_all.41.own_ref), channel_id=1, source_target_pairs={{0,1},{1,0},{2,3},{3,2},{4,5},{5,4},{6,7},{7,6},{8,9},{9,8},{10,11... | collective-permute-start | bytes 3538952 | tf_op jit(solution)/shard_map/cond/branch_0_fun/ppermute | solution.py:461
  68.7 0.0 copy-done
  68.7 2.3 %branch_0_fun.6 = (f32[128,256]{1,0:T(8,128)S(1)}, f32[128,256]{1,0:T(8,128)S(1)}, bf16[8,320,256]{2,1,0:T(8,128)(2,1)S(1)}, bf16[8,256,256]{2,1,0:T(8,128)(2,1)S(1)}, bf16[8,320,256]{2,1,0:T(8,128)(2,1)S(1)}) custom-call(s32[3]{0:T(128)S(1)} %get-tuple-element.33.info_ref, bf16[8,64,1152]{2,1,0:T(8,128)(2,1)S(1)} %all_to_all.41.own_ref, ...), custom_call_target="tpu_custom_call" | custom-call | flops 301989888 | bytes 9437184 | tf_op jit(solution)/shard_map/cond/branch_0_fun/pallas_call | solution.py:262
  71.0 0.5 collective-permute-done.other_ref
  71.5 0.0 copy-start.3
  71.5 0.7 branch_0_fun.7.own_ref
  72.2 2.2 %collective-permute-start.1 = (bf16[272,256]{1,0:T(8,128)(2,1)S(1)}, bf16[272,256]{1,0:T(8,128)(2,1)S(1)}, u32[]{:S(2)}, u32[]{:S(2)}) collective-permute-start(bf16[272,256]{1,0:T(8,128)(2,1)S(1)} %branch_0_fun.7.own_ref), channel_id=1, source_target_pairs={{0,1},{1,0},{2,3},{3,2},{4,5},{5,4},{6,7},{7,6},{8,9},{9,8},{10,11... | collective-permute-start | bytes 417800 | tf_op jit(solution)/shard_map/cond/branch_0_fun/ppermute | solution.py:461
  74.4 1.2 collective-permute-done.1.came_ref
  75.6 0.0 copy-done.3
  75.6 1.4 %branch_0_fun.8 = bf16[8,336,256]{2,1,0:T(8,128)(2,1)S(1)} custom-call(s32[3]{0:T(128)S(1)} %get-tuple-element.33.info_ref, bf16[272,256]{1,0:T(8,128)(2,1)S(1)} %branch_0_fun.7.own_ref, bf16[272,256]{1,0:T(8,128)(2,1)S(1)} %collective-permute-done.1.came_ref, bf16[8,320,256]{2,1,0:T(8,128)(2,1)S(1)} %get-tuple-element.56.s_own_ref, ...), custom_call_target="tpu_custom_call" | custom-call | tf_op jit(solution)/shard_map/cond/branch_0_fun/pallas_call | solution.py:343
  77.1 23.3 %all_to_all.42.part_ref = bf16[8,336,256]{2,1,0:T(8,128)(2,1)S(1)} all-to-all(bf16[8,336,256]{2,1,0:T(8,128)(2,1)S(1)} %branch_0_fun.8), channel_id=1, replica_groups=mesh['x'=4,'z'=8,'yh'=4,'yl'=2,'c'=2] {'x','yl'}, dimensions={0} | all-to-all | bytes 2752512 | tf_op jit(solution)/shard_map/cond/branch_0_fun/all_to_all | solution.py:29
  100.4 0.7 branch_0_fun.9
  101.0 29.9 %all_to_all.43 = bf16[128,16,128]{2,1,0:T(8,128)(2,1)S(1)} all-to-all(bf16[128,16,128]{2,1,0:T(8,128)(2,1)S(1)} %branch_0_fun.9), channel_id=1, replica_groups=mesh['x'=4,'z'=8,'yh'=4,'yl'=2,'c'=2] {'yh','x','z'}, dimensions={0} | all-to-all | bytes 1048576 | tf_op jit(solution)/shard_map/cond/branch_0_fun/all_to_all | solution.py:29
  130.9 1.6 %shard_map.79 = (bf16[1,8,320]{2,1,0:T(8,128)(2,1)}, f32[1,8]{1,0:T(1,128)}) custom-call(s32[3]{0:T(128)S(1)} %get-tuple-element.89.info_ref, bf16[128,16,128]{2,1,0:T(8,128)(2,1)S(1)} %get-tuple-element.94.part_ref), custom_call_target="tpu_custom_call" | custom-call | tf_op jit(solution)/shard_map/pallas_call | solution.py:449
Async XLA Ops:
  0.6 30.1 %collective-permute-start.6 = (bf16[5120,256]{1,0:T(8,128)(2,1)}, bf16[5120,256]{1,0:T(8,128)(2,1)}, u32[]{:S(2)}, u32[]{:S(2)}) collective-permute-start(bf16[5120,256]{1,0:T(8,128)(2,1)} %param.12), channel_id=1, source_target_pairs={{0,1},{1,0},{2,3},{3,2},{4,5},{5,4},{6,7},{7,6},{8,9},{9,8},{10,11... | collective-permute-start | bytes 7864328 | tf_op jit(solution)/shard_map/ppermute | solution.py:461
  4.1 26.6 %all-to-all-start.9 = ((bf16[32,8,640]{2,1,0:T(8,128)(2,1)}), bf16[32,8,640]{2,1,0:T(8,128)(2,1)S(1)}, u32[]{:S(2)}, u32[]{:S(2)}) async-start(bf16[32,8,640]{2,1,0:T(8,128)(2,1)} %shard_map.78), calls=%async_computation.9 | async-start | bytes 655360 | tf_op jit(solution)/shard_map/all_to_all | solution.py:29
  30.7 38.0 %copy-start = (bf16[5120,256]{1,0:T(8,128)(2,1)S(1)}, bf16[5120,256]{1,0:T(8,128)(2,1)}, u32[]{:S(2)}) copy-start(bf16[5120,256]{1,0:T(8,128)(2,1)} %get-tuple-element.51) | copy-start | bytes 7864324 | tf_op jit(solution)/shard_map/cond
  66.8 4.7 %collective-permute-start = (bf16[8,64,1152]{2,1,0:T(8,128)(2,1)S(1)}, bf16[8,64,1152]{2,1,0:T(8,128)(2,1)S(1)}, u32[]{:S(2)}, u32[]{:S(2)}) collective-permute-start(bf16[8,64,1152]{2,1,0:T(8,128)(2,1)S(1)} %all_to_all.41.own_ref), channel_id=1, source_target_pairs={{0,1},{1,0},{2,3},{3,2},{4,5},{5,4},{6,7},{7,6},{8,9},{9,8},{10,11... | collective-permute-start | bytes 3538952 | tf_op jit(solution)/shard_map/cond/branch_0_fun/ppermute | solution.py:461
  71.5 4.1 %copy-start.3 = (bf16[5120,256]{1,0:T(8,128)(2,1)S(1)}, bf16[5120,256]{1,0:T(8,128)(2,1)}, u32[]{:S(2)}) copy-start(bf16[5120,256]{1,0:T(8,128)(2,1)} %get-tuple-element.57) | copy-start | bytes 7864324 | tf_op jit(solution)/shard_map/cond
  72.2 3.4 %collective-permute-start.1 = (bf16[272,256]{1,0:T(8,128)(2,1)S(1)}, bf16[272,256]{1,0:T(8,128)(2,1)S(1)}, u32[]{:S(2)}, u32[]{:S(2)}) collective-permute-start(bf16[272,256]{1,0:T(8,128)(2,1)S(1)} %branch_0_fun.7.own_ref), channel_id=1, source_target_pairs={{0,1},{1,0},{2,3},{3,2},{4,5},{5,4},{6,7},{7,6},{8,9},{9,8},{10,11... | collective-permute-start | bytes 417800 | tf_op jit(solution)/shard_map/cond/branch_0_fun/ppermute | solution.py:461
